TPU v7x, 32 devices: a whole 2x2x4 slice. The times are simulated.
32 devices in a mesh: grp: 2 (over x), scan: 8 (over z, y), det: 2 (over core).
Axes of the slice: x: 2, y: 2, z: 4, core: 2. Of those that a mesh axis runs over, the one named last changes fastest.
Arguments:
- spectra: float32 [16384, 4096], P(('grp', 'scan'), 'det'), parts along dimension 0, may hold values from 0 to 544, as said below
- basis: float32 [64, 4096], P('grp', 'det'), parts along dimension 0, may hold values from 0.03 to 8, as said below
- loadings: float32 [64, 8192], P('grp', 'scan'), parts along dimension 0, may hold values from 0.005 to 6, as said below
Outputs:
- new_loadings: float32 [64, 8192], P('grp', 'scan'), parts along dimension 0
- new_basis: float32 [64, 4096], P('grp', 'det'), parts along dimension 0
There are 2 independent parts, one for each index of `grp`. A program takes and returns all parts, laid end to end along the dimension named above; each array names one. Nothing has to cross between parts.
Inputs may be any that keep to these rules, and one draw needn't show every extreme that they name: `spectra`: intensities are nonnegative. `basis`: entries are positive. `loadings`: entries are positive.
All inputs are finite; a program needn't handle non-finite values.
Results may differ from a plain program's by a relative error of at most 0.00005.
Values sent between devices are 32-bit elements; how exact they have to be, the bound alone decides.
No kernel may reach another device: no remote copies, remote signals or barrier semaphores. Data moves between devices by JAX's collectives and lax.ppermute only.
A program may use at most 64 MiB of HBM per device.

v0:
```python
import jax
import jax.numpy as jnp
from jax import lax
from jax.sharding import PartitionSpec as P

HIGHEST = lax.Precision.HIGHEST


def swapped(block, axis, stride):
    count = lax.axis_size(axis)
    route = []
    for low in range(count):
        high = low | 1 << stride
        if high != low and high < count:
            route += [(low, high), (high, low)]
    return lax.ppermute(block, axis, route)


def per_device(spectra, basis, loadings):
    partner = swapped(basis, "det", 0)
    tied = 0.5 * (basis + jnp.flip(partner, 1))
    local_numer = lax.dot_general(tied, spectra, (((1,), (1,)), ((), ())), precision=HIGHEST)
    gram = 2.0 * lax.dot_general(tied, tied, (((1,), (1,)), ((), ())), precision=HIGHEST)
    numer_h = lax.psum(local_numer, "det")
    new_loadings = loadings * numer_h / jnp.dot(gram, loadings, precision=HIGHEST)
    w_terms = jnp.dot(new_loadings, spectra, precision=HIGHEST)
    cross_terms = lax.dot_general(
        new_loadings, new_loadings, (((1,), (1,)), ((), ())), precision=HIGHEST
    )
    numer_w, cross = lax.psum((w_terms, cross_terms), "scan")
    mirrored = swapped(numer_w, "det", 0)
    tied_numer = 0.5 * (numer_w + jnp.flip(mirrored, 1))
    new_basis = tied * tied_numer / jnp.dot(cross, tied, precision=HIGHEST)
    return (new_loadings, new_basis)


def solution(mesh):
    in_specs = (P(("grp", "scan"), "det"), P("grp", "det"), P("grp", "scan"))
    out_specs = (P("grp", "scan"), P("grp", "det"))
    return jax.shard_map(
        per_device, mesh=mesh, in_specs=in_specs, out_specs=out_specs, check_vma=False
    )
```

profile of v0, /device:TPU:0, one launch (start us, length us, event | category | flops | bytes accessed | tf_op | source)
XLA Modules:
  0.0 169.3 jit_solution(7217789478776410331)
XLA Ops:
  7.2 0.0 copy-start.1
  7.2 0.0 all-reduce.3.cloned.1.call-start
  7.2 0.5 collective-permute-start
  7.7 1.4 collective-permute-done
  9.1 1.2 rev.7
  10.3 1.0 add_multiply_fusion
  11.3 10.6 %fusion = f32[32,1024]{1,0:T(8,128)} fusion(f32[32,2048]{1,0:T(8,128)S(1)} %add_multiply_fusion, f32[1024,2048]{1,0:T(8,128)} %param.3), kind=kOutput, calls=%fused_computation.4 | convolution fusion | flops 805306368 | bytes 8781824 | tf_op jit(solution)/shard_map/dot_general | solution.py:22
  21.9 0.0 all-reduce.3.cloned.1.call-update
  21.9 0.0 all-reduce.5.cloned.1.call-start
  21.9 0.3 convolution_multiply_fusion
  22.3 20.3 %all-reduce.3.cloned.1.call-done = f32[32,1024]{1,0:T(8,128)} async-done(((f32[32,1024]{1,0:T(8,128)}), f32[32,1024]{1,0:T(8,128)}) %all-reduce.3.cloned.1.call-update) | async-done | bytes 131088 | tf_op jit(solution)/shard_map/psum | solution.py:24
  42.6 0.0 copy-done.1
  42.6 1.2 convolution_divide_fusion
  43.7 0.0 copy-start
  43.8 7.9 %fusion.1 = f32[32,2048]{1,0:T(8,128)} fusion(f32[32,1024]{1,0:T(8,128)S(1)} %convolution_divide_fusion, f32[1024,2048]{1,0:T(8,128)} %param.3), kind=kOutput, calls=%fused_computation.5 | convolution fusion | flops 805306368 | bytes 8781824 | tf_op jit(solution)/shard_map/dot_general | solution.py:26
  51.7 0.0 all-reduce.5.cloned.1.call-update
  51.7 71.9 %all-reduce.5.cloned.1.call-done = f32[32,2048]{1,0:T(8,128)} async-done(((f32[32,2048]{1,0:T(8,128)}), f32[32,2048]{1,0:T(8,128)}) %all-reduce.5.cloned.1.call-update) | async-done | bytes 262160 | tf_op jit(solution)/shard_map/psum | solution.py:30
  123.6 0.0 collective-permute-start.1
  123.6 0.2 fusion.2
  123.8 35.4 %psum.23 = f32[32,32]{1,0:T(8,128)S(1)} all-reduce(f32[32,32]{1,0:T(8,128)S(1)} %fusion.2), channel_id=1, replica_groups=mesh['grp'=2,'scan'=8,'det'=2] {'scan'}, use_global_device_ids=true, to_apply=%region_2.3 | all-reduce | flops 1024 | bytes 8192 | tf_op jit(solution)/shard_map/psum | solution.py:30
  159.3 0.0 collective-permute-done.1
  159.3 1.2 rev.8
  160.4 2.0 %multiply_divide_fusion = f32[32,2048]{1,0:T(8,128)} fusion(f32[32,2048]{1,0:T(8,128)S(1)} %add_multiply_fusion, f32[32,2048]{1,0:T(8,128)} %all-reduce.5.cloned.1.call-done, f32[32,2048]{1,0:T(8,128)S(1)} %rev.8, f32[32,32]{1,0:T(8,128)S(1)} %psum.23), kind=kOutput, calls=%fused_computation.2 | convolution fusion | flops 25427968 | bytes 1052672 | tf_op jit(solution)/shard_map/dot_general | solution.py:33
  162.5 0.0 copy-done
Async XLA Ops:
  7.2 35.4 %copy-start.1 = (f32[32,1024]{1,0:T(8,128)S(1)}, f32[32,1024]{1,0:T(8,128)}, u32[]{:S(2)}) copy-start(f32[32,1024]{1,0:T(8,128)} %param.5) | copy-start | bytes 393220
  7.2 35.4 %all-reduce.3.cloned.1.call-start = ((), (), s32[]{:S(2)}) async-start(), calls=%async_computation | async-start | bytes 262144 | tf_op jit(solution)/shard_map/psum | solution.py:24
  7.2 1.9 %collective-permute-start = (f32[32,2048]{1,0:T(8,128)}, f32[32,2048]{1,0:T(8,128)S(1)}, u32[]{:S(2)}, u32[]{:S(2)}) collective-permute-start(f32[32,2048]{1,0:T(8,128)} %param.4), channel_id=1, source_target_pairs={{0,1},{1,0},{2,3},{3,2},{4,5},{5,4},{6,7},{7,6},{8,9},{9,8},{10,11... | collective-permute-start | bytes 786440 | tf_op jit(solution)/shard_map/ppermute | solution.py:16
  21.9 101.7 %all-reduce.5.cloned.1.call-start = ((), (), s32[]{:S(2)}) async-start(), calls=%async_computation.1 | async-start | bytes 524288 | tf_op jit(solution)/shard_map/psum | solution.py:30
  43.7 118.7 %copy-start = (f32[32,1024]{1,0:T(8,128)}, f32[32,1024]{1,0:T(8,128)S(1)}, u32[]{:S(2)}) copy-start(f32[32,1024]{1,0:T(8,128)S(1)} %convolution_divide_fusion) | copy-start | bytes 393220
  123.6 35.7 %collective-permute-start.1 = (f32[32,2048]{1,0:T(8,128)}, f32[32,2048]{1,0:T(8,128)S(1)}, u32[]{:S(2)}, u32[]{:S(2)}) collective-permute-start(f32[32,2048]{1,0:T(8,128)} %all-reduce.5.cloned.1.call-done), channel_id=1, source_target_pairs={{0,1},{1,0},{2,3},{3,2},{4,5},{5,4},{6,7},{7,6},{8,9},{9,8},{10,11... | collective-permute-start | bytes 786440 | tf_op jit(solution)/shard_map/ppermute | solution.py:16
Sparse Core Ops, SparseCore 0:
  22.0 20.5 all-reduce.2
  51.8 71.7 all-reduce.4
where the time goes:
time: 170 us; the launch traced here: 169 us
  waiting for transfers between devices  93.6 us (55%)
  blocking collectives  35.4 us (21%)
  matrix products  22.3 us (13%)
  between operations  14.1 us (8%)
  local copies, waits for them, and re-layouts  2.34 us (1%)
    psum x1, waiting for transfers between devices, per_device(): numer_w, cross = lax.psum((w_terms, cross_terms), 'scan')  71.9 us
    psum x1, blocking collectives, per_device(): numer_w, cross = lax.psum((w_terms, cross_terms), 'scan')  35.4 us
    psum x1, waiting for transfers between devices, per_device(): numer_h = lax.psum(local_numer, 'det')  20.3 us
    dot_general x1, matrix products, per_device(): lax.dot_general(tied, spectra, (((1,), (1,)), ((), ())), precision=HIGHEST)  10.6 us
    dot_general x1, matrix products, per_device(): w_terms = jnp.dot(new_loadings, spectra, precision=HIGHEST)  7.91 us
  transfers between devices with their start and end apart: 4, of which 3 were waited for; matrix products, arithmetic and copies ran while one was open for 0% of the time, Pallas kernels for 0%

commit v1 on v0

v1 whole, which is shorter than its diff:
```python
import functools

import jax
import jax.numpy as jnp
from jax import lax
from jax.experimental import pallas as pl
from jax.experimental.pallas import tpu as pltpu
from jax.sharding import PartitionSpec as P

HIGHEST = lax.Precision.HIGHEST
LANES = 128
MIB = 1 << 20
F32, BF16 = jnp.float32, jnp.bfloat16
NT = (((1,), (1,)), ((), ()))
NN = (((1,), (0,)), ((), ()))


def in_vmem(x):
    return pltpu.with_memory_space_constraint(x, pltpu.VMEM)


def vmem_specs(count):
    return [pl.BlockSpec(memory_space=pltpu.VMEM)] * count


def halves(x):
    high = x.astype(BF16)
    return high, (x - high.astype(F32)).astype(BF16)


def mirror_lanes(block):
    lane = lax.broadcasted_iota(jnp.int32, block.shape, 1)
    return jnp.take_along_axis(block, LANES - 1 - lane, axis=1, mode="promise_in_bounds")


def dot(a, b, dims, precision=None):
    return lax.dot_general(a, b, dims, precision=precision, preferred_element_type=F32)


def numer_kernel(rows, spectra, basis, partner, loadings, numer, ratio, tied, high, low, stage, sems):
    rank, cols = basis.shape
    chunks = spectra.shape[0] // rows
    copies = [
        pltpu.make_async_copy(spectra.at[pl.ds(i * rows, rows)], stage.at[pl.ds(i * rows, rows)], sems.at[i])
        for i in range(chunks)
    ]
    for copy in copies:
        copy.start()
    blocks = cols // LANES
    for j in range(blocks):
        mirrored = mirror_lanes(partner[:, pl.ds((blocks - 1 - j) * LANES, LANES)])
        at = pl.ds(j * LANES, LANES)
        tied[:, at] = 0.5 * (basis[:, at] + mirrored)
    both = tied[...]
    gram = 2.0 * dot(both, both, NT, HIGHEST)
    ratio[...] = loadings[...] / dot(gram, loadings[...], NN, HIGHEST)
    tied_high, tied_low = halves(both)
    tied_parts = jnp.concatenate([tied_high, tied_low], axis=0)
    for i in range(chunks):
        at = pl.ds(i * rows, rows)
        copies[i].wait()
        block_high, block_low = halves(stage[at, :])
        high[at, :] = block_high
        low[at, :] = block_low
        terms = dot(block_high, tied_parts, NT)
        terms = terms[:, :rank] + terms[:, rank:] + dot(block_low, tied_high, NT)
        numer[:, at] = terms.T


def terms_kernel(cols, own, other, ratio, high, low, new_loadings, keep, send):
    rank = own.shape[0]
    total = high.shape[1]
    half = total // 2
    new = ratio[...] * (own[...] + other[...])
    new_loadings[...] = new
    new_high, new_low = halves(new)
    new_parts = jnp.concatenate([new_high, new_low], axis=0)
    cross = dot(new, new, NT, HIGHEST)
    per_row = LANES // rank
    strip = rank // per_row
    packed = jnp.concatenate([cross[i * strip:(i + 1) * strip] for i in range(per_row)], axis=1)
    top = half // LANES * rank
    keep[pl.ds(top, strip), :] = packed
    send[pl.ds(top, strip), :] = jnp.zeros_like(packed)
    for c in range(0, total, cols):
        at = pl.ds(c, cols)
        terms = dot(new_parts, high[:, at], NN)
        terms = terms[:rank] + terms[rank:] + dot(new_high, low[:, at], NN)
        for b in range(cols // LANES):
            block = terms[:, b * LANES:(b + 1) * LANES]
            start = c + b * LANES
            if start < half:
                keep[pl.ds(start // LANES * rank, rank), :] = block
            else:
                turned = (total - LANES - start) // LANES * rank
                send[pl.ds(turned, rank), :] = mirror_lanes(block)


def basis_kernel(tied, own, other, new_basis):
    rank, cols = tied.shape
    half = cols // 2
    per_row = LANES // rank
    strip = rank // per_row
    top = half // LANES * rank
    packed = own[pl.ds(top, strip), :]
    cross = jnp.concatenate([packed[:, i * rank:(i + 1) * rank] for i in range(per_row)], axis=0)
    scale = dot(cross, tied[...], NN, HIGHEST)
    for start in range(0, cols, LANES):
        if start < half:
            numer = own[pl.ds(start // LANES * rank, rank), :]
        else:
            numer = mirror_lanes(other[pl.ds((cols - LANES - start) // LANES * rank, rank), :])
        at = pl.ds(start, LANES)
        new_basis[:, at] = tied[:, at] * (0.5 * numer) / scale[:, start:start + LANES]


def over_det(x):
    return lax.ppermute(x, "det", [(0, 1), (1, 0)])


def scan_sum(x):
    count = lax.axis_size("scan")
    steps = count.bit_length() - 1
    if count != 1 << steps:
        return lax.psum(x, "scan")
    for step in range(steps):
        route = []
        for core in range(2):
            stride = 1 << (step + core * (steps // 2)) % steps
            route += [(2 * i + core, 2 * (i ^ stride) + core) for i in range(count)]
        x = x + lax.ppermute(x, ("scan", "det"), route)
    return x


def per_device(spectra, basis, loadings):
    positions, cols = spectra.shape
    rank = basis.shape[0]
    rows = min(positions, 128)
    block_cols = 256
    packed = (cols // 2 // LANES * rank + rank * rank // LANES, LANES)
    partner = over_det(basis)
    numer, ratio, tied, high, low = pl.pallas_call(
        functools.partial(numer_kernel, rows),
        out_shape=[
            pltpu.VMEM((rank, positions), F32),
            pltpu.VMEM((rank, positions), F32),
            pltpu.VMEM((rank, cols), F32),
            pltpu.VMEM((positions, cols), BF16),
            pltpu.VMEM((positions, cols), BF16),
        ],
        in_specs=[pl.BlockSpec(memory_space=pl.ANY)] + vmem_specs(3),
        out_specs=vmem_specs(5),
        scratch_shapes=[pltpu.VMEM((positions, cols), F32), pltpu.SemaphoreType.DMA((positions // rows,))],
        compiler_params=pltpu.CompilerParams(vmem_limit_bytes=20 * MIB),
        name="numer",
    )(spectra, basis, partner, loadings)
    other = over_det(numer)
    new_loadings, keep, send = pl.pallas_call(
        functools.partial(terms_kernel, block_cols),
        out_shape=[
            jax.ShapeDtypeStruct((rank, positions), F32),
            pltpu.VMEM(packed, F32),
            pltpu.VMEM(packed, F32),
        ],
        in_specs=vmem_specs(5),
        out_specs=vmem_specs(3),
        compiler_params=pltpu.CompilerParams(vmem_limit_bytes=20 * MIB),
        name="terms",
    )(in_vmem(numer), in_vmem(other), in_vmem(ratio), in_vmem(high), in_vmem(low))
    sums = scan_sum(keep + over_det(send))
    new_basis = pl.pallas_call(
        basis_kernel,
        out_shape=jax.ShapeDtypeStruct((rank, cols), F32),
        in_specs=vmem_specs(3),
        out_specs=pl.BlockSpec(memory_space=pltpu.VMEM),
        compiler_params=pltpu.CompilerParams(vmem_limit_bytes=20 * MIB),
        name="basis",
    )(in_vmem(tied), in_vmem(sums), in_vmem(over_det(sums)))
    return new_loadings, new_basis


def solution(mesh):
    in_specs = (P(("grp", "scan"), "det"), P("grp", "det"), P("grp", "scan"))
    out_specs = (P("grp", "scan"), P("grp", "det"))
    return jax.shard_map(
        per_device, mesh=mesh, in_specs=in_specs, out_specs=out_specs, check_vma=False
    )
```

time: 170 us -> 39.5 us (0.23)
  waiting for transfers between devices: 93.6 us -> 14.7 us
  blocking collectives: 35.4 us -> 0 us
  matrix products: 22.3 us -> 0 us
  between operations: 14.1 us -> 0.66 us
  Pallas kernels: 0 us -> 9.17 us
  starting transfers between devices: 0.6 us -> 9.19 us
  local copies, waits for them, and re-layouts: 2.34 us -> 5.23 us
    psum x2 -> x0, waiting for transfers between devices: 92.2 us -> none  [the longest x1 71.9 us: per_device(): numer_w, cross = lax.psum((w_terms, cross_terms), 'scan')]
    psum x1 -> x0, blocking collectives: 35.4 us -> none  [per_device(): numer_w, cross = lax.psum((w_terms, cross_terms), 'scan')]
    dot_general x6 -> x0, matrix products: 22.3 us -> none  [the longest x1 10.6 us: per_device(): lax.dot_general(tied, spectra, (((1,), (1,)), ((), ())), precision=HIGHEST)]
    ppermute x2 -> x7, waiting for transfers between devices: 1.38 us -> 14.7 us  [the longest x3 10 us: scan_sum(): x = x + lax.ppermute(x, ('scan', 'det'), route)]
    pallas_call x0 -> x3, Pallas kernels: none -> 9.17 us  [the longest x1 5.95 us: per_device(): pl.pallas_call(functools.partial(numer_kernel, rows), out_shape=[pltpu.VM...]
    ppermute x2 -> x7, starting transfers between devices: 0.52 us -> 9.19 us  [the longest x3 7.8 us: scan_sum(): x = x + lax.ppermute(x, ('scan', 'det'), route)]
    unnamed x4 -> x6, local copies, waits for them, and re-layouts: 0.01 us -> 5.23 us
    rev x2 -> x0, local copies, waits for them, and re-layouts: 2.33 us -> none  [the longest x1 1.17 us: per_device(): tied_numer = 0.5 * (numer_w + jnp.flip(mirrored, 1))]
  transfers between devices with their start and end apart: 4 -> 7, of which waited for: 3 -> 7; matrix products, arithmetic and copies ran while one was open for 0% -> 0% of each run, Pallas kernels for 0% -> 0%
where the time goes in v1:
time: 39.5 us; the launch traced here: 39 us
  waiting for transfers between devices  14.7 us (37%)
  starting transfers between devices  9.19 us (23%)
  Pallas kernels  9.17 us (23%)
  local copies, waits for them, and re-layouts  5.23 us (13%)
  between operations  0.66 us (2%)
    ppermute x3, waiting for transfers between devices, scan_sum(): x = x + lax.ppermute(x, ('scan', 'det'), route)  10 us
    ppermute x3, starting transfers between devices, scan_sum(): x = x + lax.ppermute(x, ('scan', 'det'), route)  7.8 us
    pallas_call x1, Pallas kernels, per_device(): pl.pallas_call(functools.partial(numer_kernel, rows), out_shape=[pltpu.VM...  5.95 us
    unnamed x6, local copies, waits for them, and re-layouts  5.23 us
    ppermute x4, waiting for transfers between devices, over_det(): return lax.ppermute(x, 'det', [(0, 1), (1, 0)])  4.69 us
    pallas_call x1, Pallas kernels, per_device(): pl.pallas_call(functools.partial(terms_kernel, block_cols), out_shape=[ja...  2.09 us
    ppermute x4, starting transfers between devices, over_det(): return lax.ppermute(x, 'det', [(0, 1), (1, 0)])  1.39 us
    pallas_call x1, Pallas kernels, per_device(): pl.pallas_call(basis_kernel, out_shape=jax.ShapeDtypeStruct((rank, cols),...  1.13 us
  transfers between devices with their start and end apart: 7, of which 7 were waited for; matrix products, arithmetic and copies ran while one was open for 0% of the time, Pallas kernels for 0%

profile of v1, /device:TPU:0, one launch (start us, length us, event | category | flops | bytes accessed | tf_op | source)
XLA Modules:
  0.0 39.0 jit_solution(15903148754477493302)
XLA Ops:
  0.6 0.5 %collective-permute-start = (f32[32,2048]{1,0:T(8,128)}, f32[32,2048]{1,0:T(8,128)S(1)}, u32[]{:S(2)}, u32[]{:S(2)}) collective-permute-start(f32[32,2048]{1,0:T(8,128)} %basis.2), channel_id=1, source_target_pairs={{0,1},{1,0},{2,3},{3,2},{4,5},{5,4},{6,7},{7,6},{8,9},{9,8},{10,11... | collective-permute-start | bytes 786440 | tf_op jit(solution)/shard_map/ppermute | solution.py:118
  1.1 1.4 %collective-permute-done.partner = f32[32,2048]{1,0:T(8,128)S(1)} collective-permute-done((f32[32,2048]{1,0:T(8,128)}, f32[32,2048]{1,0:T(8,128)S(1)}, u32[]{:S(2)}, u32[]{:S(2)}) %collective-permute-start) | collective-permute-done | bytes 262176 | tf_op jit(solution)/shard_map/ppermute | solution.py:118
  2.5 0.0 copy-start
  2.5 3.4 %copy-done = f32[1024,2048]{1,0:T(8,128)S(1)} copy-done((f32[1024,2048]{1,0:T(8,128)S(1)}, f32[1024,2048]{1,0:T(8,128)}, u32[]{:S(2)}) %copy-start) | copy-done | bytes 8388632
  5.9 0.0 copy-start.1
  5.9 0.9 %copy-done.1 = f32[32,2048]{1,0:T(8,128)S(1)} copy-done((f32[32,2048]{1,0:T(8,128)S(1)}, f32[32,2048]{1,0:T(8,128)}, u32[]{:S(2)}) %copy-start.1) | copy-done | bytes 262168
  6.9 0.0 copy-start.2
  6.9 0.9 %copy-done.2 = f32[32,1024]{1,0:T(8,128)S(1)} copy-done((f32[32,1024]{1,0:T(8,128)S(1)}, f32[32,1024]{1,0:T(8,128)}, u32[]{:S(2)}) %copy-start.2) | copy-done | bytes 131096
  7.8 6.0 %numer.1 = (f32[32,1024]{1,0:T(8,128)S(1)}, f32[32,1024]{1,0:T(8,128)S(1)}, f32[32,2048]{1,0:T(8,128)S(1)}, bf16[1024,2048]{1,0:T(8,128)(2,1)S(1)}, bf16[1024,2048]{1,0:T(8,128)(2,1)S(1)}) custom-call(f32[1024,2048]{1,0:T(8,128)S(1)} %copy-done, f32[32,2048]{1,0:T(8,128)S(1)} %copy-done.1, f32[32,2048]{1,0:T(8,128)S(1)} %collective-permute-done.partner, ...), custom_call_target="tpu_custom_call" | custom-call | tf_op jit(solution)/shard_map/numer/pallas_call | solution.py:142
  13.7 0.4 %collective-permute-start.1 = (f32[32,1024]{1,0:T(8,128)S(1)}, f32[32,1024]{1,0:T(8,128)S(1)}, u32[]{:S(2)}, u32[]{:S(2)}) collective-permute-start(f32[32,1024]{1,0:T(8,128)S(1)} %get-tuple-element.10.own), channel_id=1, source_target_pairs={{0,1},{1,0},{2,3},{3,2},{4,5},{5,4},{6,7},{7,6},{8,9},{9,8},{10,11... | collective-permute-start | bytes 393224 | tf_op jit(solution)/shard_map/ppermute | solution.py:118
  14.2 1.0 %collective-permute-done.1.other = f32[32,1024]{1,0:T(8,128)S(1)} collective-permute-done((f32[32,1024]{1,0:T(8,128)S(1)}, f32[32,1024]{1,0:T(8,128)S(1)}, u32[]{:S(2)}, u32[]{:S(2)}) %collective-permute-start.1) | collective-permute-done | bytes 131104 | tf_op jit(solution)/shard_map/ppermute | solution.py:118
  15.1 2.1 %terms.1 = (f32[32,1024]{1,0:T(8,128)}, f32[264,128]{1,0:T(8,128)S(1)}, f32[264,128]{1,0:T(8,128)S(1)}) custom-call(f32[32,1024]{1,0:T(8,128)S(1)} %get-tuple-element.10.own, f32[32,1024]{1,0:T(8,128)S(1)} %collective-permute-done.1.other, f32[32,1024]{1,0:T(8,128)S(1)} %get-tuple-element.11.ratio, bf16[1024,2048]{1,0:T(8,128)(2,1)S(1)} %get-tuple-element.12.high, ...), custom_call_target="tpu_custom_call" | custom-call | tf_op jit(solution)/shard_map/terms/pallas_call | solution.py:158
  17.2 0.4 collective-permute-start.2
  17.6 1.0 %collective-permute-done.2 = f32[264,128]{1,0:T(8,128)S(1)} collective-permute-done((f32[264,128]{1,0:T(8,128)S(1)}, f32[264,128]{1,0:T(8,128)S(1)}, u32[]{:S(2)}, u32[]{:S(2)}) %collective-permute-start.2) | collective-permute-done | bytes 135200 | tf_op jit(solution)/shard_map/ppermute | solution.py:118
  18.6 2.9 %collective-permute-start.3 = (f32[264,128]{1,0:T(8,128)S(1)}, f32[264,128]{1,0:T(8,128)S(1)}, u32[]{:S(2)}, u32[]{:S(2)}) collective-permute-start(f32[264,128]{1,0:T(8,128)S(1)} %add.12), channel_id=1, source_target_pairs={{0,2},{2,0},{4,6},{6,4},{8,10},{10,8},{12,14},{14,12},{1,5},{3,7},... | collective-permute-start | bytes 405512 | tf_op jit(solution)/shard_map/ppermute | solution.py:131
  21.6 3.0 %collective-permute-done.3 = f32[264,128]{1,0:T(8,128)S(1)} collective-permute-done((f32[264,128]{1,0:T(8,128)S(1)}, f32[264,128]{1,0:T(8,128)S(1)}, u32[]{:S(2)}, u32[]{:S(2)}) %collective-permute-start.3) | collective-permute-done | bytes 135200 | tf_op jit(solution)/shard_map/ppermute | solution.py:131
  24.6 2.1 %collective-permute-start.4 = (f32[264,128]{1,0:T(8,128)S(1)}, f32[264,128]{1,0:T(8,128)S(1)}, u32[]{:S(2)}, u32[]{:S(2)}) collective-permute-start(f32[264,128]{1,0:T(8,128)S(1)} %add.13), channel_id=1, source_target_pairs={{0,4},{2,6},{4,0},{6,2},{8,12},{10,14},{12,8},{14,10},{1,9},{3,11}... | collective-permute-start | bytes 405512 | tf_op jit(solution)/shard_map/ppermute | solution.py:131
  26.7 3.8 %collective-permute-done.4 = f32[264,128]{1,0:T(8,128)S(1)} collective-permute-done((f32[264,128]{1,0:T(8,128)S(1)}, f32[264,128]{1,0:T(8,128)S(1)}, u32[]{:S(2)}, u32[]{:S(2)}) %collective-permute-start.4) | collective-permute-done | bytes 135200 | tf_op jit(solution)/shard_map/ppermute | solution.py:131
  30.5 2.7 %collective-permute-start.5 = (f32[264,128]{1,0:T(8,128)S(1)}, f32[264,128]{1,0:T(8,128)S(1)}, u32[]{:S(2)}, u32[]{:S(2)}) collective-permute-start(f32[264,128]{1,0:T(8,128)S(1)} %add.14), channel_id=1, source_target_pairs={{0,8},{2,10},{4,12},{6,14},{8,0},{10,2},{12,4},{14,6},{1,3},{3,1},... | collective-permute-start | bytes 405512 | tf_op jit(solution)/shard_map/ppermute | solution.py:131
  33.2 3.3 %collective-permute-done.5 = f32[264,128]{1,0:T(8,128)S(1)} collective-permute-done((f32[264,128]{1,0:T(8,128)S(1)}, f32[264,128]{1,0:T(8,128)S(1)}, u32[]{:S(2)}, u32[]{:S(2)}) %collective-permute-start.5) | collective-permute-done | bytes 135200 | tf_op jit(solution)/shard_map/ppermute | solution.py:131
  36.5 0.1 collective-permute-start.6
  36.6 1.3 %collective-permute-done.6.other = f32[264,128]{1,0:T(8,128)S(1)} collective-permute-done((f32[264,128]{1,0:T(8,128)S(1)}, f32[264,128]{1,0:T(8,128)S(1)}, u32[]{:S(2)}, u32[]{:S(2)}) %collective-permute-start.6) | collective-permute-done | bytes 135200 | tf_op jit(solution)/shard_map/ppermute | solution.py:118
  37.9 1.1 %basis.3 = f32[32,2048]{1,0:T(8,128)} custom-call(f32[32,2048]{1,0:T(8,128)S(1)} %get-tuple-element.15.tied, f32[264,128]{1,0:T(8,128)S(1)} %add.15.own, f32[264,128]{1,0:T(8,128)S(1)} %collective-permute-done.6.other), custom_call_target="tpu_custom_call" | custom-call | tf_op jit(solution)/shard_map/basis/pallas_call | solution.py:171
  (4 shorter events, 0.1 us)
Async XLA Ops:
  0.6 1.9 %collective-permute-start = (f32[32,2048]{1,0:T(8,128)}, f32[32,2048]{1,0:T(8,128)S(1)}, u32[]{:S(2)}, u32[]{:S(2)}) collective-permute-start(f32[32,2048]{1,0:T(8,128)} %basis.2), channel_id=1, source_target_pairs={{0,1},{1,0},{2,3},{3,2},{4,5},{5,4},{6,7},{7,6},{8,9},{9,8},{10,11... | collective-permute-start | bytes 786440 | tf_op jit(solution)/shard_map/ppermute | solution.py:118
  2.5 3.4 %copy-start = (f32[1024,2048]{1,0:T(8,128)S(1)}, f32[1024,2048]{1,0:T(8,128)}, u32[]{:S(2)}) copy-start(f32[1024,2048]{1,0:T(8,128)} %spectra.1) | copy-start | bytes 25165828
  5.9 0.9 %copy-start.1 = (f32[32,2048]{1,0:T(8,128)S(1)}, f32[32,2048]{1,0:T(8,128)}, u32[]{:S(2)}) copy-start(f32[32,2048]{1,0:T(8,128)} %basis.2) | copy-start | bytes 786436
  6.9 0.9 %copy-start.2 = (f32[32,1024]{1,0:T(8,128)S(1)}, f32[32,1024]{1,0:T(8,128)}, u32[]{:S(2)}) copy-start(f32[32,1024]{1,0:T(8,128)} %loadings.1) | copy-start | bytes 393220
  13.7 1.4 %collective-permute-start.1 = (f32[32,1024]{1,0:T(8,128)S(1)}, f32[32,1024]{1,0:T(8,128)S(1)}, u32[]{:S(2)}, u32[]{:S(2)}) collective-permute-start(f32[32,1024]{1,0:T(8,128)S(1)} %get-tuple-element.10.own), channel_id=1, source_target_pairs={{0,1},{1,0},{2,3},{3,2},{4,5},{5,4},{6,7},{7,6},{8,9},{9,8},{10,11... | collective-permute-start | bytes 393224 | tf_op jit(solution)/shard_map/ppermute | solution.py:118
  17.2 1.4 %collective-permute-start.2 = (f32[264,128]{1,0:T(8,128)S(1)}, f32[264,128]{1,0:T(8,128)S(1)}, u32[]{:S(2)}, u32[]{:S(2)}) collective-permute-start(f32[264,128]{1,0:T(8,128)S(1)} %get-tuple-element.17), channel_id=1, source_target_pairs={{0,1},{1,0},{2,3},{3,2},{4,5},{5,4},{6,7},{7,6},{8,9},{9,8},{10,11... | collective-permute-start | bytes 405512 | tf_op jit(solution)/shard_map/ppermute | solution.py:118
  18.6 5.9 %collective-permute-start.3 = (f32[264,128]{1,0:T(8,128)S(1)}, f32[264,128]{1,0:T(8,128)S(1)}, u32[]{:S(2)}, u32[]{:S(2)}) collective-permute-start(f32[264,128]{1,0:T(8,128)S(1)} %add.12), channel_id=1, source_target_pairs={{0,2},{2,0},{4,6},{6,4},{8,10},{10,8},{12,14},{14,12},{1,5},{3,7},... | collective-permute-start | bytes 405512 | tf_op jit(solution)/shard_map/ppermute | solution.py:131
  24.6 5.9 %collective-permute-start.4 = (f32[264,128]{1,0:T(8,128)S(1)}, f32[264,128]{1,0:T(8,128)S(1)}, u32[]{:S(2)}, u32[]{:S(2)}) collective-permute-start(f32[264,128]{1,0:T(8,128)S(1)} %add.13), channel_id=1, source_target_pairs={{0,4},{2,6},{4,0},{6,2},{8,12},{10,14},{12,8},{14,10},{1,9},{3,11}... | collective-permute-start | bytes 405512 | tf_op jit(solution)/shard_map/ppermute | solution.py:131
  30.5 6.0 %collective-permute-start.5 = (f32[264,128]{1,0:T(8,128)S(1)}, f32[264,128]{1,0:T(8,128)S(1)}, u32[]{:S(2)}, u32[]{:S(2)}) collective-permute-start(f32[264,128]{1,0:T(8,128)S(1)} %add.14), channel_id=1, source_target_pairs={{0,8},{2,10},{4,12},{6,14},{8,0},{10,2},{12,4},{14,6},{1,3},{3,1},... | collective-permute-start | bytes 405512 | tf_op jit(solution)/shard_map/ppermute | solution.py:131
  36.5 1.4 %collective-permute-start.6 = (f32[264,128]{1,0:T(8,128)S(1)}, f32[264,128]{1,0:T(8,128)S(1)}, u32[]{:S(2)}, u32[]{:S(2)}) collective-permute-start(f32[264,128]{1,0:T(8,128)S(1)} %add.15.own), channel_id=1, source_target_pairs={{0,1},{1,0},{2,3},{3,2},{4,5},{5,4},{6,7},{7,6},{8,9},{9,8},{10,11... | collective-permute-start | bytes 405512 | tf_op jit(solution)/shard_map/ppermute | solution.py:118

commit v2 on v0

v2 whole, which is shorter than its diff:
```python
import functools

import jax
import jax.numpy as jnp
from jax import lax
from jax.experimental import pallas as pl
from jax.experimental.pallas import tpu as pltpu
from jax.sharding import PartitionSpec as P

HIGHEST = lax.Precision.HIGHEST
LANES = 128
MIB = 1 << 20
F32, BF16 = jnp.float32, jnp.bfloat16
NT = (((1,), (1,)), ((), ()))
NN = (((1,), (0,)), ((), ()))
HBM, VMEM = pltpu.HBM, pltpu.VMEM


def call(kernel, name, ins, outs, scratch=(), flops=0, moved=0, aliases={}):
    params = pltpu.CompilerParams(vmem_limit_bytes=16 * MIB)
    return pl.pallas_call(
        kernel,
        out_shape=[memory(shape, dtype) for memory, shape, dtype in outs],
        in_specs=[pl.BlockSpec(memory_space=memory) for memory, _ in ins],
        out_specs=[pl.BlockSpec(memory_space=memory) for memory, _, _ in outs],
        scratch_shapes=list(scratch),
        input_output_aliases=aliases,
        compiler_params=params,
        cost_estimate=pl.CostEstimate(flops=flops, bytes_accessed=moved, transcendentals=0),
        name=name,
    )(*[pltpu.with_memory_space_constraint(x, memory) for memory, x in ins])


def halves(x):
    high = x.astype(BF16)
    return high, (x - high.astype(F32)).astype(BF16)


def both_halves(x):
    return jnp.concatenate(halves(x), axis=0)


def mirror_lanes(block):
    lane = lax.broadcasted_iota(jnp.int32, block.shape, 1)
    return jnp.take_along_axis(block, LANES - 1 - lane, axis=1, mode="promise_in_bounds")


def dot(a, b, dims, precision=None):
    return lax.dot_general(a, b, dims, precision=precision, preferred_element_type=F32)


def row_copies(spectra, stage, sems, first, rows):
    return [
        pltpu.make_async_copy(
            spectra.at[pl.ds(first + i * rows, rows)], stage.at[pl.ds(i * rows, rows)], sems.at[i]
        )
        for i in range(stage.shape[0] // rows)
    ]


def load_kernel(rows, spectra, basis, loadings, near_basis, near_loadings, high, low, stage, sems, side_sems):
    copies = row_copies(spectra, stage, sems, 0, rows)
    sides = [
        pltpu.make_async_copy(basis, near_basis, side_sems.at[0]),
        pltpu.make_async_copy(loadings, near_loadings, side_sems.at[1]),
    ]
    for copy in copies + sides:
        copy.start()
    for i, copy in enumerate(copies):
        at = pl.ds(i * rows, rows)
        copy.wait()
        high[at, :], low[at, :] = halves(stage[at, :])
    for copy in sides:
        copy.wait()


def numer_kernel(rows, spectra, basis, partner, high, low, numer, tied, late_high, late_low, stage, sems):
    rank, cols = basis.shape
    early = high.shape[0]
    copies = row_copies(spectra, stage, sems, early, rows)
    for copy in copies:
        copy.start()
    blocks = cols // LANES
    for j in range(blocks):
        mirrored = mirror_lanes(partner[:, pl.ds((blocks - 1 - j) * LANES, LANES)])
        at = pl.ds(j * LANES, LANES)
        tied[:, at] = 0.5 * (basis[:, at] + mirrored)
    tied_parts = both_halves(tied[...])

    def put(start, block_high, block_low):
        terms = dot(block_high, tied_parts, NT)
        terms = terms[:, :rank] + terms[:, rank:] + dot(block_low, tied_parts[:rank], NT)
        numer[:, pl.ds(start, block_high.shape[0])] = terms.T

    for start in range(0, early, rows):
        at = pl.ds(start, rows)
        put(start, high[at, :], low[at, :])
    for i, copy in enumerate(copies):
        at = pl.ds(i * rows, rows)
        copy.wait()
        block_high, block_low = halves(stage[at, :])
        late_high[at, :] = block_high
        late_low[at, :] = block_low
        put(early + i * rows, block_high, block_low)


def ratio_kernel(tied, loadings, ratio):
    gram = 2.0 * dot(tied[...], tied[...], NT, HIGHEST)
    ratio[...] = loadings[...] / dot(gram, loadings[...], NN, HIGHEST)


def column_terms(new, high, low, late_high, late_low, at):
    rank, early = new.shape[0], high.shape[0]
    parts = both_halves(new)
    terms = dot(parts[:, :early], high[:, at], NN) + dot(parts[:, early:], late_high[:, at], NN)
    rest = dot(parts[:rank, :early], low[:, at], NN) + dot(parts[:rank, early:], late_low[:, at], NN)
    return terms[:rank] + terms[rank:] + rest


def send_kernel(width, own, other, ratio, high, low, late_high, late_low, send):
    rank, cols = own.shape[0], high.shape[1]
    new = ratio[...] * (own[...] + other[...])
    for start in range(cols // 2, cols, width):
        terms = column_terms(new, high, low, late_high, late_low, pl.ds(start, width))
        for b in range(0, width, LANES):
            turned = (cols - LANES - start - b) // LANES * rank
            send[pl.ds(turned, rank), :] = mirror_lanes(terms[:, b:b + LANES])


def keep_kernel(width, own, other, ratio, high, low, late_high, late_low, new_loadings, keep, cross, new, sem):
    rank, cols = own.shape[0], high.shape[1]
    new[...] = ratio[...] * (own[...] + other[...])
    copy = pltpu.make_async_copy(new, new_loadings, sem)
    copy.start()
    for start in range(0, cols // 2, width):
        terms = column_terms(new[...], high, low, late_high, late_low, pl.ds(start, width))
        for b in range(0, width, LANES):
            keep[pl.ds((start + b) // LANES * rank, rank), :] = terms[:, b:b + LANES]
    square = dot(new[...], new[...], NT, HIGHEST)
    per_row = LANES // rank
    strip = rank // per_row
    cross[...] = jnp.concatenate([square[i * strip:(i + 1) * strip] for i in range(per_row)], axis=1)
    copy.wait()


def near_kernel(tied, sums, new_basis, scale, near, sem):
    rank, cols = tied.shape
    half = cols // 2
    per_row = LANES // rank
    strip = rank // per_row
    packed = sums[pl.ds(half // LANES * rank, strip), :]
    cross = jnp.concatenate([packed[:, i * rank:(i + 1) * rank] for i in range(per_row)], axis=0)
    whole = dot(cross, tied[...], NN, HIGHEST)
    scale[...] = whole[:, half:]
    for start in range(0, half, LANES):
        numer = sums[pl.ds(start // LANES * rank, rank), :]
        at = pl.ds(start, LANES)
        near[:, at] = tied[:, at] * (0.5 * numer) / whole[:, start:start + LANES]
    copy = pltpu.make_async_copy(near, new_basis.at[:, pl.ds(0, half)], sem)
    copy.start()
    copy.wait()


def far_kernel(first, tied, scale, sums, new_basis, far, sem):
    del first
    rank, cols = tied.shape
    half = cols // 2
    for start in range(0, half, LANES):
        numer = mirror_lanes(sums[pl.ds((half - LANES - start) // LANES * rank, rank), :])
        at = pl.ds(start, LANES)
        far[:, at] = tied[:, pl.ds(half + start, LANES)] * (0.5 * numer) / scale[:, at]
    copy = pltpu.make_async_copy(far, new_basis.at[:, pl.ds(half, half)], sem)
    copy.start()
    copy.wait()


def over_det(x):
    return lax.ppermute(x, "det", [(0, 1), (1, 0)])


def scan_sum(x):
    count = lax.axis_size("scan")
    steps = count.bit_length() - 1
    if count != 1 << steps:
        return lax.psum(x, "scan")
    for step in range(steps):
        route = []
        for core in range(2):
            stride = 1 << (step + core * (steps // 2)) % steps
            route += [(2 * i + core, 2 * (i ^ stride) + core) for i in range(count)]
        x = x + lax.ppermute(x, ("scan", "det"), route)
    return x


def per_device(spectra, basis, loadings):
    positions, cols = spectra.shape
    rank = basis.shape[0]
    half = cols // 2
    rows = 128
    early = positions // 2
    late = positions - early
    tall = half // LANES * rank
    strip = rank * rank // LANES
    product = 2 * rank * positions * cols
    dma = pltpu.SemaphoreType.DMA

    partner = over_det(basis)
    near_basis, near_loadings, high, low = call(
        functools.partial(load_kernel, rows), "load",
        [(HBM, spectra), (HBM, basis), (HBM, loadings)],
        [(VMEM, basis.shape, F32), (VMEM, loadings.shape, F32), (VMEM, (early, cols), BF16), (VMEM, (early, cols), BF16)],
        [VMEM((early, cols), F32), dma((early // rows,)), dma((2,))],
        moved=4 * early * cols,
    )
    numer, tied, late_high, late_low = call(
        functools.partial(numer_kernel, rows), "numer",
        [(HBM, spectra), (VMEM, near_basis), (VMEM, partner), (VMEM, high), (VMEM, low)],
        [(VMEM, loadings.shape, F32), (VMEM, basis.shape, F32), (VMEM, (late, cols), BF16), (VMEM, (late, cols), BF16)],
        [VMEM((late, cols), F32), dma((late // rows,))],
        flops=3 * product, moved=4 * late * cols,
    )
    other = over_det(numer)
    ratio, = call(ratio_kernel, "ratio", [(VMEM, tied), (VMEM, near_loadings)], [(VMEM, loadings.shape, F32)], flops=product // 16)
    operands = [(VMEM, x) for x in (numer, other, ratio, high, low, late_high, late_low)]
    send, = call(
        functools.partial(send_kernel, 256), "send", operands, [(VMEM, (tall, LANES), F32)], flops=3 * product // 2
    )
    received = over_det(send)
    new_loadings, keep, cross = call(
        functools.partial(keep_kernel, 256), "keep", operands,
        [(HBM, loadings.shape, F32), (VMEM, (tall, LANES), F32), (VMEM, (strip, LANES), F32)],
        [VMEM(loadings.shape, F32), dma(())],
        flops=3 * product // 2,
    )
    sums = scan_sum(jnp.concatenate([keep + received, cross], axis=0))
    others = over_det(sums)
    first, scale = call(
        near_kernel, "near", [(VMEM, tied), (VMEM, sums)],
        [(HBM, basis.shape, F32), (VMEM, (rank, half), F32)],
        [VMEM((rank, half), F32), dma(())],
        flops=product // 32,
    )
    new_basis, = call(
        far_kernel, "far", [(HBM, first), (VMEM, tied), (VMEM, scale), (VMEM, others)],
        [(HBM, basis.shape, F32)],
        [VMEM((rank, half), F32), dma(())],
        aliases={0: 0},
    )
    return new_loadings, new_basis


def solution(mesh):
    in_specs = (P(("grp", "scan"), "det"), P("grp", "det"), P("grp", "scan"))
    out_specs = (P("grp", "scan"), P("grp", "det"))
    return jax.shard_map(
        per_device, mesh=mesh, in_specs=in_specs, out_specs=out_specs, check_vma=False
    )
```

time: 170 us -> 31.4 us (0.18)
  waiting for transfers between devices: 93.6 us -> 11.4 us
  blocking collectives: 35.4 us -> 0 us
  matrix products: 22.3 us -> 0 us
  between operations: 14.1 us -> 0.72 us
  Pallas kernels: 0 us -> 10.5 us
  starting transfers between devices: 0.6 us -> 8.4 us
  local copies, waits for them, and re-layouts: 2.34 us -> 0 us
    psum x2 -> x0, waiting for transfers between devices: 92.2 us -> none  [the longest x1 71.9 us: per_device(): numer_w, cross = lax.psum((w_terms, cross_terms), 'scan')]
    psum x1 -> x0, blocking collectives: 35.4 us -> none  [per_device(): numer_w, cross = lax.psum((w_terms, cross_terms), 'scan')]
    dot_general x6 -> x0, matrix products: 22.3 us -> none  [the longest x1 10.6 us: per_device(): lax.dot_general(tied, spectra, (((1,), (1,)), ((), ())), precision=HIGHEST)]
    pallas_call x0 -> x7, Pallas kernels: none -> 10.5 us  [call(): pl.pallas_call(kernel, out_shape=[memory(shape, dtype) for memory, shape,...]
    ppermute x2 -> x7, waiting for transfers between devices: 1.38 us -> 11.4 us  [the longest x3 10.4 us: scan_sum(): x = x + lax.ppermute(x, ('scan', 'det'), route)]
    ppermute x2 -> x7, starting transfers between devices: 0.52 us -> 8.4 us  [the longest x3 7.47 us: scan_sum(): x = x + lax.ppermute(x, ('scan', 'det'), route)]
    rev x2 -> x0, local copies, waits for them, and re-layouts: 2.33 us -> none  [the longest x1 1.17 us: per_device(): tied_numer = 0.5 * (numer_w + jnp.flip(mirrored, 1))]
  transfers between devices with their start and end apart: 4 -> 7, of which waited for: 3 -> 6; matrix products, arithmetic and copies ran while one was open for 0% -> 0% of each run, Pallas kernels for 0% -> 17%
where the time goes in v2:
time: 31.4 us; the launch traced here: 31.1 us
  waiting for transfers between devices  11.4 us (36%)
  Pallas kernels  10.5 us (33%)
  starting transfers between devices  8.4 us (27%)
  between operations  0.72 us (2%)
    pallas_call x7, Pallas kernels, call(): pl.pallas_call(kernel, out_shape=[memory(shape, dtype) for memory, shape,...  10.5 us
    ppermute x3, waiting for transfers between devices, scan_sum(): x = x + lax.ppermute(x, ('scan', 'det'), route)  10.4 us
    ppermute x3, starting transfers between devices, scan_sum(): x = x + lax.ppermute(x, ('scan', 'det'), route)  7.47 us
    ppermute x4, waiting for transfers between devices, over_det(): return lax.ppermute(x, 'det', [(0, 1), (1, 0)])  1.08 us
    ppermute x4, starting transfers between devices, over_det(): return lax.ppermute(x, 'det', [(0, 1), (1, 0)])  0.93 us
  transfers between devices with their start and end apart: 7, of which 6 were waited for; matrix products, arithmetic and copies ran while one was open for 0% of the time, Pallas kernels for 17%

profile of v2, /device:TPU:0, one launch (start us, length us, event | category | flops | bytes accessed | tf_op | source)
XLA Modules:
  0.0 31.1 jit_solution(3431263933499446244)
XLA Ops:
  0.6 0.5 %collective-permute-start = (f32[32,2048]{1,0:T(8,128)}, f32[32,2048]{1,0:T(8,128)S(1)}, u32[]{:S(2)}, u32[]{:S(2)}) collective-permute-start(f32[32,2048]{1,0:T(8,128)} %basis.1), channel_id=1, source_target_pairs={{0,1},{1,0},{2,3},{3,2},{4,5},{5,4},{6,7},{7,6},{8,9},{9,8},{10,11... | collective-permute-start | bytes 786440 | tf_op jit(solution)/shard_map/ppermute | solution.py:178
  1.1 2.4 %load.1 = (f32[32,2048]{1,0:T(8,128)S(1)}, f32[32,1024]{1,0:T(8,128)S(1)}, bf16[512,2048]{1,0:T(8,128)(2,1)S(1)}, bf16[512,2048]{1,0:T(8,128)(2,1)S(1)}) custom-call(f32[1024,2048]{1,0:T(8,128)} %spectra.3, f32[32,2048]{1,0:T(8,128)} %basis.1, f32[32,1024]{1,0:T(8,128)} %loadings.1), custom_call_target="tpu_custom_call" | custom-call | bytes 4194304 | tf_op jit(solution)/shard_map/load/pallas_call | solution.py:21
  3.6 0.0 collective-permute-done.partner
  3.6 3.6 %numer.1 = (f32[32,1024]{1,0:T(8,128)S(1)}, f32[32,2048]{1,0:T(8,128)S(1)}, bf16[512,2048]{1,0:T(8,128)(2,1)S(1)}, bf16[512,2048]{1,0:T(8,128)(2,1)S(1)}) custom-call(f32[1024,2048]{1,0:T(8,128)} %spectra.3, f32[32,2048]{1,0:T(8,128)S(1)} %get-tuple-element.15.basis, f32[32,2048]{1,0:T(8,128)S(1)} %collective-permute-done.partner, ...), custom_call_target="tpu_custom_call" | custom-call | flops 402653184 | bytes 4194304 | tf_op jit(solution)/shard_map/numer/pallas_call | solution.py:21
  7.3 0.1 collective-permute-start.1
  7.4 0.8 %ratio.1 = f32[32,1024]{1,0:T(8,128)S(1)} custom-call(f32[32,2048]{1,0:T(8,128)S(1)} %get-tuple-element.19.tied, f32[32,1024]{1,0:T(8,128)S(1)} %get-tuple-element.20.loadings), custom_call_target="tpu_custom_call" | custom-call | flops 8388608 | tf_op jit(solution)/shard_map/ratio/pallas_call | solution.py:21
  8.2 0.5 %collective-permute-done.1.other = f32[32,1024]{1,0:T(8,128)S(1)} collective-permute-done((f32[32,1024]{1,0:T(8,128)S(1)}, f32[32,1024]{1,0:T(8,128)S(1)}, u32[]{:S(2)}, u32[]{:S(2)}) %collective-permute-start.1) | collective-permute-done | bytes 131104 | tf_op jit(solution)/shard_map/ppermute | solution.py:178
  8.7 0.9 %send.1 = f32[256,128]{1,0:T(8,128)S(1)} custom-call(f32[32,1024]{1,0:T(8,128)S(1)} %get-tuple-element.18.own, f32[32,1024]{1,0:T(8,128)S(1)} %collective-permute-done.1.other, f32[32,1024]{1,0:T(8,128)S(1)} %ratio.1, bf16[512,2048]{1,0:T(8,128)(2,1)S(1)} %get-tuple-element.16.high, bf16[512,2048]{1,0:T(8,128)(2,1)S(1)} %get-tuple-element.17.low, ...), custom_call_target="tpu_custom_call" | custom-call | flops 201326592 | tf_op jit(solution)/shard_map/send/pallas_call | solution.py:21
  9.6 0.2 collective-permute-start.2
  9.8 1.0 %keep.1 = (f32[32,1024]{1,0:T(8,128)}, f32[256,128]{1,0:T(8,128)S(1)}, f32[8,128]{1,0:T(8,128)S(1)}) custom-call(f32[32,1024]{1,0:T(8,128)S(1)} %get-tuple-element.18.own, f32[32,1024]{1,0:T(8,128)S(1)} %collective-permute-done.1.other, f32[32,1024]{1,0:T(8,128)S(1)} %ratio.1, bf16[512,2048]{1,0:T(8,128)(2,1)S(1)} %get-tuple-element.16.high, ...), custom_call_target="tpu_custom_call" | custom-call | flops 201326592 | tf_op jit(solution)/shard_map/keep/pallas_call | solution.py:21
  10.8 0.2 collective-permute-done.2
  11.0 2.8 %collective-permute-start.3 = (f32[264,128]{1,0:T(8,128)S(1)}, f32[264,128]{1,0:T(8,128)S(1)}, u32[]{:S(2)}, u32[]{:S(2)}) collective-permute-start(f32[264,128]{1,0:T(8,128)S(1)} %pad_maximum_fusion), channel_id=1, source_target_pairs={{0,2},{2,0},{4,6},{6,4},{8,10},{10,8},{12,14},{14,12},{1,5},{3,7},... | collective-permute-start | bytes 405512 | tf_op jit(solution)/shard_map/ppermute | solution.py:191
  13.8 3.0 %collective-permute-done.3 = f32[264,128]{1,0:T(8,128)S(1)} collective-permute-done((f32[264,128]{1,0:T(8,128)S(1)}, f32[264,128]{1,0:T(8,128)S(1)}, u32[]{:S(2)}, u32[]{:S(2)}) %collective-permute-start.3) | collective-permute-done | bytes 135200 | tf_op jit(solution)/shard_map/ppermute | solution.py:191
  16.8 2.1 %collective-permute-start.4 = (f32[264,128]{1,0:T(8,128)S(1)}, f32[264,128]{1,0:T(8,128)S(1)}, u32[]{:S(2)}, u32[]{:S(2)}) collective-permute-start(f32[264,128]{1,0:T(8,128)S(1)} %fusion), channel_id=1, source_target_pairs={{0,4},{2,6},{4,0},{6,2},{8,12},{10,14},{12,8},{14,10},{1,9},{3,11}... | collective-permute-start | bytes 405512 | tf_op jit(solution)/shard_map/ppermute | solution.py:191
  19.0 4.0 %collective-permute-done.4 = f32[264,128]{1,0:T(8,128)S(1)} collective-permute-done((f32[264,128]{1,0:T(8,128)S(1)}, f32[264,128]{1,0:T(8,128)S(1)}, u32[]{:S(2)}, u32[]{:S(2)}) %collective-permute-start.4) | collective-permute-done | bytes 135200 | tf_op jit(solution)/shard_map/ppermute | solution.py:191
  22.9 2.6 %collective-permute-start.5 = (f32[264,128]{1,0:T(8,128)S(1)}, f32[264,128]{1,0:T(8,128)S(1)}, u32[]{:S(2)}, u32[]{:S(2)}) collective-permute-start(f32[264,128]{1,0:T(8,128)S(1)} %add.14), channel_id=1, source_target_pairs={{0,8},{2,10},{4,12},{6,14},{8,0},{10,2},{12,4},{14,6},{1,3},{3,1},... | collective-permute-start | bytes 405512 | tf_op jit(solution)/shard_map/ppermute | solution.py:191
  25.5 3.4 %collective-permute-done.5 = f32[264,128]{1,0:T(8,128)S(1)} collective-permute-done((f32[264,128]{1,0:T(8,128)S(1)}, f32[264,128]{1,0:T(8,128)S(1)}, u32[]{:S(2)}, u32[]{:S(2)}) %collective-permute-start.5) | collective-permute-done | bytes 135200 | tf_op jit(solution)/shard_map/ppermute | solution.py:191
  28.9 0.1 collective-permute-start.6
  29.0 1.0 %near.1 = (f32[32,2048]{1,0:T(8,128)}, f32[32,1024]{1,0:T(8,128)S(1)}) custom-call(f32[32,2048]{1,0:T(8,128)S(1)} %get-tuple-element.19.tied, f32[264,128]{1,0:T(8,128)S(1)} %add.15.sums), custom_call_target="tpu_custom_call" | custom-call | flops 4194304 | tf_op jit(solution)/shard_map/near/pallas_call | solution.py:21
  30.0 0.4 %collective-permute-done.6.sums = f32[264,128]{1,0:T(8,128)S(1)} collective-permute-done((f32[264,128]{1,0:T(8,128)S(1)}, f32[264,128]{1,0:T(8,128)S(1)}, u32[]{:S(2)}, u32[]{:S(2)}) %collective-permute-start.6) | collective-permute-done | bytes 135200 | tf_op jit(solution)/shard_map/ppermute | solution.py:178
  30.3 0.8 %far.1 = f32[32,2048]{1,0:T(8,128)} custom-call(f32[32,2048]{1,0:T(8,128)} %get-tuple-element.26.first, f32[32,2048]{1,0:T(8,128)S(1)} %get-tuple-element.19.tied, f32[32,1024]{1,0:T(8,128)S(1)} %get-tuple-element.27.scale, f32[264,128]{1,0:T(8,128)S(1)} %collective-permute-done.6.sums), custom_call_target="tpu_custom_call", output_to_operand_aliasing={{}: (0, {})} | custom-call | tf_op jit(solution)/shard_map/far/pallas_call | solution.py:21
  (5 shorter events, 0.1 us)
Async XLA Ops:
  0.6 3.0 %collective-permute-start = (f32[32,2048]{1,0:T(8,128)}, f32[32,2048]{1,0:T(8,128)S(1)}, u32[]{:S(2)}, u32[]{:S(2)}) collective-permute-start(f32[32,2048]{1,0:T(8,128)} %basis.1), channel_id=1, source_target_pairs={{0,1},{1,0},{2,3},{3,2},{4,5},{5,4},{6,7},{7,6},{8,9},{9,8},{10,11... | collective-permute-start | bytes 786440 | tf_op jit(solution)/shard_map/ppermute | solution.py:178
  7.3 1.4 %collective-permute-start.1 = (f32[32,1024]{1,0:T(8,128)S(1)}, f32[32,1024]{1,0:T(8,128)S(1)}, u32[]{:S(2)}, u32[]{:S(2)}) collective-permute-start(f32[32,1024]{1,0:T(8,128)S(1)} %get-tuple-element.18.own), channel_id=1, source_target_pairs={{0,1},{1,0},{2,3},{3,2},{4,5},{5,4},{6,7},{7,6},{8,9},{9,8},{10,11... | collective-permute-start | bytes 393224 | tf_op jit(solution)/shard_map/ppermute | solution.py:178
  9.6 1.4 %collective-permute-start.2 = (f32[256,128]{1,0:T(8,128)S(1)}, f32[256,128]{1,0:T(8,128)S(1)}, u32[]{:S(2)}, u32[]{:S(2)}) collective-permute-start(f32[256,128]{1,0:T(8,128)S(1)} %send.1), channel_id=1, source_target_pairs={{0,1},{1,0},{2,3},{3,2},{4,5},{5,4},{6,7},{7,6},{8,9},{9,8},{10,11... | collective-permute-start | bytes 393224 | tf_op jit(solution)/shard_map/ppermute | solution.py:178
  11.0 5.8 %collective-permute-start.3 = (f32[264,128]{1,0:T(8,128)S(1)}, f32[264,128]{1,0:T(8,128)S(1)}, u32[]{:S(2)}, u32[]{:S(2)}) collective-permute-start(f32[264,128]{1,0:T(8,128)S(1)} %pad_maximum_fusion), channel_id=1, source_target_pairs={{0,2},{2,0},{4,6},{6,4},{8,10},{10,8},{12,14},{14,12},{1,5},{3,7},... | collective-permute-start | bytes 405512 | tf_op jit(solution)/shard_map/ppermute | solution.py:191
  16.8 6.1 %collective-permute-start.4 = (f32[264,128]{1,0:T(8,128)S(1)}, f32[264,128]{1,0:T(8,128)S(1)}, u32[]{:S(2)}, u32[]{:S(2)}) collective-permute-start(f32[264,128]{1,0:T(8,128)S(1)} %fusion), channel_id=1, source_target_pairs={{0,4},{2,6},{4,0},{6,2},{8,12},{10,14},{12,8},{14,10},{1,9},{3,11}... | collective-permute-start | bytes 405512 | tf_op jit(solution)/shard_map/ppermute | solution.py:191
  22.9 6.0 %collective-permute-start.5 = (f32[264,128]{1,0:T(8,128)S(1)}, f32[264,128]{1,0:T(8,128)S(1)}, u32[]{:S(2)}, u32[]{:S(2)}) collective-permute-start(f32[264,128]{1,0:T(8,128)S(1)} %add.14), channel_id=1, source_target_pairs={{0,8},{2,10},{4,12},{6,14},{8,0},{10,2},{12,4},{14,6},{1,3},{3,1},... | collective-permute-start | bytes 405512 | tf_op jit(solution)/shard_map/ppermute | solution.py:191
  28.9 1.4 %collective-permute-start.6 = (f32[264,128]{1,0:T(8,128)S(1)}, f32[264,128]{1,0:T(8,128)S(1)}, u32[]{:S(2)}, u32[]{:S(2)}) collective-permute-start(f32[264,128]{1,0:T(8,128)S(1)} %add.15.sums), channel_id=1, source_target_pairs={{0,1},{1,0},{2,3},{3,2},{4,5},{5,4},{6,7},{7,6},{8,9},{9,8},{10,11... | collective-permute-start | bytes 405512 | tf_op jit(solution)/shard_map/ppermute | solution.py:178

commit v3 on v2

--- a/solution.py
+++ b/solution.py
@@ -16,7 +16,7 @@
 HBM, VMEM = pltpu.HBM, pltpu.VMEM
 
 
-def call(kernel, name, ins, outs, scratch=(), flops=0, moved=0, aliases={}):
+def call(kernel, name, ins, outs, scratch=(), flops=0, moved=0):
     params = pltpu.CompilerParams(vmem_limit_bytes=16 * MIB)
     return pl.pallas_call(
         kernel,
@@ -24,7 +24,6 @@
         in_specs=[pl.BlockSpec(memory_space=memory) for memory, _ in ins],
         out_specs=[pl.BlockSpec(memory_space=memory) for memory, _, _ in outs],
         scratch_shapes=list(scratch),
-        input_output_aliases=aliases,
         compiler_params=params,
         cost_estimate=pl.CostEstimate(flops=flops, bytes_accessed=moved, transcendentals=0),
         name=name,
@@ -117,25 +116,51 @@
     return terms[:rank] + terms[rank:] + rest
 
 
+def odd_chip():
+    count = lax.axis_size("scan")
+    index = lax.axis_index("scan")
+    ones = sum(index // (1 << bit) % 2 for bit in range(scan_steps()))
+    return ones % 2 if count == 1 << scan_steps() else index * 0
+
+
+def scan_steps():
+    return lax.axis_size("scan").bit_length() - 1
+
+
+def place(block, blocks, turned):
+    return block + turned * (blocks - 1 - 2 * block)
+
+
+def maybe_mirror(block, turned):
+    lane = lax.broadcasted_iota(jnp.int32, block.shape, 1)
+    return jnp.take_along_axis(block, place(lane, LANES, turned), axis=1, mode="promise_in_bounds")
+
+
+def half_terms(width, new, arrays, turned, first, out):
+    rank, cols = new.shape[0], arrays[0].shape[1]
+    half, last = cols // 2, first + out.shape[0] // rank
+    wide = width // LANES
+    for block in range(first, last, wide):
+        group = min(wide, last - block)
+        start = block * LANES + turned * (half + (half // LANES - 2 * block - group) * LANES)
+        terms = column_terms(new, *arrays, pl.ds(pl.multiple_of(start, LANES), group * LANES))
+        for b in range(group):
+            row = (block - first + place(b, group, turned)) * rank
+            part = maybe_mirror(terms[:, b * LANES:(b + 1) * LANES], turned)
+            out[pl.ds(pl.multiple_of(row, rank), rank), :] = part
+
+
 def send_kernel(width, own, other, ratio, high, low, late_high, late_low, send):
-    rank, cols = own.shape[0], high.shape[1]
     new = ratio[...] * (own[...] + other[...])
-    for start in range(cols // 2, cols, width):
-        terms = column_terms(new, high, low, late_high, late_low, pl.ds(start, width))
-        for b in range(0, width, LANES):
-            turned = (cols - LANES - start - b) // LANES * rank
-            send[pl.ds(turned, rank), :] = mirror_lanes(terms[:, b:b + LANES])
+    half_terms(width, new, (high, low, late_high, late_low), 1 - odd_chip(), 0, send)
 
 
 def keep_kernel(width, own, other, ratio, high, low, late_high, late_low, new_loadings, keep, cross, new, sem):
-    rank, cols = own.shape[0], high.shape[1]
+    rank = own.shape[0]
     new[...] = ratio[...] * (own[...] + other[...])
     copy = pltpu.make_async_copy(new, new_loadings, sem)
     copy.start()
-    for start in range(0, cols // 2, width):
-        terms = column_terms(new[...], high, low, late_high, late_low, pl.ds(start, width))
-        for b in range(0, width, LANES):
-            keep[pl.ds((start + b) // LANES * rank, rank), :] = terms[:, b:b + LANES]
+    half_terms(width, new[...], (high, low, late_high, late_low), odd_chip(), 0, keep)
     square = dot(new[...], new[...], NT, HIGHEST)
     per_row = LANES // rank
     strip = rank // per_row
@@ -143,53 +168,73 @@
     copy.wait()
 
 
-def near_kernel(tied, sums, new_basis, scale, near, sem):
+def half_basis(tied, scale, numers, turned, out):
     rank, cols = tied.shape
     half = cols // 2
+    for block in range(half // LANES):
+        numer = maybe_mirror(numers[block * rank:(block + 1) * rank], turned)
+        column = place(block, half // LANES, turned) * LANES
+        at = pl.ds(pl.multiple_of(turned * half + column, LANES), LANES)
+        out[:, pl.ds(pl.multiple_of(column, LANES), LANES)] = tied[:, at] * (0.5 * numer) / scale[:, at]
+
+
+def near_kernel(tied, sums, more, scale, near):
+    rank = tied.shape[0]
     per_row = LANES // rank
     strip = rank // per_row
-    packed = sums[pl.ds(half // LANES * rank, strip), :]
+    packed = sums[:strip, :]
     cross = jnp.concatenate([packed[:, i * rank:(i + 1) * rank] for i in range(per_row)], axis=0)
-    whole = dot(cross, tied[...], NN, HIGHEST)
-    scale[...] = whole[:, half:]
-    for start in range(0, half, LANES):
-        numer = sums[pl.ds(start // LANES * rank, rank), :]
-        at = pl.ds(start, LANES)
-        near[:, at] = tied[:, at] * (0.5 * numer) / whole[:, start:start + LANES]
-    copy = pltpu.make_async_copy(near, new_basis.at[:, pl.ds(0, half)], sem)
-    copy.start()
-    copy.wait()
-
-
-def far_kernel(first, tied, scale, sums, new_basis, far, sem):
-    del first
-    rank, cols = tied.shape
-    half = cols // 2
-    for start in range(0, half, LANES):
-        numer = mirror_lanes(sums[pl.ds((half - LANES - start) // LANES * rank, rank), :])
-        at = pl.ds(start, LANES)
-        far[:, at] = tied[:, pl.ds(half + start, LANES)] * (0.5 * numer) / scale[:, at]
-    copy = pltpu.make_async_copy(far, new_basis.at[:, pl.ds(half, half)], sem)
-    copy.start()
-    copy.wait()
+    scale[...] = dot(cross, tied[...], NN, HIGHEST)
+    numers = jnp.concatenate([sums[strip:, :], more[...]], axis=0)
+    half_basis(tied, scale, numers, odd_chip(), near)
+
+
+def far_kernel(tied, scale, near, sums, more, new_basis, far, sems):
+    half = near.shape[1]
+    odd = odd_chip()
+    copies = [
+        pltpu.make_async_copy(
+            part, new_basis.at[:, pl.ds(pl.multiple_of(turned * half, LANES), half)], sems.at[i]
+        )
+        for i, (part, turned) in enumerate(((near, odd), (far, 1 - odd)))
+    ]
+    copies[0].start()
+    numers = jnp.concatenate([sums[...], more[...]], axis=0)
+    half_basis(tied, scale, numers, 1 - odd, far)
+    copies[1].start()
+    for copy in copies:
+        copy.wait()
 
 
 def over_det(x):
     return lax.ppermute(x, "det", [(0, 1), (1, 0)])
 
 
-def scan_sum(x):
-    count = lax.axis_size("scan")
-    steps = count.bit_length() - 1
+def stride_orders(steps):
+    cuts = [round(steps * i / 3) for i in range(4)]
+    groups = [list(range(a, b)) for a, b in zip(cuts, cuts[1:])]
+    return [
+        [sum((groups[g] for g in order), []) for order in stream]
+        for stream in (((1, 0, 2), (0, 2, 1)), ((1, 2, 0), (2, 1, 0)))
+    ]
+
+
+def scan_sums(parts):
+    count, steps = lax.axis_size("scan"), scan_steps()
     if count != 1 << steps:
-        return lax.psum(x, "scan")
+        return lax.psum(parts, "scan")
+    orders = stride_orders(steps)
     for step in range(steps):
-        route = []
-        for core in range(2):
-            stride = 1 << (step + core * (steps // 2)) % steps
-            route += [(2 * i + core, 2 * (i ^ stride) + core) for i in range(count)]
-        x = x + lax.ppermute(x, ("scan", "det"), route)
-    return x
+        received = []
+        for part, order in zip(parts, orders):
+            route = []
+            for i in range(count):
+                for core in range(2):
+                    half = (core + i.bit_count()) % 2
+                    route.append((2 * i + core, 2 * (i ^ 1 << order[half][step]) + 1 - core))
+            received.append(lax.ppermute(part, ("scan", "det"), route))
+        parts = [part + other for part, other in zip(parts, received)]
+    return parts
 
 
 def per_device(spectra, basis, loadings):
@@ -213,10 +258,10 @@
         moved=4 * early * cols,
     )
     numer, tied, late_high, late_low = call(
-        functools.partial(numer_kernel, rows), "numer",
+        functools.partial(numer_kernel, 2 * rows), "numer",
         [(HBM, spectra), (VMEM, near_basis), (VMEM, partner), (VMEM, high), (VMEM, low)],
         [(VMEM, loadings.shape, F32), (VMEM, basis.shape, F32), (VMEM, (late, cols), BF16), (VMEM, (late, cols), BF16)],
-        [VMEM((late, cols), F32), dma((late // rows,))],
+        [VMEM((late, cols), F32), dma((late // (2 * rows),))],
         flops=3 * product, moved=4 * late * cols,
     )
     other = over_det(numer)
@@ -232,19 +277,20 @@
         [VMEM(loadings.shape, F32), dma(())],
         flops=3 * product // 2,
     )
-    sums = scan_sum(jnp.concatenate([keep + received, cross], axis=0))
-    others = over_det(sums)
-    first, scale = call(
-        near_kernel, "near", [(VMEM, tied), (VMEM, sums)],
-        [(HBM, basis.shape, F32), (VMEM, (rank, half), F32)],
-        [VMEM((rank, half), F32), dma(())],
+    folded = keep + received
+    cut = tall // 2
+    parts = (jnp.concatenate([cross, folded[:cut]], axis=0), folded[cut:])
+    sums = scan_sums(lax.optimization_barrier(parts))
+    others = [over_det(sums[0][strip:]), over_det(sums[1])]
+    scale, near = call(
+        near_kernel, "near", [(VMEM, tied), (VMEM, sums[0]), (VMEM, sums[1])],
+        [(VMEM, basis.shape, F32), (VMEM, (rank, half), F32)],
         flops=product // 32,
     )
     new_basis, = call(
-        far_kernel, "far", [(HBM, first), (VMEM, tied), (VMEM, scale), (VMEM, others)],
+        far_kernel, "far", [(VMEM, x) for x in (tied, scale, near, *others)],
         [(HBM, basis.shape, F32)],
-        [VMEM((rank, half), F32), dma(())],
-        aliases={0: 0},
+        [VMEM((rank, half), F32), dma((2,))],
     )
     return new_loadings, new_basis
 

time: 31.4 us -> 29.5 us (0.939)
  waiting for transfers between devices: 11.4 us -> 5.3 us
  starting transfers between devices: 8.4 us -> 13.4 us
  Pallas kernels: 10.5 us -> 9.88 us
    ppermute x3 -> x6, waiting for transfers between devices: 10.4 us -> 4.31 us  [scan_sums(): received.append(lax.ppermute(part, ('scan', 'det'), route))]
    ppermute x3 -> x6, starting transfers between devices: 7.47 us -> 11.9 us  [scan_sums(): received.append(lax.ppermute(part, ('scan', 'det'), route))]
    pallas_call x7, Pallas kernels: 10.5 us -> 9.88 us  [call(): pl.pallas_call(kernel, out_shape=[memory(shape, dtype) for memory, shape,...]
    ppermute x4 -> x5, starting transfers between devices: 0.93 us -> 1.49 us  [over_det(): return lax.ppermute(x, 'det', [(0, 1), (1, 0)])]
    ppermute x4 -> x5, waiting for transfers between devices: 1.08 us -> 1 us  [over_det(): return lax.ppermute(x, 'det', [(0, 1), (1, 0)])]
  transfers between devices with their start and end apart: 7 -> 11, of which waited for: 6 -> 6; matrix products, arithmetic and copies ran while one was open for 0% -> 0% of each run, Pallas kernels for 17% -> 17%
where the time goes in v3:
time: 29.5 us; the launch traced here: 29.4 us
  starting transfers between devices  13.4 us (45%)
  Pallas kernels  9.88 us (33%)
  waiting for transfers between devices  5.3 us (18%)
  between operations  0.75 us (3%)
    ppermute x6, starting transfers between devices, scan_sums(): received.append(lax.ppermute(part, ('scan', 'det'), route))  11.9 us
    pallas_call x7, Pallas kernels, call(): pl.pallas_call(kernel, out_shape=[memory(shape, dtype) for memory, shape,...  9.88 us
    ppermute x6, waiting for transfers between devices, scan_sums(): received.append(lax.ppermute(part, ('scan', 'det'), route))  4.31 us
    ppermute x5, starting transfers between devices, over_det(): return lax.ppermute(x, 'det', [(0, 1), (1, 0)])  1.49 us
    ppermute x5, waiting for transfers between devices, over_det(): return lax.ppermute(x, 'det', [(0, 1), (1, 0)])  1 us
  transfers between devices with their start and end apart: 11, of which 6 were waited for; matrix products, arithmetic and copies ran while one was open for 0% of the time, Pallas kernels for 17%

profile of v3, /device:TPU:0, one launch (start us, length us, event | category | flops | bytes accessed | tf_op | source)
XLA Modules:
  0.0 29.4 jit_solution(4842465519819517928)
XLA Ops:
  0.6 0.5 %collective-permute-start = (f32[32,2048]{1,0:T(8,128)}, f32[32,2048]{1,0:T(8,128)S(1)}, u32[]{:S(2)}, u32[]{:S(2)}) collective-permute-start(f32[32,2048]{1,0:T(8,128)} %basis.1), channel_id=1, source_target_pairs={{0,1},{1,0},{2,3},{3,2},{4,5},{5,4},{6,7},{7,6},{8,9},{9,8},{10,11... | collective-permute-start | bytes 786440 | tf_op jit(solution)/shard_map/ppermute | solution.py:210
  1.1 2.4 %load.1 = (f32[32,2048]{1,0:T(8,128)S(1)}, f32[32,1024]{1,0:T(8,128)S(1)}, bf16[512,2048]{1,0:T(8,128)(2,1)S(1)}, bf16[512,2048]{1,0:T(8,128)(2,1)S(1)}) custom-call(f32[1024,2048]{1,0:T(8,128)} %spectra.3, f32[32,2048]{1,0:T(8,128)} %basis.1, f32[32,1024]{1,0:T(8,128)} %loadings.1), custom_call_target="tpu_custom_call" | custom-call | bytes 4194304 | tf_op jit(solution)/shard_map/load/pallas_call | solution.py:21
  3.6 0.0 collective-permute-done.partner
  3.6 3.3 %numer.1 = (f32[32,1024]{1,0:T(8,128)S(1)}, f32[32,2048]{1,0:T(8,128)S(1)}, bf16[512,2048]{1,0:T(8,128)(2,1)S(1)}, bf16[512,2048]{1,0:T(8,128)(2,1)S(1)}) custom-call(f32[1024,2048]{1,0:T(8,128)} %spectra.3, f32[32,2048]{1,0:T(8,128)S(1)} %get-tuple-element.17.basis, f32[32,2048]{1,0:T(8,128)S(1)} %collective-permute-done.partner, ...), custom_call_target="tpu_custom_call" | custom-call | flops 402653184 | bytes 4194304 | tf_op jit(solution)/shard_map/numer/pallas_call | solution.py:21
  6.9 0.1 collective-permute-start.1
  7.0 0.7 %ratio.1 = f32[32,1024]{1,0:T(8,128)S(1)} custom-call(f32[32,2048]{1,0:T(8,128)S(1)} %get-tuple-element.21.tied, f32[32,1024]{1,0:T(8,128)S(1)} %get-tuple-element.22.loadings), custom_call_target="tpu_custom_call" | custom-call | flops 8388608 | tf_op jit(solution)/shard_map/ratio/pallas_call | solution.py:21
  7.8 0.5 %collective-permute-done.1.other = f32[32,1024]{1,0:T(8,128)S(1)} collective-permute-done((f32[32,1024]{1,0:T(8,128)S(1)}, f32[32,1024]{1,0:T(8,128)S(1)}, u32[]{:S(2)}, u32[]{:S(2)}) %collective-permute-start.1) | collective-permute-done | bytes 131104 | tf_op jit(solution)/shard_map/ppermute | solution.py:210
  8.3 0.9 %send.1 = f32[256,128]{1,0:T(8,128)S(1)} custom-call(f32[32,1024]{1,0:T(8,128)S(1)} %get-tuple-element.20.own, f32[32,1024]{1,0:T(8,128)S(1)} %collective-permute-done.1.other, f32[32,1024]{1,0:T(8,128)S(1)} %ratio.1, bf16[512,2048]{1,0:T(8,128)(2,1)S(1)} %get-tuple-element.18.high, bf16[512,2048]{1,0:T(8,128)(2,1)S(1)} %get-tuple-element.19.low, ...), custom_call_target="tpu_custom_call" | custom-call | flops 201326592 | tf_op jit(solution)/shard_map/send/pallas_call | solution.py:21
  9.2 0.2 collective-permute-start.2
  9.5 1.3 %keep.1 = (f32[32,1024]{1,0:T(8,128)}, f32[256,128]{1,0:T(8,128)S(1)}, f32[8,128]{1,0:T(8,128)S(1)}) custom-call(f32[32,1024]{1,0:T(8,128)S(1)} %get-tuple-element.20.own, f32[32,1024]{1,0:T(8,128)S(1)} %collective-permute-done.1.other, f32[32,1024]{1,0:T(8,128)S(1)} %ratio.1, bf16[512,2048]{1,0:T(8,128)(2,1)S(1)} %get-tuple-element.18.high, ...), custom_call_target="tpu_custom_call" | custom-call | flops 201326592 | tf_op jit(solution)/shard_map/keep/pallas_call | solution.py:21
  10.7 0.0 collective-permute-done.2
  10.8 2.7 %collective-permute-start.3 = (f32[136,128]{1,0:T(8,128)S(1)}, f32[136,128]{1,0:T(8,128)S(1)}, u32[]{:S(2)}, u32[]{:S(2)}) collective-permute-start(f32[136,128]{1,0:T(8,128)S(1)} %pad_maximum_fusion), channel_id=1, source_target_pairs={{0,5},{1,2},{2,1},{3,6},{4,7},{5,0},{6,3},{7,4},{8,11},{9,12},{10,... | collective-permute-start | bytes 208904 | tf_op jit(solution)/shard_map/ppermute | solution.py:235
  13.5 0.1 collective-permute-start.6
  13.6 1.9 %collective-permute-done.3 = f32[136,128]{1,0:T(8,128)S(1)} collective-permute-done((f32[136,128]{1,0:T(8,128)S(1)}, f32[136,128]{1,0:T(8,128)S(1)}, u32[]{:S(2)}, u32[]{:S(2)}) %collective-permute-start.3) | collective-permute-done | bytes 69664 | tf_op jit(solution)/shard_map/ppermute | solution.py:235
  15.5 1.7 %collective-permute-start.4 = (f32[136,128]{1,0:T(8,128)S(1)}, f32[136,128]{1,0:T(8,128)S(1)}, u32[]{:S(2)}, u32[]{:S(2)}) collective-permute-start(f32[136,128]{1,0:T(8,128)S(1)} %add.22), channel_id=1, source_target_pairs={{0,3},{1,8},{2,11},{3,0},{4,13},{5,6},{6,5},{7,14},{8,1},{9,10},{1... | collective-permute-start | bytes 208904 | tf_op jit(solution)/shard_map/ppermute | solution.py:235
  17.3 0.0 collective-permute-done.6
  17.3 2.8 %collective-permute-start.7 = (f32[128,128]{1,0:T(8,128)S(1)}, f32[128,128]{1,0:T(8,128)S(1)}, u32[]{:S(2)}, u32[]{:S(2)}) collective-permute-start(f32[128,128]{1,0:T(8,128)S(1)} %add.25), channel_id=1, source_target_pairs={{0,9},{1,4},{2,7},{3,10},{4,1},{5,12},{6,15},{7,2},{8,13},{9,0},{1... | collective-permute-start | bytes 196616 | tf_op jit(solution)/shard_map/ppermute | solution.py:235
  20.2 0.0 collective-permute-done.4
  20.2 2.3 %collective-permute-start.5 = (f32[136,128]{1,0:T(8,128)S(1)}, f32[136,128]{1,0:T(8,128)S(1)}, u32[]{:S(2)}, u32[]{:S(2)}) collective-permute-start(f32[136,128]{1,0:T(8,128)S(1)} %add.23), channel_id=1, source_target_pairs={{0,9},{1,4},{2,7},{3,10},{4,1},{5,12},{6,15},{7,2},{8,13},{9,0},{1... | collective-permute-start | bytes 208904 | tf_op jit(solution)/shard_map/ppermute | solution.py:235
  22.5 0.1 collective-permute-done.7
  22.6 2.2 %collective-permute-start.8 = (f32[128,128]{1,0:T(8,128)S(1)}, f32[128,128]{1,0:T(8,128)S(1)}, u32[]{:S(2)}, u32[]{:S(2)}) collective-permute-start(f32[128,128]{1,0:T(8,128)S(1)} %add.26), channel_id=1, source_target_pairs={{0,3},{1,2},{2,1},{3,0},{4,7},{5,6},{6,5},{7,4},{8,11},{9,10},{10,... | collective-permute-start | bytes 196616 | tf_op jit(solution)/shard_map/ppermute | solution.py:235
  24.7 2.3 %collective-permute-done.8 = f32[128,128]{1,0:T(8,128)S(1)} collective-permute-done((f32[128,128]{1,0:T(8,128)S(1)}, f32[128,128]{1,0:T(8,128)S(1)}, u32[]{:S(2)}, u32[]{:S(2)}) %collective-permute-start.8) | collective-permute-done | bytes 65568 | tf_op jit(solution)/shard_map/ppermute | solution.py:235
  27.0 0.2 collective-permute-start.10
  27.3 0.0 collective-permute-done.5
  27.3 0.4 %collective-permute-start.9 = (f32[128,128]{1,0:T(8,128)S(1)}, f32[128,128]{1,0:T(8,128)S(1)}, u32[]{:S(2)}, u32[]{:S(2)}) collective-permute-start(f32[128,128]{1,0:T(8,128)S(1)} %slice.14), channel_id=1, source_target_pairs={{0,1},{1,0},{2,3},{3,2},{4,5},{5,4},{6,7},{7,6},{8,9},{9,8},{10,11... | collective-permute-start | bytes 196616 | tf_op jit(solution)/shard_map/ppermute | solution.py:210
  27.7 0.4 %near.1 = (f32[32,2048]{1,0:T(8,128)S(1)}, f32[32,1024]{1,0:T(8,128)S(1)}) custom-call(f32[32,2048]{1,0:T(8,128)S(1)} %get-tuple-element.21.tied, f32[136,128]{1,0:T(8,128)S(1)} %add.24.sums, f32[128,128]{1,0:T(8,128)S(1)} %add.27.more), custom_call_target="tpu_custom_call" | custom-call | flops 4194304 | tf_op jit(solution)/shard_map/near/pallas_call | solution.py:21
  28.2 0.2 collective-permute-done.10.more
  28.4 0.3 collective-permute-done.9.sums
  28.6 0.8 %far.1 = f32[32,2048]{1,0:T(8,128)} custom-call(f32[32,2048]{1,0:T(8,128)S(1)} %get-tuple-element.21.tied, f32[32,2048]{1,0:T(8,128)S(1)} %get-tuple-element.30.scale, f32[32,1024]{1,0:T(8,128)S(1)} %get-tuple-element.31.near, f32[128,128]{1,0:T(8,128)S(1)} %collective-permute-done.9.sums, f32[128,128]{1,0:T(8,128)S(1)} %collective-permute-done.10.more), custom_call_target="tpu_custom_call" | custom-call | tf_op jit(solution)/shard_map/far/pallas_call | solution.py:21
  (10 shorter events, 0.1 us)
Async XLA Ops:
  0.6 3.0 %collective-permute-start = (f32[32,2048]{1,0:T(8,128)}, f32[32,2048]{1,0:T(8,128)S(1)}, u32[]{:S(2)}, u32[]{:S(2)}) collective-permute-start(f32[32,2048]{1,0:T(8,128)} %basis.1), channel_id=1, source_target_pairs={{0,1},{1,0},{2,3},{3,2},{4,5},{5,4},{6,7},{7,6},{8,9},{9,8},{10,11... | collective-permute-start | bytes 786440 | tf_op jit(solution)/shard_map/ppermute | solution.py:210
  6.9 1.4 %collective-permute-start.1 = (f32[32,1024]{1,0:T(8,128)S(1)}, f32[32,1024]{1,0:T(8,128)S(1)}, u32[]{:S(2)}, u32[]{:S(2)}) collective-permute-start(f32[32,1024]{1,0:T(8,128)S(1)} %get-tuple-element.20.own), channel_id=1, source_target_pairs={{0,1},{1,0},{2,3},{3,2},{4,5},{5,4},{6,7},{7,6},{8,9},{9,8},{10,11... | collective-permute-start | bytes 393224 | tf_op jit(solution)/shard_map/ppermute | solution.py:210
  9.2 1.5 %collective-permute-start.2 = (f32[256,128]{1,0:T(8,128)S(1)}, f32[256,128]{1,0:T(8,128)S(1)}, u32[]{:S(2)}, u32[]{:S(2)}) collective-permute-start(f32[256,128]{1,0:T(8,128)S(1)} %send.1), channel_id=1, source_target_pairs={{0,1},{1,0},{2,3},{3,2},{4,5},{5,4},{6,7},{7,6},{8,9},{9,8},{10,11... | collective-permute-start | bytes 393224 | tf_op jit(solution)/shard_map/ppermute | solution.py:210
  10.8 4.7 %collective-permute-start.3 = (f32[136,128]{1,0:T(8,128)S(1)}, f32[136,128]{1,0:T(8,128)S(1)}, u32[]{:S(2)}, u32[]{:S(2)}) collective-permute-start(f32[136,128]{1,0:T(8,128)S(1)} %pad_maximum_fusion), channel_id=1, source_target_pairs={{0,5},{1,2},{2,1},{3,6},{4,7},{5,0},{6,3},{7,4},{8,11},{9,12},{10,... | collective-permute-start | bytes 208904 | tf_op jit(solution)/shard_map/ppermute | solution.py:235
  13.5 3.8 %collective-permute-start.6 = (f32[128,128]{1,0:T(8,128)S(1)}, f32[128,128]{1,0:T(8,128)S(1)}, u32[]{:S(2)}, u32[]{:S(2)}) collective-permute-start(f32[128,128]{1,0:T(8,128)S(1)} %get-tuple-element.29), channel_id=1, source_target_pairs={{0,5},{1,8},{2,11},{3,6},{4,13},{5,0},{6,3},{7,14},{8,1},{9,12},{1... | collective-permute-start | bytes 196616 | tf_op jit(solution)/shard_map/ppermute | solution.py:235
  15.5 4.6 %collective-permute-start.4 = (f32[136,128]{1,0:T(8,128)S(1)}, f32[136,128]{1,0:T(8,128)S(1)}, u32[]{:S(2)}, u32[]{:S(2)}) collective-permute-start(f32[136,128]{1,0:T(8,128)S(1)} %add.22), channel_id=1, source_target_pairs={{0,3},{1,8},{2,11},{3,0},{4,13},{5,6},{6,5},{7,14},{8,1},{9,10},{1... | collective-permute-start | bytes 208904 | tf_op jit(solution)/shard_map/ppermute | solution.py:235
  17.3 5.2 %collective-permute-start.7 = (f32[128,128]{1,0:T(8,128)S(1)}, f32[128,128]{1,0:T(8,128)S(1)}, u32[]{:S(2)}, u32[]{:S(2)}) collective-permute-start(f32[128,128]{1,0:T(8,128)S(1)} %add.25), channel_id=1, source_target_pairs={{0,9},{1,4},{2,7},{3,10},{4,1},{5,12},{6,15},{7,2},{8,13},{9,0},{1... | collective-permute-start | bytes 196616 | tf_op jit(solution)/shard_map/ppermute | solution.py:235
  20.2 7.1 %collective-permute-start.5 = (f32[136,128]{1,0:T(8,128)S(1)}, f32[136,128]{1,0:T(8,128)S(1)}, u32[]{:S(2)}, u32[]{:S(2)}) collective-permute-start(f32[136,128]{1,0:T(8,128)S(1)} %add.23), channel_id=1, source_target_pairs={{0,9},{1,4},{2,7},{3,10},{4,1},{5,12},{6,15},{7,2},{8,13},{9,0},{1... | collective-permute-start | bytes 208904 | tf_op jit(solution)/shard_map/ppermute | solution.py:235
  22.6 4.5 %collective-permute-start.8 = (f32[128,128]{1,0:T(8,128)S(1)}, f32[128,128]{1,0:T(8,128)S(1)}, u32[]{:S(2)}, u32[]{:S(2)}) collective-permute-start(f32[128,128]{1,0:T(8,128)S(1)} %add.26), channel_id=1, source_target_pairs={{0,3},{1,2},{2,1},{3,0},{4,7},{5,6},{6,5},{7,4},{8,11},{9,10},{10,... | collective-permute-start | bytes 196616 | tf_op jit(solution)/shard_map/ppermute | solution.py:235
  27.0 1.3 %collective-permute-start.10 = (f32[128,128]{1,0:T(8,128)S(1)}, f32[128,128]{1,0:T(8,128)S(1)}, u32[]{:S(2)}, u32[]{:S(2)}) collective-permute-start(f32[128,128]{1,0:T(8,128)S(1)} %add.27.more), channel_id=1, source_target_pairs={{0,1},{1,0},{2,3},{3,2},{4,5},{5,4},{6,7},{7,6},{8,9},{9,8},{10,11... | collective-permute-start | bytes 196616 | tf_op jit(solution)/shard_map/ppermute | solution.py:210
  27.3 1.3 %collective-permute-start.9 = (f32[128,128]{1,0:T(8,128)S(1)}, f32[128,128]{1,0:T(8,128)S(1)}, u32[]{:S(2)}, u32[]{:S(2)}) collective-permute-start(f32[128,128]{1,0:T(8,128)S(1)} %slice.14), channel_id=1, source_target_pairs={{0,1},{1,0},{2,3},{3,2},{4,5},{5,4},{6,7},{7,6},{8,9},{9,8},{10,11... | collective-permute-start | bytes 196616 | tf_op jit(solution)/shard_map/ppermute | solution.py:210

commit v4 on v3

--- a/solution.py
+++ b/solution.py
@@ -155,53 +155,65 @@
     half_terms(width, new, (high, low, late_high, late_low), 1 - odd_chip(), 0, send)
 
 
-def keep_kernel(width, own, other, ratio, high, low, late_high, late_low, new_loadings, keep, cross, new, sem):
+def keep_kernel(width, own, other, ratio, high, low, late_high, late_low, new_loadings, keep, cross, stage, sem):
     rank = own.shape[0]
-    new[...] = ratio[...] * (own[...] + other[...])
-    copy = pltpu.make_async_copy(new, new_loadings, sem)
+    new = ratio[...] * (own[...] + other[...])
+    stage[...] = new
+    copy = pltpu.make_async_copy(stage, new_loadings, sem)
     copy.start()
-    half_terms(width, new[...], (high, low, late_high, late_low), odd_chip(), 0, keep)
-    square = dot(new[...], new[...], NT, HIGHEST)
+    square = dot(new, new, NT, HIGHEST)
     per_row = LANES // rank
     strip = rank // per_row
     cross[...] = jnp.concatenate([square[i * strip:(i + 1) * strip] for i in range(per_row)], axis=1)
+    half_terms(width, new, (high, low, late_high, late_low), odd_chip(), 0, keep)
     copy.wait()
 
 
-def half_basis(tied, scale, numers, turned, out):
+def piece_start(turned, first, count, blocks):
+    return pl.multiple_of((first + turned * (2 * blocks - 2 * first - count)) * LANES, LANES)
+
+
+def basis_piece(tied, scale, numers, turned, first, out):
     rank, cols = tied.shape
-    half = cols // 2
-    for block in range(half // LANES):
+    count = numers.shape[0] // rank
+    start = piece_start(turned, first, count, cols // 2 // LANES)
+    for block in range(count):
         numer = maybe_mirror(numers[block * rank:(block + 1) * rank], turned)
-        column = place(block, half // LANES, turned) * LANES
-        at = pl.ds(pl.multiple_of(turned * half + column, LANES), LANES)
-        out[:, pl.ds(pl.multiple_of(column, LANES), LANES)] = tied[:, at] * (0.5 * numer) / scale[:, at]
-
-
-def near_kernel(tied, sums, more, scale, near):
+        column = pl.multiple_of(place(block, count, turned) * LANES, LANES)
+        at = pl.ds(pl.multiple_of(start + column, LANES), LANES)
+        out[:, pl.ds(column, LANES)] = tied[:, at] * (0.5 * numer) / scale[:, at]
+
+
+def first_kernel(tied, sums, scale, near):
     rank = tied.shape[0]
     per_row = LANES // rank
     strip = rank // per_row
     packed = sums[:strip, :]
     cross = jnp.concatenate([packed[:, i * rank:(i + 1) * rank] for i in range(per_row)], axis=0)
     scale[...] = dot(cross, tied[...], NN, HIGHEST)
-    numers = jnp.concatenate([sums[strip:, :], more[...]], axis=0)
-    half_basis(tied, scale, numers, odd_chip(), near)
-
-
-def far_kernel(tied, scale, near, sums, more, new_basis, far, sems):
-    half = near.shape[1]
+    basis_piece(tied, scale, sums[strip:, :], odd_chip(), 0, near)
+
+
+def middle_kernel(first, tied, scale, sums, others, near, far):
     odd = odd_chip()
-    copies = [
-        pltpu.make_async_copy(
-            part, new_basis.at[:, pl.ds(pl.multiple_of(turned * half, LANES), half)], sems.at[i]
-        )
-        for i, (part, turned) in enumerate(((near, odd), (far, 1 - odd)))
-    ]
-    copies[0].start()
-    numers = jnp.concatenate([sums[...], more[...]], axis=0)
-    half_basis(tied, scale, numers, 1 - odd, far)
-    copies[1].start()
+    basis_piece(tied, scale, sums[...], odd, first, near)
+    basis_piece(tied, scale, others[...], 1 - odd, 0, far)
+
+
+def last_kernel(first, tied, scale, near, more, far, others, new_basis, rest, sems):
+    cols = tied.shape[1]
+    blocks = cols // 2 // LANES
+    odd = odd_chip()
+    copies = []
+    for i, (piece, turned, begin) in enumerate(
+        ((near, odd, 0), (more, odd, first), (far, 1 - odd, 0), (rest, 1 - odd, first))
+    ):
+        if piece is rest:
+            basis_piece(tied, scale, others[...], turned, first, rest)
+        width = piece.shape[1]
+        start = piece_start(turned, begin, width // LANES, blocks)
+        copies.append(pltpu.make_async_copy(piece, new_basis.at[:, pl.ds(start, width)], sems.at[i]))
+        copies[-1].start()
     for copy in copies:
         copy.wait()
 
@@ -215,15 +227,16 @@
     groups = [list(range(a, b)) for a, b in zip(cuts, cuts[1:])]
     return [
         [sum((groups[g] for g in order), []) for order in stream]
-        for stream in (((1, 0, 2), (0, 2, 1)), ((1, 2, 0), (2, 1, 0)))
+        for stream in (((1, 0, 2), (2, 1, 0)), ((1, 2, 0), (2, 0, 1)))
     ]
 
 
 def scan_sums(parts):
     count, steps = lax.axis_size("scan"), scan_steps()
     if count != 1 << steps:
-        return lax.psum(parts, "scan")
+        return [(total, jnp.zeros_like(total)) for total in lax.psum(parts, "scan")]
     orders = stride_orders(steps)
+    pairs = [(part, jnp.zeros_like(part)) for part in parts]
     for step in range(steps):
         received = []
         for part, order in zip(parts, orders):
@@ -233,8 +246,9 @@
                     half = (core + i.bit_count()) % 2
                     route.append((2 * i + core, 2 * (i ^ 1 << order[half][step]) + 1 - core))
             received.append(lax.ppermute(part, ("scan", "det"), route))
-        parts = [part + other for part, other in zip(parts, received)]
-    return parts
+        pairs = list(zip(parts, received))
+        parts = [part + other for part, other in pairs]
+    return pairs
 
 
 def per_device(spectra, basis, loadings):
@@ -268,29 +282,41 @@
     ratio, = call(ratio_kernel, "ratio", [(VMEM, tied), (VMEM, near_loadings)], [(VMEM, loadings.shape, F32)], flops=product // 16)
     operands = [(VMEM, x) for x in (numer, other, ratio, high, low, late_high, late_low)]
     send, = call(
-        functools.partial(send_kernel, 256), "send", operands, [(VMEM, (tall, LANES), F32)], flops=3 * product // 2
+        functools.partial(send_kernel, 512), "send", operands, [(VMEM, (tall, LANES), F32)], flops=3 * product // 2
     )
     received = over_det(send)
     new_loadings, keep, cross = call(
-        functools.partial(keep_kernel, 256), "keep", operands,
+        functools.partial(keep_kernel, 512), "keep", operands,
         [(HBM, loadings.shape, F32), (VMEM, (tall, LANES), F32), (VMEM, (strip, LANES), F32)],
         [VMEM(loadings.shape, F32), dma(())],
         flops=3 * product // 2,
     )
     folded = keep + received
-    cut = tall // 2
+    cut = tall // rank // 2 * rank
     parts = (jnp.concatenate([cross, folded[:cut]], axis=0), folded[cut:])
-    sums = scan_sums(lax.optimization_barrier(parts))
-    others = [over_det(sums[0][strip:]), over_det(sums[1])]
+    (mine, theirs), (my_rest, their_rest) = scan_sums(lax.optimization_barrier(parts))
+    sums = mine + theirs
+    others = over_det(sums[strip:])
     scale, near = call(
-        near_kernel, "near", [(VMEM, tied), (VMEM, sums[0]), (VMEM, sums[1])],
-        [(VMEM, basis.shape, F32), (VMEM, (rank, half), F32)],
+        first_kernel, "first", [(VMEM, tied), (VMEM, sums)],
+        [(VMEM, basis.shape, F32), (VMEM, (rank, cut // rank * LANES), F32)],
         flops=product // 32,
     )
+    scale, near, their_rest = lax.optimization_barrier((scale, near, their_rest))
+    rest = my_rest + their_rest
+    other_rest = over_det(rest)
+    wide = (rank, half - cut // rank * LANES)
+    more, far = call(
+        functools.partial(middle_kernel, cut // rank), "middle",
+        [(VMEM, x) for x in (tied, scale, rest, others)],
+        [(VMEM, wide, F32), (VMEM, near.shape, F32)],
+        flops=product // 64,
+    )
     new_basis, = call(
-        far_kernel, "far", [(VMEM, x) for x in (tied, scale, near, *others)],
+        functools.partial(last_kernel, cut // rank), "last",
+        [(VMEM, x) for x in (tied, scale, near, more, far, other_rest)],
         [(HBM, basis.shape, F32)],
-        [VMEM((rank, half), F32), dma((2,))],
+        [VMEM(wide, F32), dma((4,))],
     )
     return new_loadings, new_basis
 

time: 29.5 us -> 28.7 us (0.973)
  starting transfers between devices: 13.4 us -> 12.7 us
    ppermute x6, starting transfers between devices: 11.9 us -> 11.2 us  [scan_sums(): received.append(lax.ppermute(part, ('scan', 'det'), route))]
    ppermute x6, waiting for transfers between devices: 4.31 us -> 3.83 us  [scan_sums(): received.append(lax.ppermute(part, ('scan', 'det'), route))]
    ppermute x5, waiting for transfers between devices: 1 us -> 1.46 us  [over_det(): return lax.ppermute(x, 'det', [(0, 1), (1, 0)])]
    pallas_call x7 -> x8, Pallas kernels: 9.88 us -> 9.75 us  [call(): pl.pallas_call(kernel, out_shape=[memory(shape, dtype) for memory, shape,...]
  transfers between devices with their start and end apart: 11 -> 11, of which waited for: 6 -> 7; matrix products, arithmetic and copies ran while one was open for 0% -> 0% of each run, Pallas kernels for 17% -> 17%
where the time goes in v4:
time: 28.7 us; the launch traced here: 28.6 us
  starting transfers between devices  12.7 us (44%)
  Pallas kernels  9.75 us (34%)
  waiting for transfers between devices  5.29 us (18%)
  between operations  0.75 us (3%)
    ppermute x6, starting transfers between devices, scan_sums(): received.append(lax.ppermute(part, ('scan', 'det'), route))  11.2 us
    pallas_call x8, Pallas kernels, call(): pl.pallas_call(kernel, out_shape=[memory(shape, dtype) for memory, shape,...  9.75 us
    ppermute x6, waiting for transfers between devices, scan_sums(): received.append(lax.ppermute(part, ('scan', 'det'), route))  3.83 us
    ppermute x5, starting transfers between devices, over_det(): return lax.ppermute(x, 'det', [(0, 1), (1, 0)])  1.51 us
    ppermute x5, waiting for transfers between devices, over_det(): return lax.ppermute(x, 'det', [(0, 1), (1, 0)])  1.46 us
  transfers between devices with their start and end apart: 11, of which 7 were waited for; matrix products, arithmetic and copies ran while one was open for 0% of the time, Pallas kernels for 17%

profile of v4, /device:TPU:0, one launch (start us, length us, event | category | flops | bytes accessed | tf_op | source)
XLA Modules:
  0.0 28.6 jit_solution(13503836845763943442)
XLA Ops:
  0.6 0.5 %collective-permute-start = (f32[32,2048]{1,0:T(8,128)}, f32[32,2048]{1,0:T(8,128)S(1)}, u32[]{:S(2)}, u32[]{:S(2)}) collective-permute-start(f32[32,2048]{1,0:T(8,128)} %basis.1), channel_id=1, source_target_pairs={{0,1},{1,0},{2,3},{3,2},{4,5},{5,4},{6,7},{7,6},{8,9},{9,8},{10,11... | collective-permute-start | bytes 786440 | tf_op jit(solution)/shard_map/ppermute | solution.py:222
  1.1 2.4 %load.1 = (f32[32,2048]{1,0:T(8,128)S(1)}, f32[32,1024]{1,0:T(8,128)S(1)}, bf16[512,2048]{1,0:T(8,128)(2,1)S(1)}, bf16[512,2048]{1,0:T(8,128)(2,1)S(1)}) custom-call(f32[1024,2048]{1,0:T(8,128)} %spectra.3, f32[32,2048]{1,0:T(8,128)} %basis.1, f32[32,1024]{1,0:T(8,128)} %loadings.1), custom_call_target="tpu_custom_call" | custom-call | bytes 4194304 | tf_op jit(solution)/shard_map/load/pallas_call | solution.py:21
  3.6 0.0 collective-permute-done.partner
  3.6 3.3 %numer.1 = (f32[32,1024]{1,0:T(8,128)S(1)}, f32[32,2048]{1,0:T(8,128)S(1)}, bf16[512,2048]{1,0:T(8,128)(2,1)S(1)}, bf16[512,2048]{1,0:T(8,128)(2,1)S(1)}) custom-call(f32[1024,2048]{1,0:T(8,128)} %spectra.3, f32[32,2048]{1,0:T(8,128)S(1)} %get-tuple-element.22.basis, f32[32,2048]{1,0:T(8,128)S(1)} %collective-permute-done.partner, ...), custom_call_target="tpu_custom_call" | custom-call | flops 402653184 | bytes 4194304 | tf_op jit(solution)/shard_map/numer/pallas_call | solution.py:21
  6.9 0.1 collective-permute-start.1
  7.0 0.7 %ratio.1 = f32[32,1024]{1,0:T(8,128)S(1)} custom-call(f32[32,2048]{1,0:T(8,128)S(1)} %get-tuple-element.26.tied, f32[32,1024]{1,0:T(8,128)S(1)} %get-tuple-element.27.loadings), custom_call_target="tpu_custom_call" | custom-call | flops 8388608 | tf_op jit(solution)/shard_map/ratio/pallas_call | solution.py:21
  7.8 0.5 %collective-permute-done.1.other = f32[32,1024]{1,0:T(8,128)S(1)} collective-permute-done((f32[32,1024]{1,0:T(8,128)S(1)}, f32[32,1024]{1,0:T(8,128)S(1)}, u32[]{:S(2)}, u32[]{:S(2)}) %collective-permute-start.1) | collective-permute-done | bytes 131104 | tf_op jit(solution)/shard_map/ppermute | solution.py:222
  8.3 0.9 %send.1 = f32[256,128]{1,0:T(8,128)S(1)} custom-call(f32[32,1024]{1,0:T(8,128)S(1)} %get-tuple-element.25.own, f32[32,1024]{1,0:T(8,128)S(1)} %collective-permute-done.1.other, f32[32,1024]{1,0:T(8,128)S(1)} %ratio.1, bf16[512,2048]{1,0:T(8,128)(2,1)S(1)} %get-tuple-element.23.high, bf16[512,2048]{1,0:T(8,128)(2,1)S(1)} %get-tuple-element.24.low, ...), custom_call_target="tpu_custom_call" | custom-call | flops 201326592 | tf_op jit(solution)/shard_map/send/pallas_call | solution.py:21
  9.2 0.2 collective-permute-start.2
  9.4 1.0 %keep.1 = (f32[32,1024]{1,0:T(8,128)}, f32[256,128]{1,0:T(8,128)S(1)}, f32[8,128]{1,0:T(8,128)S(1)}) custom-call(f32[32,1024]{1,0:T(8,128)S(1)} %get-tuple-element.25.own, f32[32,1024]{1,0:T(8,128)S(1)} %collective-permute-done.1.other, f32[32,1024]{1,0:T(8,128)S(1)} %ratio.1, bf16[512,2048]{1,0:T(8,128)(2,1)S(1)} %get-tuple-element.23.high, ...), custom_call_target="tpu_custom_call" | custom-call | flops 201326592 | tf_op jit(solution)/shard_map/keep/pallas_call | solution.py:21
  10.5 0.2 collective-permute-done.2
  10.7 2.7 %collective-permute-start.3 = (f32[136,128]{1,0:T(8,128)S(1)}, f32[136,128]{1,0:T(8,128)S(1)}, u32[]{:S(2)}, u32[]{:S(2)}) collective-permute-start(f32[136,128]{1,0:T(8,128)S(1)} %pad_maximum_fusion), channel_id=1, source_target_pairs={{0,5},{1,8},{2,11},{3,6},{4,13},{5,0},{6,3},{7,14},{8,1},{9,12},{1... | collective-permute-start | bytes 208904 | tf_op jit(solution)/shard_map/ppermute | solution.py:248
  13.4 0.1 collective-permute-start.6
  13.5 2.0 %collective-permute-done.3 = f32[136,128]{1,0:T(8,128)S(1)} collective-permute-done((f32[136,128]{1,0:T(8,128)S(1)}, f32[136,128]{1,0:T(8,128)S(1)}, u32[]{:S(2)}, u32[]{:S(2)}) %collective-permute-start.3) | collective-permute-done | bytes 69664 | tf_op jit(solution)/shard_map/ppermute | solution.py:248
  15.5 2.4 %collective-permute-start.4 = (f32[136,128]{1,0:T(8,128)S(1)}, f32[136,128]{1,0:T(8,128)S(1)}, u32[]{:S(2)}, u32[]{:S(2)}) collective-permute-start(f32[136,128]{1,0:T(8,128)S(1)} %add.22), channel_id=1, source_target_pairs={{0,3},{1,4},{2,7},{3,0},{4,1},{5,6},{6,5},{7,2},{8,13},{9,10},{10,... | collective-permute-start | bytes 208904 | tf_op jit(solution)/shard_map/ppermute | solution.py:248
  17.9 0.0 collective-permute-done.6
  18.0 2.3 %collective-permute-start.7 = (f32[128,128]{1,0:T(8,128)S(1)}, f32[128,128]{1,0:T(8,128)S(1)}, u32[]{:S(2)}, u32[]{:S(2)}) collective-permute-start(f32[128,128]{1,0:T(8,128)S(1)} %add.25), channel_id=1, source_target_pairs={{0,9},{1,2},{2,1},{3,10},{4,7},{5,12},{6,15},{7,4},{8,11},{9,0},{1... | collective-permute-start | bytes 196616 | tf_op jit(solution)/shard_map/ppermute | solution.py:248
  20.2 0.0 collective-permute-done.4
  20.2 2.3 %collective-permute-start.5 = (f32[136,128]{1,0:T(8,128)S(1)}, f32[136,128]{1,0:T(8,128)S(1)}, u32[]{:S(2)}, u32[]{:S(2)}) collective-permute-start(f32[136,128]{1,0:T(8,128)S(1)} %add.23), channel_id=1, source_target_pairs={{0,9},{1,2},{2,1},{3,10},{4,7},{5,12},{6,15},{7,4},{8,11},{9,0},{1... | collective-permute-start | bytes 208904 | tf_op jit(solution)/shard_map/ppermute | solution.py:248
  22.6 0.1 collective-permute-done.7
  22.6 1.4 %collective-permute-start.8 = (f32[128,128]{1,0:T(8,128)S(1)}, f32[128,128]{1,0:T(8,128)S(1)}, u32[]{:S(2)}, u32[]{:S(2)}) collective-permute-start(f32[128,128]{1,0:T(8,128)S(1)} %add.26), channel_id=1, source_target_pairs={{0,3},{1,4},{2,7},{3,0},{4,1},{5,6},{6,5},{7,2},{8,13},{9,10},{10,... | collective-permute-start | bytes 196616 | tf_op jit(solution)/shard_map/ppermute | solution.py:248
  24.0 0.9 %collective-permute-done.5 = f32[136,128]{1,0:T(8,128)S(1)} collective-permute-done((f32[136,128]{1,0:T(8,128)S(1)}, f32[136,128]{1,0:T(8,128)S(1)}, u32[]{:S(2)}, u32[]{:S(2)}) %collective-permute-start.5) | collective-permute-done | bytes 69664 | tf_op jit(solution)/shard_map/ppermute | solution.py:248
  25.0 0.2 collective-permute-start.9
  25.1 0.4 %first.1 = (f32[32,2048]{1,0:T(8,128)S(1)}, f32[32,512]{1,0:T(8,128)S(1)}) custom-call(f32[32,2048]{1,0:T(8,128)S(1)} %get-tuple-element.26.tied, f32[136,128]{1,0:T(8,128)S(1)} %add.24.sums), custom_call_target="tpu_custom_call" | custom-call | flops 4194304 | tf_op jit(solution)/shard_map/first/pallas_call | solution.py:21
  25.6 0.8 %collective-permute-done.8 = f32[128,128]{1,0:T(8,128)S(1)} collective-permute-done((f32[128,128]{1,0:T(8,128)S(1)}, f32[128,128]{1,0:T(8,128)S(1)}, u32[]{:S(2)}, u32[]{:S(2)}) %collective-permute-start.8) | collective-permute-done | bytes 65568 | tf_op jit(solution)/shard_map/ppermute | solution.py:248
  26.4 0.5 %collective-permute-start.10 = (f32[128,128]{1,0:T(8,128)S(1)}, f32[128,128]{1,0:T(8,128)S(1)}, u32[]{:S(2)}, u32[]{:S(2)}) collective-permute-start(f32[128,128]{1,0:T(8,128)S(1)} %add.27.sums), channel_id=1, source_target_pairs={{0,1},{1,0},{2,3},{3,2},{4,5},{5,4},{6,7},{7,6},{8,9},{9,8},{10,11... | collective-permute-start | bytes 196616 | tf_op jit(solution)/shard_map/ppermute | solution.py:222
  26.9 0.0 collective-permute-done.9.others
  26.9 0.1 middle.1
  27.0 0.8 %collective-permute-done.10.others = f32[128,128]{1,0:T(8,128)S(1)} collective-permute-done((f32[128,128]{1,0:T(8,128)S(1)}, f32[128,128]{1,0:T(8,128)S(1)}, u32[]{:S(2)}, u32[]{:S(2)}) %collective-permute-start.10) | collective-permute-done | bytes 65568 | tf_op jit(solution)/shard_map/ppermute | solution.py:222
  27.8 0.8 %last.1 = f32[32,2048]{1,0:T(8,128)} custom-call(f32[32,2048]{1,0:T(8,128)S(1)} %get-tuple-element.26.tied, f32[32,2048]{1,0:T(8,128)S(1)} %get-tuple-element.37.scale, f32[32,512]{1,0:T(8,128)S(1)} %get-tuple-element.38.near, f32[32,512]{1,0:T(8,128)S(1)} %get-tuple-element.40.more, f32[32,512]{1,0:T(8,128)S(1)} %get-tuple-element.41.far, ...), custom_call_target="tpu_custom_call" | custom-call | tf_op jit(solution)/shard_map/last/pallas_call | solution.py:21
  (10 shorter events, 0.1 us)
Async XLA Ops:
  0.6 3.0 %collective-permute-start = (f32[32,2048]{1,0:T(8,128)}, f32[32,2048]{1,0:T(8,128)S(1)}, u32[]{:S(2)}, u32[]{:S(2)}) collective-permute-start(f32[32,2048]{1,0:T(8,128)} %basis.1), channel_id=1, source_target_pairs={{0,1},{1,0},{2,3},{3,2},{4,5},{5,4},{6,7},{7,6},{8,9},{9,8},{10,11... | collective-permute-start | bytes 786440 | tf_op jit(solution)/shard_map/ppermute | solution.py:222
  6.9 1.4 %collective-permute-start.1 = (f32[32,1024]{1,0:T(8,128)S(1)}, f32[32,1024]{1,0:T(8,128)S(1)}, u32[]{:S(2)}, u32[]{:S(2)}) collective-permute-start(f32[32,1024]{1,0:T(8,128)S(1)} %get-tuple-element.25.own), channel_id=1, source_target_pairs={{0,1},{1,0},{2,3},{3,2},{4,5},{5,4},{6,7},{7,6},{8,9},{9,8},{10,11... | collective-permute-start | bytes 393224 | tf_op jit(solution)/shard_map/ppermute | solution.py:222
  9.2 1.4 %collective-permute-start.2 = (f32[256,128]{1,0:T(8,128)S(1)}, f32[256,128]{1,0:T(8,128)S(1)}, u32[]{:S(2)}, u32[]{:S(2)}) collective-permute-start(f32[256,128]{1,0:T(8,128)S(1)} %send.1), channel_id=1, source_target_pairs={{0,1},{1,0},{2,3},{3,2},{4,5},{5,4},{6,7},{7,6},{8,9},{9,8},{10,11... | collective-permute-start | bytes 393224 | tf_op jit(solution)/shard_map/ppermute | solution.py:222
  10.7 4.8 %collective-permute-start.3 = (f32[136,128]{1,0:T(8,128)S(1)}, f32[136,128]{1,0:T(8,128)S(1)}, u32[]{:S(2)}, u32[]{:S(2)}) collective-permute-start(f32[136,128]{1,0:T(8,128)S(1)} %pad_maximum_fusion), channel_id=1, source_target_pairs={{0,5},{1,8},{2,11},{3,6},{4,13},{5,0},{6,3},{7,14},{8,1},{9,12},{1... | collective-permute-start | bytes 208904 | tf_op jit(solution)/shard_map/ppermute | solution.py:248
  13.4 4.5 %collective-permute-start.6 = (f32[128,128]{1,0:T(8,128)S(1)}, f32[128,128]{1,0:T(8,128)S(1)}, u32[]{:S(2)}, u32[]{:S(2)}) collective-permute-start(f32[128,128]{1,0:T(8,128)S(1)} %get-tuple-element.36), channel_id=1, source_target_pairs={{0,5},{1,8},{2,11},{3,6},{4,13},{5,0},{6,3},{7,14},{8,1},{9,12},{1... | collective-permute-start | bytes 196616 | tf_op jit(solution)/shard_map/ppermute | solution.py:248
  15.5 4.7 %collective-permute-start.4 = (f32[136,128]{1,0:T(8,128)S(1)}, f32[136,128]{1,0:T(8,128)S(1)}, u32[]{:S(2)}, u32[]{:S(2)}) collective-permute-start(f32[136,128]{1,0:T(8,128)S(1)} %add.22), channel_id=1, source_target_pairs={{0,3},{1,4},{2,7},{3,0},{4,1},{5,6},{6,5},{7,2},{8,13},{9,10},{10,... | collective-permute-start | bytes 208904 | tf_op jit(solution)/shard_map/ppermute | solution.py:248
  18.0 4.7 %collective-permute-start.7 = (f32[128,128]{1,0:T(8,128)S(1)}, f32[128,128]{1,0:T(8,128)S(1)}, u32[]{:S(2)}, u32[]{:S(2)}) collective-permute-start(f32[128,128]{1,0:T(8,128)S(1)} %add.25), channel_id=1, source_target_pairs={{0,9},{1,2},{2,1},{3,10},{4,7},{5,12},{6,15},{7,4},{8,11},{9,0},{1... | collective-permute-start | bytes 196616 | tf_op jit(solution)/shard_map/ppermute | solution.py:248
  20.2 4.7 %collective-permute-start.5 = (f32[136,128]{1,0:T(8,128)S(1)}, f32[136,128]{1,0:T(8,128)S(1)}, u32[]{:S(2)}, u32[]{:S(2)}) collective-permute-start(f32[136,128]{1,0:T(8,128)S(1)} %add.23), channel_id=1, source_target_pairs={{0,9},{1,2},{2,1},{3,10},{4,7},{5,12},{6,15},{7,4},{8,11},{9,0},{1... | collective-permute-start | bytes 208904 | tf_op jit(solution)/shard_map/ppermute | solution.py:248
  22.6 3.8 %collective-permute-start.8 = (f32[128,128]{1,0:T(8,128)S(1)}, f32[128,128]{1,0:T(8,128)S(1)}, u32[]{:S(2)}, u32[]{:S(2)}) collective-permute-start(f32[128,128]{1,0:T(8,128)S(1)} %add.26), channel_id=1, source_target_pairs={{0,3},{1,4},{2,7},{3,0},{4,1},{5,6},{6,5},{7,2},{8,13},{9,10},{10,... | collective-permute-start | bytes 196616 | tf_op jit(solution)/shard_map/ppermute | solution.py:248
  25.0 1.9 %collective-permute-start.9 = (f32[128,128]{1,0:T(8,128)S(1)}, f32[128,128]{1,0:T(8,128)S(1)}, u32[]{:S(2)}, u32[]{:S(2)}) collective-permute-start(f32[128,128]{1,0:T(8,128)S(1)} %slice.14), channel_id=1, source_target_pairs={{0,1},{1,0},{2,3},{3,2},{4,5},{5,4},{6,7},{7,6},{8,9},{9,8},{10,11... | collective-permute-start | bytes 196616 | tf_op jit(solution)/shard_map/ppermute | solution.py:222
  26.4 1.4 %collective-permute-start.10 = (f32[128,128]{1,0:T(8,128)S(1)}, f32[128,128]{1,0:T(8,128)S(1)}, u32[]{:S(2)}, u32[]{:S(2)}) collective-permute-start(f32[128,128]{1,0:T(8,128)S(1)} %add.27.sums), channel_id=1, source_target_pairs={{0,1},{1,0},{2,3},{3,2},{4,5},{5,4},{6,7},{7,6},{8,9},{9,8},{10,11... | collective-permute-start | bytes 196616 | tf_op jit(solution)/shard_map/ppermute | solution.py:222

commit v5 on v4

--- a/solution.py
+++ b/solution.py
@@ -48,36 +48,35 @@
     return lax.dot_general(a, b, dims, precision=precision, preferred_element_type=F32)
 
 
-def row_copies(spectra, stage, sems, first, rows):
-    return [
-        pltpu.make_async_copy(
-            spectra.at[pl.ds(first + i * rows, rows)], stage.at[pl.ds(i * rows, rows)], sems.at[i]
-        )
-        for i in range(stage.shape[0] // rows)
-    ]
-
-
-def load_kernel(rows, spectra, basis, loadings, near_basis, near_loadings, high, low, stage, sems, side_sems):
-    copies = row_copies(spectra, stage, sems, 0, rows)
+def row_copies(spectra, stage, sems, first, sizes):
+    copies, start = [], 0
+    for i, rows in enumerate(sizes):
+        at = pl.ds(start, rows)
+        copies.append((at, pltpu.make_async_copy(spectra.at[pl.ds(first + start, rows)], stage.at[at], sems.at[i])))
+        start += rows
+    return copies
+
+
+def load_kernel(sizes, spectra, basis, loadings, near_basis, near_loadings, high, low, stage, sems, side_sems):
+    copies = row_copies(spectra, stage, sems, 0, sizes)
     sides = [
         pltpu.make_async_copy(basis, near_basis, side_sems.at[0]),
         pltpu.make_async_copy(loadings, near_loadings, side_sems.at[1]),
     ]
-    for copy in copies + sides:
+    for copy in [copy for _, copy in copies] + sides:
         copy.start()
-    for i, copy in enumerate(copies):
-        at = pl.ds(i * rows, rows)
+    for at, copy in copies:
         copy.wait()
         high[at, :], low[at, :] = halves(stage[at, :])
     for copy in sides:
         copy.wait()
 
 
-def numer_kernel(rows, spectra, basis, partner, high, low, numer, tied, late_high, late_low, stage, sems):
+def numer_kernel(group, sizes, spectra, basis, partner, high, low, numer, tied, late_high, late_low, stage, sems):
     rank, cols = basis.shape
     early = high.shape[0]
-    copies = row_copies(spectra, stage, sems, early, rows)
-    for copy in copies:
+    copies = row_copies(spectra, stage, sems, early, sizes)
+    for _, copy in copies:
         copy.start()
     blocks = cols // LANES
     for j in range(blocks):
@@ -91,16 +90,13 @@
         terms = terms[:, :rank] + terms[:, rank:] + dot(block_low, tied_parts[:rank], NT)
         numer[:, pl.ds(start, block_high.shape[0])] = terms.T
 
-    for start in range(0, early, rows):
-        at = pl.ds(start, rows)
+    for start in range(0, early, group):
+        at = pl.ds(start, min(group, early - start))
         put(start, high[at, :], low[at, :])
-    for i, copy in enumerate(copies):
-        at = pl.ds(i * rows, rows)
+    for whole, copy in copies:
         copy.wait()
-        block_high, block_low = halves(stage[at, :])
-        late_high[at, :] = block_high
-        late_low[at, :] = block_low
-        put(early + i * rows, block_high, block_low)
+        late_high[whole, :], late_low[whole, :] = halves(stage[whole, :])
+        put(early + whole.start, late_high[whole, :], late_low[whole, :])
 
 
 def ratio_kernel(tied, loadings, ratio):
@@ -255,9 +251,10 @@
     positions, cols = spectra.shape
     rank = basis.shape[0]
     half = cols // 2
-    rows = 128
     early = positions // 2
     late = positions - early
+    early_sizes = (early // 2, early // 4, early // 8, early // 8)
+    late_sizes = (late // 2, late // 2)
     tall = half // LANES * rank
     strip = rank * rank // LANES
     product = 2 * rank * positions * cols
@@ -265,17 +262,17 @@
 
     partner = over_det(basis)
     near_basis, near_loadings, high, low = call(
-        functools.partial(load_kernel, rows), "load",
+        functools.partial(load_kernel, early_sizes), "load",
         [(HBM, spectra), (HBM, basis), (HBM, loadings)],
         [(VMEM, basis.shape, F32), (VMEM, loadings.shape, F32), (VMEM, (early, cols), BF16), (VMEM, (early, cols), BF16)],
-        [VMEM((early, cols), F32), dma((early // rows,)), dma((2,))],
+        [VMEM((early, cols), F32), dma((len(early_sizes),)), dma((2,))],
         moved=4 * early * cols,
     )
     numer, tied, late_high, late_low = call(
-        functools.partial(numer_kernel, 2 * rows), "numer",
+        functools.partial(numer_kernel, 128, late_sizes), "numer",
         [(HBM, spectra), (VMEM, near_basis), (VMEM, partner), (VMEM, high), (VMEM, low)],
         [(VMEM, loadings.shape, F32), (VMEM, basis.shape, F32), (VMEM, (late, cols), BF16), (VMEM, (late, cols), BF16)],
-        [VMEM((late, cols), F32), dma((late // (2 * rows),))],
+        [VMEM((late, cols), F32), dma((len(late_sizes),))],
         flops=3 * product, moved=4 * late * cols,
     )
     other = over_det(numer)

time: 28.7 us -> 28.6 us (level)
  no operation moved by 1% of the time
where the time goes in v5:
time: 28.6 us; the launch traced here: 28.5 us
  starting transfers between devices  12.7 us (44%)
  Pallas kernels  9.67 us (34%)
  waiting for transfers between devices  5.28 us (18%)
  between operations  0.75 us (3%)
    ppermute x6, starting transfers between devices, scan_sums(): received.append(lax.ppermute(part, ('scan', 'det'), route))  11.2 us
    pallas_call x8, Pallas kernels, call(): pl.pallas_call(kernel, out_shape=[memory(shape, dtype) for memory, shape,...  9.67 us
    ppermute x6, waiting for transfers between devices, scan_sums(): received.append(lax.ppermute(part, ('scan', 'det'), route))  3.83 us
    ppermute x5, starting transfers between devices, over_det(): return lax.ppermute(x, 'det', [(0, 1), (1, 0)])  1.51 us
    ppermute x5, waiting for transfers between devices, over_det(): return lax.ppermute(x, 'det', [(0, 1), (1, 0)])  1.45 us
  transfers between devices with their start and end apart: 11, of which 7 were waited for; matrix products, arithmetic and copies ran while one was open for 0% of the time, Pallas kernels for 17%

profile of v5, /device:TPU:0, one launch (start us, length us, event | category | flops | bytes accessed | tf_op | source)
XLA Modules:
  0.0 28.5 jit_solution(15785611397515151745)
XLA Ops:
  0.6 0.5 %collective-permute-start = (f32[32,2048]{1,0:T(8,128)}, f32[32,2048]{1,0:T(8,128)S(1)}, u32[]{:S(2)}, u32[]{:S(2)}) collective-permute-start(f32[32,2048]{1,0:T(8,128)} %basis.1), channel_id=1, source_target_pairs={{0,1},{1,0},{2,3},{3,2},{4,5},{5,4},{6,7},{7,6},{8,9},{9,8},{10,11... | collective-permute-start | bytes 786440 | tf_op jit(solution)/shard_map/ppermute | solution.py:218
  1.1 2.4 %load.1 = (f32[32,2048]{1,0:T(8,128)S(1)}, f32[32,1024]{1,0:T(8,128)S(1)}, bf16[512,2048]{1,0:T(8,128)(2,1)S(1)}, bf16[512,2048]{1,0:T(8,128)(2,1)S(1)}) custom-call(f32[1024,2048]{1,0:T(8,128)} %spectra.3, f32[32,2048]{1,0:T(8,128)} %basis.1, f32[32,1024]{1,0:T(8,128)} %loadings.1), custom_call_target="tpu_custom_call" | custom-call | bytes 4194304 | tf_op jit(solution)/shard_map/load/pallas_call | solution.py:21
  3.5 0.0 collective-permute-done.partner
  3.5 3.3 %numer.1 = (f32[32,1024]{1,0:T(8,128)S(1)}, f32[32,2048]{1,0:T(8,128)S(1)}, bf16[512,2048]{1,0:T(8,128)(2,1)S(1)}, bf16[512,2048]{1,0:T(8,128)(2,1)S(1)}) custom-call(f32[1024,2048]{1,0:T(8,128)} %spectra.3, f32[32,2048]{1,0:T(8,128)S(1)} %get-tuple-element.22.basis, f32[32,2048]{1,0:T(8,128)S(1)} %collective-permute-done.partner, ...), custom_call_target="tpu_custom_call" | custom-call | flops 402653184 | bytes 4194304 | tf_op jit(solution)/shard_map/numer/pallas_call | solution.py:21
  6.8 0.1 collective-permute-start.1
  6.9 0.8 %ratio.1 = f32[32,1024]{1,0:T(8,128)S(1)} custom-call(f32[32,2048]{1,0:T(8,128)S(1)} %get-tuple-element.26.tied, f32[32,1024]{1,0:T(8,128)S(1)} %get-tuple-element.27.loadings), custom_call_target="tpu_custom_call" | custom-call | flops 8388608 | tf_op jit(solution)/shard_map/ratio/pallas_call | solution.py:21
  7.7 0.5 %collective-permute-done.1.other = f32[32,1024]{1,0:T(8,128)S(1)} collective-permute-done((f32[32,1024]{1,0:T(8,128)S(1)}, f32[32,1024]{1,0:T(8,128)S(1)}, u32[]{:S(2)}, u32[]{:S(2)}) %collective-permute-start.1) | collective-permute-done | bytes 131104 | tf_op jit(solution)/shard_map/ppermute | solution.py:218
  8.2 0.9 %send.1 = f32[256,128]{1,0:T(8,128)S(1)} custom-call(f32[32,1024]{1,0:T(8,128)S(1)} %get-tuple-element.25.own, f32[32,1024]{1,0:T(8,128)S(1)} %collective-permute-done.1.other, f32[32,1024]{1,0:T(8,128)S(1)} %ratio.1, bf16[512,2048]{1,0:T(8,128)(2,1)S(1)} %get-tuple-element.23.high, bf16[512,2048]{1,0:T(8,128)(2,1)S(1)} %get-tuple-element.24.low, ...), custom_call_target="tpu_custom_call" | custom-call | flops 201326592 | tf_op jit(solution)/shard_map/send/pallas_call | solution.py:21
  9.2 0.2 collective-permute-start.2
  9.4 1.0 %keep.1 = (f32[32,1024]{1,0:T(8,128)}, f32[256,128]{1,0:T(8,128)S(1)}, f32[8,128]{1,0:T(8,128)S(1)}) custom-call(f32[32,1024]{1,0:T(8,128)S(1)} %get-tuple-element.25.own, f32[32,1024]{1,0:T(8,128)S(1)} %collective-permute-done.1.other, f32[32,1024]{1,0:T(8,128)S(1)} %ratio.1, bf16[512,2048]{1,0:T(8,128)(2,1)S(1)} %get-tuple-element.23.high, ...), custom_call_target="tpu_custom_call" | custom-call | flops 201326592 | tf_op jit(solution)/shard_map/keep/pallas_call | solution.py:21
  10.4 0.2 collective-permute-done.2
  10.6 2.7 %collective-permute-start.3 = (f32[136,128]{1,0:T(8,128)S(1)}, f32[136,128]{1,0:T(8,128)S(1)}, u32[]{:S(2)}, u32[]{:S(2)}) collective-permute-start(f32[136,128]{1,0:T(8,128)S(1)} %pad_maximum_fusion), channel_id=1, source_target_pairs={{0,5},{1,8},{2,11},{3,6},{4,13},{5,0},{6,3},{7,14},{8,1},{9,12},{1... | collective-permute-start | bytes 208904 | tf_op jit(solution)/shard_map/ppermute | solution.py:244
  13.4 0.1 collective-permute-start.6
  13.4 2.0 %collective-permute-done.3 = f32[136,128]{1,0:T(8,128)S(1)} collective-permute-done((f32[136,128]{1,0:T(8,128)S(1)}, f32[136,128]{1,0:T(8,128)S(1)}, u32[]{:S(2)}, u32[]{:S(2)}) %collective-permute-start.3) | collective-permute-done | bytes 69664 | tf_op jit(solution)/shard_map/ppermute | solution.py:244
  15.5 2.4 %collective-permute-start.4 = (f32[136,128]{1,0:T(8,128)S(1)}, f32[136,128]{1,0:T(8,128)S(1)}, u32[]{:S(2)}, u32[]{:S(2)}) collective-permute-start(f32[136,128]{1,0:T(8,128)S(1)} %add.22), channel_id=1, source_target_pairs={{0,3},{1,4},{2,7},{3,0},{4,1},{5,6},{6,5},{7,2},{8,13},{9,10},{10,... | collective-permute-start | bytes 208904 | tf_op jit(solution)/shard_map/ppermute | solution.py:244
  17.9 0.0 collective-permute-done.6
  17.9 2.2 %collective-permute-start.7 = (f32[128,128]{1,0:T(8,128)S(1)}, f32[128,128]{1,0:T(8,128)S(1)}, u32[]{:S(2)}, u32[]{:S(2)}) collective-permute-start(f32[128,128]{1,0:T(8,128)S(1)} %add.25), channel_id=1, source_target_pairs={{0,9},{1,2},{2,1},{3,10},{4,7},{5,12},{6,15},{7,4},{8,11},{9,0},{1... | collective-permute-start | bytes 196616 | tf_op jit(solution)/shard_map/ppermute | solution.py:244
  20.1 0.0 collective-permute-done.4
  20.1 2.3 %collective-permute-start.5 = (f32[136,128]{1,0:T(8,128)S(1)}, f32[136,128]{1,0:T(8,128)S(1)}, u32[]{:S(2)}, u32[]{:S(2)}) collective-permute-start(f32[136,128]{1,0:T(8,128)S(1)} %add.23), channel_id=1, source_target_pairs={{0,9},{1,2},{2,1},{3,10},{4,7},{5,12},{6,15},{7,4},{8,11},{9,0},{1... | collective-permute-start | bytes 208904 | tf_op jit(solution)/shard_map/ppermute | solution.py:244
  22.5 0.1 collective-permute-done.7
  22.6 1.4 %collective-permute-start.8 = (f32[128,128]{1,0:T(8,128)S(1)}, f32[128,128]{1,0:T(8,128)S(1)}, u32[]{:S(2)}, u32[]{:S(2)}) collective-permute-start(f32[128,128]{1,0:T(8,128)S(1)} %add.26), channel_id=1, source_target_pairs={{0,3},{1,4},{2,7},{3,0},{4,1},{5,6},{6,5},{7,2},{8,13},{9,10},{10,... | collective-permute-start | bytes 196616 | tf_op jit(solution)/shard_map/ppermute | solution.py:244
  23.9 0.9 %collective-permute-done.5 = f32[136,128]{1,0:T(8,128)S(1)} collective-permute-done((f32[136,128]{1,0:T(8,128)S(1)}, f32[136,128]{1,0:T(8,128)S(1)}, u32[]{:S(2)}, u32[]{:S(2)}) %collective-permute-start.5) | collective-permute-done | bytes 69664 | tf_op jit(solution)/shard_map/ppermute | solution.py:244
  24.9 0.2 collective-permute-start.9
  25.0 0.4 %first.1 = (f32[32,2048]{1,0:T(8,128)S(1)}, f32[32,512]{1,0:T(8,128)S(1)}) custom-call(f32[32,2048]{1,0:T(8,128)S(1)} %get-tuple-element.26.tied, f32[136,128]{1,0:T(8,128)S(1)} %add.24.sums), custom_call_target="tpu_custom_call" | custom-call | flops 4194304 | tf_op jit(solution)/shard_map/first/pallas_call | solution.py:21
  25.5 0.8 %collective-permute-done.8 = f32[128,128]{1,0:T(8,128)S(1)} collective-permute-done((f32[128,128]{1,0:T(8,128)S(1)}, f32[128,128]{1,0:T(8,128)S(1)}, u32[]{:S(2)}, u32[]{:S(2)}) %collective-permute-start.8) | collective-permute-done | bytes 65568 | tf_op jit(solution)/shard_map/ppermute | solution.py:244
  26.3 0.5 %collective-permute-start.10 = (f32[128,128]{1,0:T(8,128)S(1)}, f32[128,128]{1,0:T(8,128)S(1)}, u32[]{:S(2)}, u32[]{:S(2)}) collective-permute-start(f32[128,128]{1,0:T(8,128)S(1)} %add.27.sums), channel_id=1, source_target_pairs={{0,1},{1,0},{2,3},{3,2},{4,5},{5,4},{6,7},{7,6},{8,9},{9,8},{10,11... | collective-permute-start | bytes 196616 | tf_op jit(solution)/shard_map/ppermute | solution.py:218
  26.8 0.0 collective-permute-done.9.others
  26.8 0.1 middle.1
  27.0 0.8 %collective-permute-done.10.others = f32[128,128]{1,0:T(8,128)S(1)} collective-permute-done((f32[128,128]{1,0:T(8,128)S(1)}, f32[128,128]{1,0:T(8,128)S(1)}, u32[]{:S(2)}, u32[]{:S(2)}) %collective-permute-start.10) | collective-permute-done | bytes 65568 | tf_op jit(solution)/shard_map/ppermute | solution.py:218
  27.7 0.8 %last.1 = f32[32,2048]{1,0:T(8,128)} custom-call(f32[32,2048]{1,0:T(8,128)S(1)} %get-tuple-element.26.tied, f32[32,2048]{1,0:T(8,128)S(1)} %get-tuple-element.37.scale, f32[32,512]{1,0:T(8,128)S(1)} %get-tuple-element.38.near, f32[32,512]{1,0:T(8,128)S(1)} %get-tuple-element.40.more, f32[32,512]{1,0:T(8,128)S(1)} %get-tuple-element.41.far, ...), custom_call_target="tpu_custom_call" | custom-call | tf_op jit(solution)/shard_map/last/pallas_call | solution.py:21
  (10 shorter events, 0.1 us)
Async XLA Ops:
  0.6 2.9 %collective-permute-start = (f32[32,2048]{1,0:T(8,128)}, f32[32,2048]{1,0:T(8,128)S(1)}, u32[]{:S(2)}, u32[]{:S(2)}) collective-permute-start(f32[32,2048]{1,0:T(8,128)} %basis.1), channel_id=1, source_target_pairs={{0,1},{1,0},{2,3},{3,2},{4,5},{5,4},{6,7},{7,6},{8,9},{9,8},{10,11... | collective-permute-start | bytes 786440 | tf_op jit(solution)/shard_map/ppermute | solution.py:218
  6.8 1.4 %collective-permute-start.1 = (f32[32,1024]{1,0:T(8,128)S(1)}, f32[32,1024]{1,0:T(8,128)S(1)}, u32[]{:S(2)}, u32[]{:S(2)}) collective-permute-start(f32[32,1024]{1,0:T(8,128)S(1)} %get-tuple-element.25.own), channel_id=1, source_target_pairs={{0,1},{1,0},{2,3},{3,2},{4,5},{5,4},{6,7},{7,6},{8,9},{9,8},{10,11... | collective-permute-start | bytes 393224 | tf_op jit(solution)/shard_map/ppermute | solution.py:218
  9.2 1.4 %collective-permute-start.2 = (f32[256,128]{1,0:T(8,128)S(1)}, f32[256,128]{1,0:T(8,128)S(1)}, u32[]{:S(2)}, u32[]{:S(2)}) collective-permute-start(f32[256,128]{1,0:T(8,128)S(1)} %send.1), channel_id=1, source_target_pairs={{0,1},{1,0},{2,3},{3,2},{4,5},{5,4},{6,7},{7,6},{8,9},{9,8},{10,11... | collective-permute-start | bytes 393224 | tf_op jit(solution)/shard_map/ppermute | solution.py:218
  10.6 4.8 %collective-permute-start.3 = (f32[136,128]{1,0:T(8,128)S(1)}, f32[136,128]{1,0:T(8,128)S(1)}, u32[]{:S(2)}, u32[]{:S(2)}) collective-permute-start(f32[136,128]{1,0:T(8,128)S(1)} %pad_maximum_fusion), channel_id=1, source_target_pairs={{0,5},{1,8},{2,11},{3,6},{4,13},{5,0},{6,3},{7,14},{8,1},{9,12},{1... | collective-permute-start | bytes 208904 | tf_op jit(solution)/shard_map/ppermute | solution.py:244
  13.4 4.5 %collective-permute-start.6 = (f32[128,128]{1,0:T(8,128)S(1)}, f32[128,128]{1,0:T(8,128)S(1)}, u32[]{:S(2)}, u32[]{:S(2)}) collective-permute-start(f32[128,128]{1,0:T(8,128)S(1)} %get-tuple-element.36), channel_id=1, source_target_pairs={{0,5},{1,8},{2,11},{3,6},{4,13},{5,0},{6,3},{7,14},{8,1},{9,12},{1... | collective-permute-start | bytes 196616 | tf_op jit(solution)/shard_map/ppermute | solution.py:244
  15.5 4.7 %collective-permute-start.4 = (f32[136,128]{1,0:T(8,128)S(1)}, f32[136,128]{1,0:T(8,128)S(1)}, u32[]{:S(2)}, u32[]{:S(2)}) collective-permute-start(f32[136,128]{1,0:T(8,128)S(1)} %add.22), channel_id=1, source_target_pairs={{0,3},{1,4},{2,7},{3,0},{4,1},{5,6},{6,5},{7,2},{8,13},{9,10},{10,... | collective-permute-start | bytes 208904 | tf_op jit(solution)/shard_map/ppermute | solution.py:244
  17.9 4.7 %collective-permute-start.7 = (f32[128,128]{1,0:T(8,128)S(1)}, f32[128,128]{1,0:T(8,128)S(1)}, u32[]{:S(2)}, u32[]{:S(2)}) collective-permute-start(f32[128,128]{1,0:T(8,128)S(1)} %add.25), channel_id=1, source_target_pairs={{0,9},{1,2},{2,1},{3,10},{4,7},{5,12},{6,15},{7,4},{8,11},{9,0},{1... | collective-permute-start | bytes 196616 | tf_op jit(solution)/shard_map/ppermute | solution.py:244
  20.1 4.7 %collective-permute-start.5 = (f32[136,128]{1,0:T(8,128)S(1)}, f32[136,128]{1,0:T(8,128)S(1)}, u32[]{:S(2)}, u32[]{:S(2)}) collective-permute-start(f32[136,128]{1,0:T(8,128)S(1)} %add.23), channel_id=1, source_target_pairs={{0,9},{1,2},{2,1},{3,10},{4,7},{5,12},{6,15},{7,4},{8,11},{9,0},{1... | collective-permute-start | bytes 208904 | tf_op jit(solution)/shard_map/ppermute | solution.py:244
  22.6 3.8 %collective-permute-start.8 = (f32[128,128]{1,0:T(8,128)S(1)}, f32[128,128]{1,0:T(8,128)S(1)}, u32[]{:S(2)}, u32[]{:S(2)}) collective-permute-start(f32[128,128]{1,0:T(8,128)S(1)} %add.26), channel_id=1, source_target_pairs={{0,3},{1,4},{2,7},{3,0},{4,1},{5,6},{6,5},{7,2},{8,13},{9,10},{10,... | collective-permute-start | bytes 196616 | tf_op jit(solution)/shard_map/ppermute | solution.py:244
  24.9 2.0 %collective-permute-start.9 = (f32[128,128]{1,0:T(8,128)S(1)}, f32[128,128]{1,0:T(8,128)S(1)}, u32[]{:S(2)}, u32[]{:S(2)}) collective-permute-start(f32[128,128]{1,0:T(8,128)S(1)} %slice.14), channel_id=1, source_target_pairs={{0,1},{1,0},{2,3},{3,2},{4,5},{5,4},{6,7},{7,6},{8,9},{9,8},{10,11... | collective-permute-start | bytes 196616 | tf_op jit(solution)/shard_map/ppermute | solution.py:218
  26.3 1.4 %collective-permute-start.10 = (f32[128,128]{1,0:T(8,128)S(1)}, f32[128,128]{1,0:T(8,128)S(1)}, u32[]{:S(2)}, u32[]{:S(2)}) collective-permute-start(f32[128,128]{1,0:T(8,128)S(1)} %add.27.sums), channel_id=1, source_target_pairs={{0,1},{1,0},{2,3},{3,2},{4,5},{5,4},{6,7},{7,6},{8,9},{9,8},{10,11... | collective-permute-start | bytes 196616 | tf_op jit(solution)/shard_map/ppermute | solution.py:218

commit v6 on v5

--- a/solution.py
+++ b/solution.py
@@ -16,7 +16,7 @@
 HBM, VMEM = pltpu.HBM, pltpu.VMEM
 
 
-def call(kernel, name, ins, outs, scratch=(), flops=0, moved=0):
+def call(kernel, name, ins, outs, scratch=(), flops=0, moved=0, aliases=None):
     params = pltpu.CompilerParams(vmem_limit_bytes=16 * MIB)
     return pl.pallas_call(
         kernel,
@@ -24,6 +24,7 @@
         in_specs=[pl.BlockSpec(memory_space=memory) for memory, _ in ins],
         out_specs=[pl.BlockSpec(memory_space=memory) for memory, _, _ in outs],
         scratch_shapes=list(scratch),
+        input_output_aliases=aliases or {},
         compiler_params=params,
         cost_estimate=pl.CostEstimate(flops=flops, bytes_accessed=moved, transcendentals=0),
         name=name,
@@ -190,27 +191,30 @@
     basis_piece(tied, scale, sums[strip:, :], odd_chip(), 0, near)
 
 
-def middle_kernel(first, tied, scale, sums, others, near, far):
-    odd = odd_chip()
-    basis_piece(tied, scale, sums[...], odd, first, near)
-    basis_piece(tied, scale, others[...], 1 - odd, 0, far)
-
-
-def last_kernel(first, tied, scale, near, more, far, others, new_basis, rest, sems):
-    cols = tied.shape[1]
-    blocks = cols // 2 // LANES
-    odd = odd_chip()
+def write_pieces(new_basis, pieces, sems):
+    blocks = new_basis.shape[1] // 2 // LANES
     copies = []
-    for i, (piece, turned, begin) in enumerate(
-        ((near, odd, 0), (more, odd, first), (far, 1 - odd, 0), (rest, 1 - odd, first))
-    ):
-        if piece is rest:
-            basis_piece(tied, scale, others[...], turned, first, rest)
+    for i, (piece, turned, first) in enumerate(pieces):
         width = piece.shape[1]
-        start = piece_start(turned, begin, width // LANES, blocks)
+        start = piece_start(turned, first, width // LANES, blocks)
         copies.append(pltpu.make_async_copy(piece, new_basis.at[:, pl.ds(start, width)], sems.at[i]))
         copies[-1].start()
-    for copy in copies:
+    return copies
+
+
+def middle_kernel(first, tied, scale, near, sums, others, new_basis, more, far, sems):
+    odd = odd_chip()
+    basis_piece(tied, scale, sums[...], odd, first, more)
+    basis_piece(tied, scale, others[...], 1 - odd, 0, far)
+    for copy in write_pieces(new_basis, ((near, odd, 0), (more, odd, first), (far, 1 - odd, 0)), sems):
+        copy.wait()
+
+
+def last_kernel(first, begun, tied, scale, others, new_basis, rest, sems):
+    del begun
+    turned = 1 - odd_chip()
+    basis_piece(tied, scale, others[...], turned, first, rest)
+    for copy in write_pieces(new_basis, ((rest, turned, first),), sems):
         copy.wait()
 
 
@@ -303,17 +307,19 @@
     rest = my_rest + their_rest
     other_rest = over_det(rest)
     wide = (rank, half - cut // rank * LANES)
-    more, far = call(
+    begun, = call(
         functools.partial(middle_kernel, cut // rank), "middle",
-        [(VMEM, x) for x in (tied, scale, rest, others)],
-        [(VMEM, wide, F32), (VMEM, near.shape, F32)],
+        [(VMEM, x) for x in (tied, scale, near, rest, others)],
+        [(HBM, basis.shape, F32)],
+        [VMEM(wide, F32), VMEM(near.shape, F32), dma((3,))],
         flops=product // 64,
     )
     new_basis, = call(
         functools.partial(last_kernel, cut // rank), "last",
-        [(VMEM, x) for x in (tied, scale, near, more, far, other_rest)],
+        [(HBM, begun)] + [(VMEM, x) for x in (tied, scale, other_rest)],
         [(HBM, basis.shape, F32)],
-        [VMEM(wide, F32), dma((4,))],
+        [VMEM(wide, F32), dma((1,))],
+        aliases={0: 0},
     )
     return new_loadings, new_basis
 

time: 28.6 us -> 28.6 us (level)
  waiting for transfers between devices: 5.28 us -> 4.62 us
  Pallas kernels: 9.67 us -> 10.3 us
    ppermute x5, waiting for transfers between devices: 1.45 us -> 0.79 us  [over_det(): return lax.ppermute(x, 'det', [(0, 1), (1, 0)])]
    pallas_call x8, Pallas kernels: 9.67 us -> 10.3 us  [call(): pl.pallas_call(kernel, out_shape=[memory(shape, dtype) for memory, shape,...]
  transfers between devices with their start and end apart: 11 -> 11, of which waited for: 7 -> 7; matrix products, arithmetic and copies ran while one was open for 0% -> 0% of each run, Pallas kernels for 17% -> 19%
where the time goes in v6:
time: 28.6 us; the launch traced here: 28.5 us
  starting transfers between devices  12.7 us (44%)
  Pallas kernels  10.3 us (36%)
  waiting for transfers between devices  4.62 us (16%)
  between operations  0.75 us (3%)
    ppermute x6, starting transfers between devices, scan_sums(): received.append(lax.ppermute(part, ('scan', 'det'), route))  11.2 us
    pallas_call x8, Pallas kernels, call(): pl.pallas_call(kernel, out_shape=[memory(shape, dtype) for memory, shape,...  10.3 us
    ppermute x6, waiting for transfers between devices, scan_sums(): received.append(lax.ppermute(part, ('scan', 'det'), route))  3.83 us
    ppermute x5, starting transfers between devices, over_det(): return lax.ppermute(x, 'det', [(0, 1), (1, 0)])  1.51 us
    ppermute x5, waiting for transfers between devices, over_det(): return lax.ppermute(x, 'det', [(0, 1), (1, 0)])  0.79 us
  transfers between devices with their start and end apart: 11, of which 7 were waited for; matrix products, arithmetic and copies ran while one was open for 0% of the time, Pallas kernels for 19%

profile of v6, /device:TPU:0, one launch (start us, length us, event | category | flops | bytes accessed | tf_op | source)
XLA Modules:
  0.0 28.5 jit_solution(6153093906669635852)
XLA Ops:
  0.6 0.5 %collective-permute-start = (f32[32,2048]{1,0:T(8,128)}, f32[32,2048]{1,0:T(8,128)S(1)}, u32[]{:S(2)}, u32[]{:S(2)}) collective-permute-start(f32[32,2048]{1,0:T(8,128)} %basis.1), channel_id=1, source_target_pairs={{0,1},{1,0},{2,3},{3,2},{4,5},{5,4},{6,7},{7,6},{8,9},{9,8},{10,11... | collective-permute-start | bytes 786440 | tf_op jit(solution)/shard_map/ppermute | solution.py:222
  1.1 2.4 %load.1 = (f32[32,2048]{1,0:T(8,128)S(1)}, f32[32,1024]{1,0:T(8,128)S(1)}, bf16[512,2048]{1,0:T(8,128)(2,1)S(1)}, bf16[512,2048]{1,0:T(8,128)(2,1)S(1)}) custom-call(f32[1024,2048]{1,0:T(8,128)} %spectra.3, f32[32,2048]{1,0:T(8,128)} %basis.1, f32[32,1024]{1,0:T(8,128)} %loadings.1), custom_call_target="tpu_custom_call" | custom-call | bytes 4194304 | tf_op jit(solution)/shard_map/load/pallas_call | solution.py:21
  3.5 0.0 collective-permute-done.partner
  3.5 3.3 %numer.1 = (f32[32,1024]{1,0:T(8,128)S(1)}, f32[32,2048]{1,0:T(8,128)S(1)}, bf16[512,2048]{1,0:T(8,128)(2,1)S(1)}, bf16[512,2048]{1,0:T(8,128)(2,1)S(1)}) custom-call(f32[1024,2048]{1,0:T(8,128)} %spectra.3, f32[32,2048]{1,0:T(8,128)S(1)} %get-tuple-element.20.basis, f32[32,2048]{1,0:T(8,128)S(1)} %collective-permute-done.partner, ...), custom_call_target="tpu_custom_call" | custom-call | flops 402653184 | bytes 4194304 | tf_op jit(solution)/shard_map/numer/pallas_call | solution.py:21
  6.8 0.1 collective-permute-start.1
  6.9 0.8 %ratio.1 = f32[32,1024]{1,0:T(8,128)S(1)} custom-call(f32[32,2048]{1,0:T(8,128)S(1)} %get-tuple-element.24.tied, f32[32,1024]{1,0:T(8,128)S(1)} %get-tuple-element.25.loadings), custom_call_target="tpu_custom_call" | custom-call | flops 8388608 | tf_op jit(solution)/shard_map/ratio/pallas_call | solution.py:21
  7.7 0.5 %collective-permute-done.1.other = f32[32,1024]{1,0:T(8,128)S(1)} collective-permute-done((f32[32,1024]{1,0:T(8,128)S(1)}, f32[32,1024]{1,0:T(8,128)S(1)}, u32[]{:S(2)}, u32[]{:S(2)}) %collective-permute-start.1) | collective-permute-done | bytes 131104 | tf_op jit(solution)/shard_map/ppermute | solution.py:222
  8.2 0.9 %send.1 = f32[256,128]{1,0:T(8,128)S(1)} custom-call(f32[32,1024]{1,0:T(8,128)S(1)} %get-tuple-element.23.own, f32[32,1024]{1,0:T(8,128)S(1)} %collective-permute-done.1.other, f32[32,1024]{1,0:T(8,128)S(1)} %ratio.1, bf16[512,2048]{1,0:T(8,128)(2,1)S(1)} %get-tuple-element.21.high, bf16[512,2048]{1,0:T(8,128)(2,1)S(1)} %get-tuple-element.22.low, ...), custom_call_target="tpu_custom_call" | custom-call | flops 201326592 | tf_op jit(solution)/shard_map/send/pallas_call | solution.py:21
  9.2 0.2 collective-permute-start.2
  9.4 1.0 %keep.1 = (f32[32,1024]{1,0:T(8,128)}, f32[256,128]{1,0:T(8,128)S(1)}, f32[8,128]{1,0:T(8,128)S(1)}) custom-call(f32[32,1024]{1,0:T(8,128)S(1)} %get-tuple-element.23.own, f32[32,1024]{1,0:T(8,128)S(1)} %collective-permute-done.1.other, f32[32,1024]{1,0:T(8,128)S(1)} %ratio.1, bf16[512,2048]{1,0:T(8,128)(2,1)S(1)} %get-tuple-element.21.high, ...), custom_call_target="tpu_custom_call" | custom-call | flops 201326592 | tf_op jit(solution)/shard_map/keep/pallas_call | solution.py:21
  10.4 0.2 collective-permute-done.2
  10.6 2.7 %collective-permute-start.3 = (f32[136,128]{1,0:T(8,128)S(1)}, f32[136,128]{1,0:T(8,128)S(1)}, u32[]{:S(2)}, u32[]{:S(2)}) collective-permute-start(f32[136,128]{1,0:T(8,128)S(1)} %pad_maximum_fusion), channel_id=1, source_target_pairs={{0,5},{1,8},{2,11},{3,6},{4,13},{5,0},{6,3},{7,14},{8,1},{9,12},{1... | collective-permute-start | bytes 208904 | tf_op jit(solution)/shard_map/ppermute | solution.py:248
  13.4 0.1 collective-permute-start.6
  13.4 2.0 %collective-permute-done.3 = f32[136,128]{1,0:T(8,128)S(1)} collective-permute-done((f32[136,128]{1,0:T(8,128)S(1)}, f32[136,128]{1,0:T(8,128)S(1)}, u32[]{:S(2)}, u32[]{:S(2)}) %collective-permute-start.3) | collective-permute-done | bytes 69664 | tf_op jit(solution)/shard_map/ppermute | solution.py:248
  15.5 2.4 %collective-permute-start.4 = (f32[136,128]{1,0:T(8,128)S(1)}, f32[136,128]{1,0:T(8,128)S(1)}, u32[]{:S(2)}, u32[]{:S(2)}) collective-permute-start(f32[136,128]{1,0:T(8,128)S(1)} %add.22), channel_id=1, source_target_pairs={{0,3},{1,4},{2,7},{3,0},{4,1},{5,6},{6,5},{7,2},{8,13},{9,10},{10,... | collective-permute-start | bytes 208904 | tf_op jit(solution)/shard_map/ppermute | solution.py:248
  17.9 0.0 collective-permute-done.6
  17.9 2.2 %collective-permute-start.7 = (f32[128,128]{1,0:T(8,128)S(1)}, f32[128,128]{1,0:T(8,128)S(1)}, u32[]{:S(2)}, u32[]{:S(2)}) collective-permute-start(f32[128,128]{1,0:T(8,128)S(1)} %add.25), channel_id=1, source_target_pairs={{0,9},{1,2},{2,1},{3,10},{4,7},{5,12},{6,15},{7,4},{8,11},{9,0},{1... | collective-permute-start | bytes 196616 | tf_op jit(solution)/shard_map/ppermute | solution.py:248
  20.1 0.0 collective-permute-done.4
  20.1 2.3 %collective-permute-start.5 = (f32[136,128]{1,0:T(8,128)S(1)}, f32[136,128]{1,0:T(8,128)S(1)}, u32[]{:S(2)}, u32[]{:S(2)}) collective-permute-start(f32[136,128]{1,0:T(8,128)S(1)} %add.23), channel_id=1, source_target_pairs={{0,9},{1,2},{2,1},{3,10},{4,7},{5,12},{6,15},{7,4},{8,11},{9,0},{1... | collective-permute-start | bytes 208904 | tf_op jit(solution)/shard_map/ppermute | solution.py:248
  22.5 0.1 collective-permute-done.7
  22.6 1.4 %collective-permute-start.8 = (f32[128,128]{1,0:T(8,128)S(1)}, f32[128,128]{1,0:T(8,128)S(1)}, u32[]{:S(2)}, u32[]{:S(2)}) collective-permute-start(f32[128,128]{1,0:T(8,128)S(1)} %add.26), channel_id=1, source_target_pairs={{0,3},{1,4},{2,7},{3,0},{4,1},{5,6},{6,5},{7,2},{8,13},{9,10},{10,... | collective-permute-start | bytes 196616 | tf_op jit(solution)/shard_map/ppermute | solution.py:248
  23.9 0.9 %collective-permute-done.5 = f32[136,128]{1,0:T(8,128)S(1)} collective-permute-done((f32[136,128]{1,0:T(8,128)S(1)}, f32[136,128]{1,0:T(8,128)S(1)}, u32[]{:S(2)}, u32[]{:S(2)}) %collective-permute-start.5) | collective-permute-done | bytes 69664 | tf_op jit(solution)/shard_map/ppermute | solution.py:248
  24.9 0.2 collective-permute-start.9
  25.0 0.4 %first.1 = (f32[32,2048]{1,0:T(8,128)S(1)}, f32[32,512]{1,0:T(8,128)S(1)}) custom-call(f32[32,2048]{1,0:T(8,128)S(1)} %get-tuple-element.24.tied, f32[136,128]{1,0:T(8,128)S(1)} %add.24.sums), custom_call_target="tpu_custom_call" | custom-call | flops 4194304 | tf_op jit(solution)/shard_map/first/pallas_call | solution.py:21
  25.5 0.8 %collective-permute-done.8 = f32[128,128]{1,0:T(8,128)S(1)} collective-permute-done((f32[128,128]{1,0:T(8,128)S(1)}, f32[128,128]{1,0:T(8,128)S(1)}, u32[]{:S(2)}, u32[]{:S(2)}) %collective-permute-start.8) | collective-permute-done | bytes 65568 | tf_op jit(solution)/shard_map/ppermute | solution.py:248
  26.3 0.5 %collective-permute-start.10 = (f32[128,128]{1,0:T(8,128)S(1)}, f32[128,128]{1,0:T(8,128)S(1)}, u32[]{:S(2)}, u32[]{:S(2)}) collective-permute-start(f32[128,128]{1,0:T(8,128)S(1)} %add.27.sums), channel_id=1, source_target_pairs={{0,1},{1,0},{2,3},{3,2},{4,5},{5,4},{6,7},{7,6},{8,9},{9,8},{10,11... | collective-permute-start | bytes 196616 | tf_op jit(solution)/shard_map/ppermute | solution.py:222
  26.8 0.0 collective-permute-done.9.others
  26.8 0.8 %middle.1.begun = f32[32,2048]{1,0:T(8,128)} custom-call(f32[32,2048]{1,0:T(8,128)S(1)} %get-tuple-element.24.tied, f32[32,2048]{1,0:T(8,128)S(1)} %get-tuple-element.35.scale, f32[32,512]{1,0:T(8,128)S(1)} %get-tuple-element.36.near, f32[128,128]{1,0:T(8,128)S(1)} %add.27.sums, f32[128,128]{1,0:T(8,128)S(1)} %collective-permute-done.9.others), custom_call_target="tpu_custom_call" | custom-call | flops 2097152 | tf_op jit(solution)/shard_map/middle/pallas_call | solution.py:21
  27.6 0.1 collective-permute-done.10.others
  27.7 0.7 %last.1 = f32[32,2048]{1,0:T(8,128)} custom-call(f32[32,2048]{1,0:T(8,128)} %middle.1.begun, f32[32,2048]{1,0:T(8,128)S(1)} %get-tuple-element.24.tied, f32[32,2048]{1,0:T(8,128)S(1)} %get-tuple-element.35.scale, f32[128,128]{1,0:T(8,128)S(1)} %collective-permute-done.10.others), custom_call_target="tpu_custom_call", output_to_operand_aliasing={{}: (0, {})} | custom-call | tf_op jit(solution)/shard_map/last/pallas_call | solution.py:21
  (10 shorter events, 0.1 us)
Async XLA Ops:
  0.6 2.9 %collective-permute-start = (f32[32,2048]{1,0:T(8,128)}, f32[32,2048]{1,0:T(8,128)S(1)}, u32[]{:S(2)}, u32[]{:S(2)}) collective-permute-start(f32[32,2048]{1,0:T(8,128)} %basis.1), channel_id=1, source_target_pairs={{0,1},{1,0},{2,3},{3,2},{4,5},{5,4},{6,7},{7,6},{8,9},{9,8},{10,11... | collective-permute-start | bytes 786440 | tf_op jit(solution)/shard_map/ppermute | solution.py:222
  6.8 1.4 %collective-permute-start.1 = (f32[32,1024]{1,0:T(8,128)S(1)}, f32[32,1024]{1,0:T(8,128)S(1)}, u32[]{:S(2)}, u32[]{:S(2)}) collective-permute-start(f32[32,1024]{1,0:T(8,128)S(1)} %get-tuple-element.23.own), channel_id=1, source_target_pairs={{0,1},{1,0},{2,3},{3,2},{4,5},{5,4},{6,7},{7,6},{8,9},{9,8},{10,11... | collective-permute-start | bytes 393224 | tf_op jit(solution)/shard_map/ppermute | solution.py:222
  9.2 1.4 %collective-permute-start.2 = (f32[256,128]{1,0:T(8,128)S(1)}, f32[256,128]{1,0:T(8,128)S(1)}, u32[]{:S(2)}, u32[]{:S(2)}) collective-permute-start(f32[256,128]{1,0:T(8,128)S(1)} %send.1), channel_id=1, source_target_pairs={{0,1},{1,0},{2,3},{3,2},{4,5},{5,4},{6,7},{7,6},{8,9},{9,8},{10,11... | collective-permute-start | bytes 393224 | tf_op jit(solution)/shard_map/ppermute | solution.py:222
  10.6 4.8 %collective-permute-start.3 = (f32[136,128]{1,0:T(8,128)S(1)}, f32[136,128]{1,0:T(8,128)S(1)}, u32[]{:S(2)}, u32[]{:S(2)}) collective-permute-start(f32[136,128]{1,0:T(8,128)S(1)} %pad_maximum_fusion), channel_id=1, source_target_pairs={{0,5},{1,8},{2,11},{3,6},{4,13},{5,0},{6,3},{7,14},{8,1},{9,12},{1... | collective-permute-start | bytes 208904 | tf_op jit(solution)/shard_map/ppermute | solution.py:248
  13.4 4.5 %collective-permute-start.6 = (f32[128,128]{1,0:T(8,128)S(1)}, f32[128,128]{1,0:T(8,128)S(1)}, u32[]{:S(2)}, u32[]{:S(2)}) collective-permute-start(f32[128,128]{1,0:T(8,128)S(1)} %get-tuple-element.34), channel_id=1, source_target_pairs={{0,5},{1,8},{2,11},{3,6},{4,13},{5,0},{6,3},{7,14},{8,1},{9,12},{1... | collective-permute-start | bytes 196616 | tf_op jit(solution)/shard_map/ppermute | solution.py:248
  15.5 4.7 %collective-permute-start.4 = (f32[136,128]{1,0:T(8,128)S(1)}, f32[136,128]{1,0:T(8,128)S(1)}, u32[]{:S(2)}, u32[]{:S(2)}) collective-permute-start(f32[136,128]{1,0:T(8,128)S(1)} %add.22), channel_id=1, source_target_pairs={{0,3},{1,4},{2,7},{3,0},{4,1},{5,6},{6,5},{7,2},{8,13},{9,10},{10,... | collective-permute-start | bytes 208904 | tf_op jit(solution)/shard_map/ppermute | solution.py:248
  17.9 4.7 %collective-permute-start.7 = (f32[128,128]{1,0:T(8,128)S(1)}, f32[128,128]{1,0:T(8,128)S(1)}, u32[]{:S(2)}, u32[]{:S(2)}) collective-permute-start(f32[128,128]{1,0:T(8,128)S(1)} %add.25), channel_id=1, source_target_pairs={{0,9},{1,2},{2,1},{3,10},{4,7},{5,12},{6,15},{7,4},{8,11},{9,0},{1... | collective-permute-start | bytes 196616 | tf_op jit(solution)/shard_map/ppermute | solution.py:248
  20.1 4.7 %collective-permute-start.5 = (f32[136,128]{1,0:T(8,128)S(1)}, f32[136,128]{1,0:T(8,128)S(1)}, u32[]{:S(2)}, u32[]{:S(2)}) collective-permute-start(f32[136,128]{1,0:T(8,128)S(1)} %add.23), channel_id=1, source_target_pairs={{0,9},{1,2},{2,1},{3,10},{4,7},{5,12},{6,15},{7,4},{8,11},{9,0},{1... | collective-permute-start | bytes 208904 | tf_op jit(solution)/shard_map/ppermute | solution.py:248
  22.6 3.8 %collective-permute-start.8 = (f32[128,128]{1,0:T(8,128)S(1)}, f32[128,128]{1,0:T(8,128)S(1)}, u32[]{:S(2)}, u32[]{:S(2)}) collective-permute-start(f32[128,128]{1,0:T(8,128)S(1)} %add.26), channel_id=1, source_target_pairs={{0,3},{1,4},{2,7},{3,0},{4,1},{5,6},{6,5},{7,2},{8,13},{9,10},{10,... | collective-permute-start | bytes 196616 | tf_op jit(solution)/shard_map/ppermute | solution.py:248
  24.9 2.0 %collective-permute-start.9 = (f32[128,128]{1,0:T(8,128)S(1)}, f32[128,128]{1,0:T(8,128)S(1)}, u32[]{:S(2)}, u32[]{:S(2)}) collective-permute-start(f32[128,128]{1,0:T(8,128)S(1)} %slice.14), channel_id=1, source_target_pairs={{0,1},{1,0},{2,3},{3,2},{4,5},{5,4},{6,7},{7,6},{8,9},{9,8},{10,11... | collective-permute-start | bytes 196616 | tf_op jit(solution)/shard_map/ppermute | solution.py:222
  26.3 1.4 %collective-permute-start.10 = (f32[128,128]{1,0:T(8,128)S(1)}, f32[128,128]{1,0:T(8,128)S(1)}, u32[]{:S(2)}, u32[]{:S(2)}) collective-permute-start(f32[128,128]{1,0:T(8,128)S(1)} %add.27.sums), channel_id=1, source_target_pairs={{0,1},{1,0},{2,3},{3,2},{4,5},{5,4},{6,7},{7,6},{8,9},{9,8},{10,11... | collective-permute-start | bytes 196616 | tf_op jit(solution)/shard_map/ppermute | solution.py:222

commit v7 on v5

--- a/solution.py
+++ b/solution.py
@@ -90,13 +90,22 @@
         terms = terms[:, :rank] + terms[:, rank:] + dot(block_low, tied_parts[:rank], NT)
         numer[:, pl.ds(start, block_high.shape[0])] = terms.T
 
+    def turn(start, block_high, block_low):
+        terms = dot(tied_parts, block_high, NT)
+        numer[:, pl.ds(start, block_high.shape[0])] = (
+            terms[:rank] + terms[rank:] + dot(tied_parts[:rank], block_low, NT)
+        )
+
     for start in range(0, early, group):
         at = pl.ds(start, min(group, early - start))
-        put(start, high[at, :], low[at, :])
+        (turn if start // group % 2 == 1 else put)(start, high[at, :], low[at, :])
     for whole, copy in copies:
         copy.wait()
         late_high[whole, :], late_low[whole, :] = halves(stage[whole, :])
-        put(early + whole.start, late_high[whole, :], late_low[whole, :])
+        size = whole.size // 2
+        for i, step in enumerate((put, turn)):
+            at = pl.ds(whole.start + i * size, size)
+            step(early + at.start, late_high[at, :], late_low[at, :])
 
 
 def ratio_kernel(tied, loadings, ratio):

time: 28.6 us -> 28.6 us (level)
  no operation moved by 1% of the time
where the time goes in v7:
time: 28.6 us; the launch traced here: 28.4 us
  starting transfers between devices  12.7 us (44%)
  Pallas kernels  9.62 us (34%)
  waiting for transfers between devices  5.28 us (18%)
  between operations  0.75 us (3%)
    ppermute x6, starting transfers between devices, scan_sums(): received.append(lax.ppermute(part, ('scan', 'det'), route))  11.2 us
    pallas_call x8, Pallas kernels, call(): pl.pallas_call(kernel, out_shape=[memory(shape, dtype) for memory, shape,...  9.62 us
    ppermute x6, waiting for transfers between devices, scan_sums(): received.append(lax.ppermute(part, ('scan', 'det'), route))  3.83 us
    ppermute x5, starting transfers between devices, over_det(): return lax.ppermute(x, 'det', [(0, 1), (1, 0)])  1.51 us
    ppermute x5, waiting for transfers between devices, over_det(): return lax.ppermute(x, 'det', [(0, 1), (1, 0)])  1.45 us
  transfers between devices with their start and end apart: 11, of which 7 were waited for; matrix products, arithmetic and copies ran while one was open for 0% of the time, Pallas kernels for 17%

profile of v7, /device:TPU:0, one launch (start us, length us, event | category | flops | bytes accessed | tf_op | source)
XLA Modules:
  0.0 28.4 jit_solution(14240909905337376941)
XLA Ops:
  0.6 0.5 %collective-permute-start = (f32[32,2048]{1,0:T(8,128)}, f32[32,2048]{1,0:T(8,128)S(1)}, u32[]{:S(2)}, u32[]{:S(2)}) collective-permute-start(f32[32,2048]{1,0:T(8,128)} %basis.1), channel_id=1, source_target_pairs={{0,1},{1,0},{2,3},{3,2},{4,5},{5,4},{6,7},{7,6},{8,9},{9,8},{10,11... | collective-permute-start | bytes 786440 | tf_op jit(solution)/shard_map/ppermute | solution.py:227
  1.1 2.4 %load.1 = (f32[32,2048]{1,0:T(8,128)S(1)}, f32[32,1024]{1,0:T(8,128)S(1)}, bf16[512,2048]{1,0:T(8,128)(2,1)S(1)}, bf16[512,2048]{1,0:T(8,128)(2,1)S(1)}) custom-call(f32[1024,2048]{1,0:T(8,128)} %spectra.3, f32[32,2048]{1,0:T(8,128)} %basis.1, f32[32,1024]{1,0:T(8,128)} %loadings.1), custom_call_target="tpu_custom_call" | custom-call | bytes 4194304 | tf_op jit(solution)/shard_map/load/pallas_call | solution.py:21
  3.5 0.0 collective-permute-done.partner
  3.5 3.2 %numer.1 = (f32[32,1024]{1,0:T(8,128)S(1)}, f32[32,2048]{1,0:T(8,128)S(1)}, bf16[512,2048]{1,0:T(8,128)(2,1)S(1)}, bf16[512,2048]{1,0:T(8,128)(2,1)S(1)}) custom-call(f32[1024,2048]{1,0:T(8,128)} %spectra.3, f32[32,2048]{1,0:T(8,128)S(1)} %get-tuple-element.22.basis, f32[32,2048]{1,0:T(8,128)S(1)} %collective-permute-done.partner, ...), custom_call_target="tpu_custom_call" | custom-call | flops 402653184 | bytes 4194304 | tf_op jit(solution)/shard_map/numer/pallas_call | solution.py:21
  6.8 0.1 collective-permute-start.1
  6.9 0.7 %ratio.1 = f32[32,1024]{1,0:T(8,128)S(1)} custom-call(f32[32,2048]{1,0:T(8,128)S(1)} %get-tuple-element.26.tied, f32[32,1024]{1,0:T(8,128)S(1)} %get-tuple-element.27.loadings), custom_call_target="tpu_custom_call" | custom-call | flops 8388608 | tf_op jit(solution)/shard_map/ratio/pallas_call | solution.py:21
  7.6 0.5 %collective-permute-done.1.other = f32[32,1024]{1,0:T(8,128)S(1)} collective-permute-done((f32[32,1024]{1,0:T(8,128)S(1)}, f32[32,1024]{1,0:T(8,128)S(1)}, u32[]{:S(2)}, u32[]{:S(2)}) %collective-permute-start.1) | collective-permute-done | bytes 131104 | tf_op jit(solution)/shard_map/ppermute | solution.py:227
  8.2 0.9 %send.1 = f32[256,128]{1,0:T(8,128)S(1)} custom-call(f32[32,1024]{1,0:T(8,128)S(1)} %get-tuple-element.25.own, f32[32,1024]{1,0:T(8,128)S(1)} %collective-permute-done.1.other, f32[32,1024]{1,0:T(8,128)S(1)} %ratio.1, bf16[512,2048]{1,0:T(8,128)(2,1)S(1)} %get-tuple-element.23.high, bf16[512,2048]{1,0:T(8,128)(2,1)S(1)} %get-tuple-element.24.low, ...), custom_call_target="tpu_custom_call" | custom-call | flops 201326592 | tf_op jit(solution)/shard_map/send/pallas_call | solution.py:21
  9.1 0.2 collective-permute-start.2
  9.3 1.0 %keep.1 = (f32[32,1024]{1,0:T(8,128)}, f32[256,128]{1,0:T(8,128)S(1)}, f32[8,128]{1,0:T(8,128)S(1)}) custom-call(f32[32,1024]{1,0:T(8,128)S(1)} %get-tuple-element.25.own, f32[32,1024]{1,0:T(8,128)S(1)} %collective-permute-done.1.other, f32[32,1024]{1,0:T(8,128)S(1)} %ratio.1, bf16[512,2048]{1,0:T(8,128)(2,1)S(1)} %get-tuple-element.23.high, ...), custom_call_target="tpu_custom_call" | custom-call | flops 201326592 | tf_op jit(solution)/shard_map/keep/pallas_call | solution.py:21
  10.4 0.2 collective-permute-done.2
  10.6 2.7 %collective-permute-start.3 = (f32[136,128]{1,0:T(8,128)S(1)}, f32[136,128]{1,0:T(8,128)S(1)}, u32[]{:S(2)}, u32[]{:S(2)}) collective-permute-start(f32[136,128]{1,0:T(8,128)S(1)} %pad_maximum_fusion), channel_id=1, source_target_pairs={{0,5},{1,8},{2,11},{3,6},{4,13},{5,0},{6,3},{7,14},{8,1},{9,12},{1... | collective-permute-start | bytes 208904 | tf_op jit(solution)/shard_map/ppermute | solution.py:253
  13.3 0.1 collective-permute-start.6
  13.4 2.0 %collective-permute-done.3 = f32[136,128]{1,0:T(8,128)S(1)} collective-permute-done((f32[136,128]{1,0:T(8,128)S(1)}, f32[136,128]{1,0:T(8,128)S(1)}, u32[]{:S(2)}, u32[]{:S(2)}) %collective-permute-start.3) | collective-permute-done | bytes 69664 | tf_op jit(solution)/shard_map/ppermute | solution.py:253
  15.4 2.4 %collective-permute-start.4 = (f32[136,128]{1,0:T(8,128)S(1)}, f32[136,128]{1,0:T(8,128)S(1)}, u32[]{:S(2)}, u32[]{:S(2)}) collective-permute-start(f32[136,128]{1,0:T(8,128)S(1)} %add.22), channel_id=1, source_target_pairs={{0,3},{1,4},{2,7},{3,0},{4,1},{5,6},{6,5},{7,2},{8,13},{9,10},{10,... | collective-permute-start | bytes 208904 | tf_op jit(solution)/shard_map/ppermute | solution.py:253
  17.8 0.0 collective-permute-done.6
  17.8 2.3 %collective-permute-start.7 = (f32[128,128]{1,0:T(8,128)S(1)}, f32[128,128]{1,0:T(8,128)S(1)}, u32[]{:S(2)}, u32[]{:S(2)}) collective-permute-start(f32[128,128]{1,0:T(8,128)S(1)} %add.25), channel_id=1, source_target_pairs={{0,9},{1,2},{2,1},{3,10},{4,7},{5,12},{6,15},{7,4},{8,11},{9,0},{1... | collective-permute-start | bytes 196616 | tf_op jit(solution)/shard_map/ppermute | solution.py:253
  20.1 0.0 collective-permute-done.4
  20.1 2.3 %collective-permute-start.5 = (f32[136,128]{1,0:T(8,128)S(1)}, f32[136,128]{1,0:T(8,128)S(1)}, u32[]{:S(2)}, u32[]{:S(2)}) collective-permute-start(f32[136,128]{1,0:T(8,128)S(1)} %add.23), channel_id=1, source_target_pairs={{0,9},{1,2},{2,1},{3,10},{4,7},{5,12},{6,15},{7,4},{8,11},{9,0},{1... | collective-permute-start | bytes 208904 | tf_op jit(solution)/shard_map/ppermute | solution.py:253
  22.4 0.1 collective-permute-done.7
  22.5 1.4 %collective-permute-start.8 = (f32[128,128]{1,0:T(8,128)S(1)}, f32[128,128]{1,0:T(8,128)S(1)}, u32[]{:S(2)}, u32[]{:S(2)}) collective-permute-start(f32[128,128]{1,0:T(8,128)S(1)} %add.26), channel_id=1, source_target_pairs={{0,3},{1,4},{2,7},{3,0},{4,1},{5,6},{6,5},{7,2},{8,13},{9,10},{10,... | collective-permute-start | bytes 196616 | tf_op jit(solution)/shard_map/ppermute | solution.py:253
  23.9 0.9 %collective-permute-done.5 = f32[136,128]{1,0:T(8,128)S(1)} collective-permute-done((f32[136,128]{1,0:T(8,128)S(1)}, f32[136,128]{1,0:T(8,128)S(1)}, u32[]{:S(2)}, u32[]{:S(2)}) %collective-permute-start.5) | collective-permute-done | bytes 69664 | tf_op jit(solution)/shard_map/ppermute | solution.py:253
  24.8 0.2 collective-permute-start.9
  25.0 0.4 %first.1 = (f32[32,2048]{1,0:T(8,128)S(1)}, f32[32,512]{1,0:T(8,128)S(1)}) custom-call(f32[32,2048]{1,0:T(8,128)S(1)} %get-tuple-element.26.tied, f32[136,128]{1,0:T(8,128)S(1)} %add.24.sums), custom_call_target="tpu_custom_call" | custom-call | flops 4194304 | tf_op jit(solution)/shard_map/first/pallas_call | solution.py:21
  25.4 0.8 %collective-permute-done.8 = f32[128,128]{1,0:T(8,128)S(1)} collective-permute-done((f32[128,128]{1,0:T(8,128)S(1)}, f32[128,128]{1,0:T(8,128)S(1)}, u32[]{:S(2)}, u32[]{:S(2)}) %collective-permute-start.8) | collective-permute-done | bytes 65568 | tf_op jit(solution)/shard_map/ppermute | solution.py:253
  26.3 0.5 %collective-permute-start.10 = (f32[128,128]{1,0:T(8,128)S(1)}, f32[128,128]{1,0:T(8,128)S(1)}, u32[]{:S(2)}, u32[]{:S(2)}) collective-permute-start(f32[128,128]{1,0:T(8,128)S(1)} %add.27.sums), channel_id=1, source_target_pairs={{0,1},{1,0},{2,3},{3,2},{4,5},{5,4},{6,7},{7,6},{8,9},{9,8},{10,11... | collective-permute-start | bytes 196616 | tf_op jit(solution)/shard_map/ppermute | solution.py:227
  26.8 0.0 collective-permute-done.9.others
  26.8 0.1 middle.1
  26.9 0.8 %collective-permute-done.10.others = f32[128,128]{1,0:T(8,128)S(1)} collective-permute-done((f32[128,128]{1,0:T(8,128)S(1)}, f32[128,128]{1,0:T(8,128)S(1)}, u32[]{:S(2)}, u32[]{:S(2)}) %collective-permute-start.10) | collective-permute-done | bytes 65568 | tf_op jit(solution)/shard_map/ppermute | solution.py:227
  27.7 0.8 %last.1 = f32[32,2048]{1,0:T(8,128)} custom-call(f32[32,2048]{1,0:T(8,128)S(1)} %get-tuple-element.26.tied, f32[32,2048]{1,0:T(8,128)S(1)} %get-tuple-element.37.scale, f32[32,512]{1,0:T(8,128)S(1)} %get-tuple-element.38.near, f32[32,512]{1,0:T(8,128)S(1)} %get-tuple-element.40.more, f32[32,512]{1,0:T(8,128)S(1)} %get-tuple-element.41.far, ...), custom_call_target="tpu_custom_call" | custom-call | tf_op jit(solution)/shard_map/last/pallas_call | solution.py:21
  (10 shorter events, 0.1 us)
Async XLA Ops:
  0.6 2.9 %collective-permute-start = (f32[32,2048]{1,0:T(8,128)}, f32[32,2048]{1,0:T(8,128)S(1)}, u32[]{:S(2)}, u32[]{:S(2)}) collective-permute-start(f32[32,2048]{1,0:T(8,128)} %basis.1), channel_id=1, source_target_pairs={{0,1},{1,0},{2,3},{3,2},{4,5},{5,4},{6,7},{7,6},{8,9},{9,8},{10,11... | collective-permute-start | bytes 786440 | tf_op jit(solution)/shard_map/ppermute | solution.py:227
  6.8 1.4 %collective-permute-start.1 = (f32[32,1024]{1,0:T(8,128)S(1)}, f32[32,1024]{1,0:T(8,128)S(1)}, u32[]{:S(2)}, u32[]{:S(2)}) collective-permute-start(f32[32,1024]{1,0:T(8,128)S(1)} %get-tuple-element.25.own), channel_id=1, source_target_pairs={{0,1},{1,0},{2,3},{3,2},{4,5},{5,4},{6,7},{7,6},{8,9},{9,8},{10,11... | collective-permute-start | bytes 393224 | tf_op jit(solution)/shard_map/ppermute | solution.py:227
  9.1 1.4 %collective-permute-start.2 = (f32[256,128]{1,0:T(8,128)S(1)}, f32[256,128]{1,0:T(8,128)S(1)}, u32[]{:S(2)}, u32[]{:S(2)}) collective-permute-start(f32[256,128]{1,0:T(8,128)S(1)} %send.1), channel_id=1, source_target_pairs={{0,1},{1,0},{2,3},{3,2},{4,5},{5,4},{6,7},{7,6},{8,9},{9,8},{10,11... | collective-permute-start | bytes 393224 | tf_op jit(solution)/shard_map/ppermute | solution.py:227
  10.6 4.8 %collective-permute-start.3 = (f32[136,128]{1,0:T(8,128)S(1)}, f32[136,128]{1,0:T(8,128)S(1)}, u32[]{:S(2)}, u32[]{:S(2)}) collective-permute-start(f32[136,128]{1,0:T(8,128)S(1)} %pad_maximum_fusion), channel_id=1, source_target_pairs={{0,5},{1,8},{2,11},{3,6},{4,13},{5,0},{6,3},{7,14},{8,1},{9,12},{1... | collective-permute-start | bytes 208904 | tf_op jit(solution)/shard_map/ppermute | solution.py:253
  13.3 4.5 %collective-permute-start.6 = (f32[128,128]{1,0:T(8,128)S(1)}, f32[128,128]{1,0:T(8,128)S(1)}, u32[]{:S(2)}, u32[]{:S(2)}) collective-permute-start(f32[128,128]{1,0:T(8,128)S(1)} %get-tuple-element.36), channel_id=1, source_target_pairs={{0,5},{1,8},{2,11},{3,6},{4,13},{5,0},{6,3},{7,14},{8,1},{9,12},{1... | collective-permute-start | bytes 196616 | tf_op jit(solution)/shard_map/ppermute | solution.py:253
  15.4 4.7 %collective-permute-start.4 = (f32[136,128]{1,0:T(8,128)S(1)}, f32[136,128]{1,0:T(8,128)S(1)}, u32[]{:S(2)}, u32[]{:S(2)}) collective-permute-start(f32[136,128]{1,0:T(8,128)S(1)} %add.22), channel_id=1, source_target_pairs={{0,3},{1,4},{2,7},{3,0},{4,1},{5,6},{6,5},{7,2},{8,13},{9,10},{10,... | collective-permute-start | bytes 208904 | tf_op jit(solution)/shard_map/ppermute | solution.py:253
  17.8 4.7 %collective-permute-start.7 = (f32[128,128]{1,0:T(8,128)S(1)}, f32[128,128]{1,0:T(8,128)S(1)}, u32[]{:S(2)}, u32[]{:S(2)}) collective-permute-start(f32[128,128]{1,0:T(8,128)S(1)} %add.25), channel_id=1, source_target_pairs={{0,9},{1,2},{2,1},{3,10},{4,7},{5,12},{6,15},{7,4},{8,11},{9,0},{1... | collective-permute-start | bytes 196616 | tf_op jit(solution)/shard_map/ppermute | solution.py:253
  20.1 4.7 %collective-permute-start.5 = (f32[136,128]{1,0:T(8,128)S(1)}, f32[136,128]{1,0:T(8,128)S(1)}, u32[]{:S(2)}, u32[]{:S(2)}) collective-permute-start(f32[136,128]{1,0:T(8,128)S(1)} %add.23), channel_id=1, source_target_pairs={{0,9},{1,2},{2,1},{3,10},{4,7},{5,12},{6,15},{7,4},{8,11},{9,0},{1... | collective-permute-start | bytes 208904 | tf_op jit(solution)/shard_map/ppermute | solution.py:253
  22.5 3.8 %collective-permute-start.8 = (f32[128,128]{1,0:T(8,128)S(1)}, f32[128,128]{1,0:T(8,128)S(1)}, u32[]{:S(2)}, u32[]{:S(2)}) collective-permute-start(f32[128,128]{1,0:T(8,128)S(1)} %add.26), channel_id=1, source_target_pairs={{0,3},{1,4},{2,7},{3,0},{4,1},{5,6},{6,5},{7,2},{8,13},{9,10},{10,... | collective-permute-start | bytes 196616 | tf_op jit(solution)/shard_map/ppermute | solution.py:253
  24.8 2.0 %collective-permute-start.9 = (f32[128,128]{1,0:T(8,128)S(1)}, f32[128,128]{1,0:T(8,128)S(1)}, u32[]{:S(2)}, u32[]{:S(2)}) collective-permute-start(f32[128,128]{1,0:T(8,128)S(1)} %slice.14), channel_id=1, source_target_pairs={{0,1},{1,0},{2,3},{3,2},{4,5},{5,4},{6,7},{7,6},{8,9},{9,8},{10,11... | collective-permute-start | bytes 196616 | tf_op jit(solution)/shard_map/ppermute | solution.py:227
  26.3 1.4 %collective-permute-start.10 = (f32[128,128]{1,0:T(8,128)S(1)}, f32[128,128]{1,0:T(8,128)S(1)}, u32[]{:S(2)}, u32[]{:S(2)}) collective-permute-start(f32[128,128]{1,0:T(8,128)S(1)} %add.27.sums), channel_id=1, source_target_pairs={{0,1},{1,0},{2,3},{3,2},{4,5},{5,4},{6,7},{7,6},{8,9},{9,8},{10,11... | collective-permute-start | bytes 196616 | tf_op jit(solution)/shard_map/ppermute | solution.py:227

commit v8 on v7

--- a/solution.py
+++ b/solution.py
@@ -288,7 +288,7 @@
     ratio, = call(ratio_kernel, "ratio", [(VMEM, tied), (VMEM, near_loadings)], [(VMEM, loadings.shape, F32)], flops=product // 16)
     operands = [(VMEM, x) for x in (numer, other, ratio, high, low, late_high, late_low)]
     send, = call(
-        functools.partial(send_kernel, 512), "send", operands, [(VMEM, (tall, LANES), F32)], flops=3 * product // 2
+        functools.partial(send_kernel, 256), "send", operands, [(VMEM, (tall, LANES), F32)], flops=3 * product // 2
     )
     received = over_det(send)
     new_loadings, keep, cross = call(

time: 28.6 us -> 28.6 us (level)
  no operation moved by 1% of the time
where the time goes in v8:
time: 28.6 us; the launch traced here: 28.5 us
  starting transfers between devices  12.7 us (44%)
  Pallas kernels  9.62 us (34%)
  waiting for transfers between devices  5.3 us (19%)
  between operations  0.75 us (3%)
    ppermute x6, starting transfers between devices, scan_sums(): received.append(lax.ppermute(part, ('scan', 'det'), route))  11.2 us
    pallas_call x8, Pallas kernels, call(): pl.pallas_call(kernel, out_shape=[memory(shape, dtype) for memory, shape,...  9.62 us
    ppermute x6, waiting for transfers between devices, scan_sums(): received.append(lax.ppermute(part, ('scan', 'det'), route))  3.85 us
    ppermute x5, starting transfers between devices, over_det(): return lax.ppermute(x, 'det', [(0, 1), (1, 0)])  1.51 us
    ppermute x5, waiting for transfers between devices, over_det(): return lax.ppermute(x, 'det', [(0, 1), (1, 0)])  1.45 us
  transfers between devices with their start and end apart: 11, of which 7 were waited for; matrix products, arithmetic and copies ran while one was open for 0% of the time, Pallas kernels for 17%

profile of v8, /device:TPU:0, one launch (start us, length us, event | category | flops | bytes accessed | tf_op | source)
XLA Modules:
  0.0 28.5 jit_solution(1223931120607786155)
XLA Ops:
  0.6 0.5 %collective-permute-start = (f32[32,2048]{1,0:T(8,128)}, f32[32,2048]{1,0:T(8,128)S(1)}, u32[]{:S(2)}, u32[]{:S(2)}) collective-permute-start(f32[32,2048]{1,0:T(8,128)} %basis.1), channel_id=1, source_target_pairs={{0,1},{1,0},{2,3},{3,2},{4,5},{5,4},{6,7},{7,6},{8,9},{9,8},{10,11... | collective-permute-start | bytes 786440 | tf_op jit(solution)/shard_map/ppermute | solution.py:227
  1.1 2.4 %load.1 = (f32[32,2048]{1,0:T(8,128)S(1)}, f32[32,1024]{1,0:T(8,128)S(1)}, bf16[512,2048]{1,0:T(8,128)(2,1)S(1)}, bf16[512,2048]{1,0:T(8,128)(2,1)S(1)}) custom-call(f32[1024,2048]{1,0:T(8,128)} %spectra.3, f32[32,2048]{1,0:T(8,128)} %basis.1, f32[32,1024]{1,0:T(8,128)} %loadings.1), custom_call_target="tpu_custom_call" | custom-call | bytes 4194304 | tf_op jit(solution)/shard_map/load/pallas_call | solution.py:21
  3.5 0.0 collective-permute-done.partner
  3.5 3.2 %numer.1 = (f32[32,1024]{1,0:T(8,128)S(1)}, f32[32,2048]{1,0:T(8,128)S(1)}, bf16[512,2048]{1,0:T(8,128)(2,1)S(1)}, bf16[512,2048]{1,0:T(8,128)(2,1)S(1)}) custom-call(f32[1024,2048]{1,0:T(8,128)} %spectra.3, f32[32,2048]{1,0:T(8,128)S(1)} %get-tuple-element.22.basis, f32[32,2048]{1,0:T(8,128)S(1)} %collective-permute-done.partner, ...), custom_call_target="tpu_custom_call" | custom-call | flops 402653184 | bytes 4194304 | tf_op jit(solution)/shard_map/numer/pallas_call | solution.py:21
  6.8 0.1 collective-permute-start.1
  6.9 0.7 %ratio.1 = f32[32,1024]{1,0:T(8,128)S(1)} custom-call(f32[32,2048]{1,0:T(8,128)S(1)} %get-tuple-element.26.tied, f32[32,1024]{1,0:T(8,128)S(1)} %get-tuple-element.27.loadings), custom_call_target="tpu_custom_call" | custom-call | flops 8388608 | tf_op jit(solution)/shard_map/ratio/pallas_call | solution.py:21
  7.6 0.5 %collective-permute-done.1.other = f32[32,1024]{1,0:T(8,128)S(1)} collective-permute-done((f32[32,1024]{1,0:T(8,128)S(1)}, f32[32,1024]{1,0:T(8,128)S(1)}, u32[]{:S(2)}, u32[]{:S(2)}) %collective-permute-start.1) | collective-permute-done | bytes 131104 | tf_op jit(solution)/shard_map/ppermute | solution.py:227
  8.2 0.9 %send.1 = f32[256,128]{1,0:T(8,128)S(1)} custom-call(f32[32,1024]{1,0:T(8,128)S(1)} %get-tuple-element.25.own, f32[32,1024]{1,0:T(8,128)S(1)} %collective-permute-done.1.other, f32[32,1024]{1,0:T(8,128)S(1)} %ratio.1, bf16[512,2048]{1,0:T(8,128)(2,1)S(1)} %get-tuple-element.23.high, bf16[512,2048]{1,0:T(8,128)(2,1)S(1)} %get-tuple-element.24.low, ...), custom_call_target="tpu_custom_call" | custom-call | flops 201326592 | tf_op jit(solution)/shard_map/send/pallas_call | solution.py:21
  9.1 0.2 collective-permute-start.2
  9.3 1.0 %keep.1 = (f32[32,1024]{1,0:T(8,128)}, f32[256,128]{1,0:T(8,128)S(1)}, f32[8,128]{1,0:T(8,128)S(1)}) custom-call(f32[32,1024]{1,0:T(8,128)S(1)} %get-tuple-element.25.own, f32[32,1024]{1,0:T(8,128)S(1)} %collective-permute-done.1.other, f32[32,1024]{1,0:T(8,128)S(1)} %ratio.1, bf16[512,2048]{1,0:T(8,128)(2,1)S(1)} %get-tuple-element.23.high, ...), custom_call_target="tpu_custom_call" | custom-call | flops 201326592 | tf_op jit(solution)/shard_map/keep/pallas_call | solution.py:21
  10.4 0.2 collective-permute-done.2
  10.6 2.7 %collective-permute-start.3 = (f32[136,128]{1,0:T(8,128)S(1)}, f32[136,128]{1,0:T(8,128)S(1)}, u32[]{:S(2)}, u32[]{:S(2)}) collective-permute-start(f32[136,128]{1,0:T(8,128)S(1)} %pad_maximum_fusion), channel_id=1, source_target_pairs={{0,5},{1,8},{2,11},{3,6},{4,13},{5,0},{6,3},{7,14},{8,1},{9,12},{1... | collective-permute-start | bytes 208904 | tf_op jit(solution)/shard_map/ppermute | solution.py:253
  13.3 0.1 collective-permute-start.6
  13.4 2.0 %collective-permute-done.3 = f32[136,128]{1,0:T(8,128)S(1)} collective-permute-done((f32[136,128]{1,0:T(8,128)S(1)}, f32[136,128]{1,0:T(8,128)S(1)}, u32[]{:S(2)}, u32[]{:S(2)}) %collective-permute-start.3) | collective-permute-done | bytes 69664 | tf_op jit(solution)/shard_map/ppermute | solution.py:253
  15.4 2.4 %collective-permute-start.4 = (f32[136,128]{1,0:T(8,128)S(1)}, f32[136,128]{1,0:T(8,128)S(1)}, u32[]{:S(2)}, u32[]{:S(2)}) collective-permute-start(f32[136,128]{1,0:T(8,128)S(1)} %add.22), channel_id=1, source_target_pairs={{0,3},{1,4},{2,7},{3,0},{4,1},{5,6},{6,5},{7,2},{8,13},{9,10},{10,... | collective-permute-start | bytes 208904 | tf_op jit(solution)/shard_map/ppermute | solution.py:253
  17.8 0.0 collective-permute-done.6
  17.8 2.3 %collective-permute-start.7 = (f32[128,128]{1,0:T(8,128)S(1)}, f32[128,128]{1,0:T(8,128)S(1)}, u32[]{:S(2)}, u32[]{:S(2)}) collective-permute-start(f32[128,128]{1,0:T(8,128)S(1)} %add.25), channel_id=1, source_target_pairs={{0,9},{1,2},{2,1},{3,10},{4,7},{5,12},{6,15},{7,4},{8,11},{9,0},{1... | collective-permute-start | bytes 196616 | tf_op jit(solution)/shard_map/ppermute | solution.py:253
  20.1 0.0 collective-permute-done.4
  20.1 2.3 %collective-permute-start.5 = (f32[136,128]{1,0:T(8,128)S(1)}, f32[136,128]{1,0:T(8,128)S(1)}, u32[]{:S(2)}, u32[]{:S(2)}) collective-permute-start(f32[136,128]{1,0:T(8,128)S(1)} %add.23), channel_id=1, source_target_pairs={{0,9},{1,2},{2,1},{3,10},{4,7},{5,12},{6,15},{7,4},{8,11},{9,0},{1... | collective-permute-start | bytes 208904 | tf_op jit(solution)/shard_map/ppermute | solution.py:253
  22.4 0.1 collective-permute-done.7
  22.5 1.4 %collective-permute-start.8 = (f32[128,128]{1,0:T(8,128)S(1)}, f32[128,128]{1,0:T(8,128)S(1)}, u32[]{:S(2)}, u32[]{:S(2)}) collective-permute-start(f32[128,128]{1,0:T(8,128)S(1)} %add.26), channel_id=1, source_target_pairs={{0,3},{1,4},{2,7},{3,0},{4,1},{5,6},{6,5},{7,2},{8,13},{9,10},{10,... | collective-permute-start | bytes 196616 | tf_op jit(solution)/shard_map/ppermute | solution.py:253
  23.9 0.9 %collective-permute-done.5 = f32[136,128]{1,0:T(8,128)S(1)} collective-permute-done((f32[136,128]{1,0:T(8,128)S(1)}, f32[136,128]{1,0:T(8,128)S(1)}, u32[]{:S(2)}, u32[]{:S(2)}) %collective-permute-start.5) | collective-permute-done | bytes 69664 | tf_op jit(solution)/shard_map/ppermute | solution.py:253
  24.8 0.1 collective-permute-start.9
  25.0 0.4 %first.1 = (f32[32,2048]{1,0:T(8,128)S(1)}, f32[32,512]{1,0:T(8,128)S(1)}) custom-call(f32[32,2048]{1,0:T(8,128)S(1)} %get-tuple-element.26.tied, f32[136,128]{1,0:T(8,128)S(1)} %add.24.sums), custom_call_target="tpu_custom_call" | custom-call | flops 4194304 | tf_op jit(solution)/shard_map/first/pallas_call | solution.py:21
  25.4 0.9 %collective-permute-done.8 = f32[128,128]{1,0:T(8,128)S(1)} collective-permute-done((f32[128,128]{1,0:T(8,128)S(1)}, f32[128,128]{1,0:T(8,128)S(1)}, u32[]{:S(2)}, u32[]{:S(2)}) %collective-permute-start.8) | collective-permute-done | bytes 65568 | tf_op jit(solution)/shard_map/ppermute | solution.py:253
  26.3 0.5 %collective-permute-start.10 = (f32[128,128]{1,0:T(8,128)S(1)}, f32[128,128]{1,0:T(8,128)S(1)}, u32[]{:S(2)}, u32[]{:S(2)}) collective-permute-start(f32[128,128]{1,0:T(8,128)S(1)} %add.27.sums), channel_id=1, source_target_pairs={{0,1},{1,0},{2,3},{3,2},{4,5},{5,4},{6,7},{7,6},{8,9},{9,8},{10,11... | collective-permute-start | bytes 196616 | tf_op jit(solution)/shard_map/ppermute | solution.py:227
  26.8 0.0 collective-permute-done.9.others
  26.8 0.1 middle.1
  26.9 0.8 %collective-permute-done.10.others = f32[128,128]{1,0:T(8,128)S(1)} collective-permute-done((f32[128,128]{1,0:T(8,128)S(1)}, f32[128,128]{1,0:T(8,128)S(1)}, u32[]{:S(2)}, u32[]{:S(2)}) %collective-permute-start.10) | collective-permute-done | bytes 65568 | tf_op jit(solution)/shard_map/ppermute | solution.py:227
  27.7 0.8 %last.1 = f32[32,2048]{1,0:T(8,128)} custom-call(f32[32,2048]{1,0:T(8,128)S(1)} %get-tuple-element.26.tied, f32[32,2048]{1,0:T(8,128)S(1)} %get-tuple-element.37.scale, f32[32,512]{1,0:T(8,128)S(1)} %get-tuple-element.38.near, f32[32,512]{1,0:T(8,128)S(1)} %get-tuple-element.40.more, f32[32,512]{1,0:T(8,128)S(1)} %get-tuple-element.41.far, ...), custom_call_target="tpu_custom_call" | custom-call | tf_op jit(solution)/shard_map/last/pallas_call | solution.py:21
  (10 shorter events, 0.1 us)
Async XLA Ops:
  0.6 2.9 %collective-permute-start = (f32[32,2048]{1,0:T(8,128)}, f32[32,2048]{1,0:T(8,128)S(1)}, u32[]{:S(2)}, u32[]{:S(2)}) collective-permute-start(f32[32,2048]{1,0:T(8,128)} %basis.1), channel_id=1, source_target_pairs={{0,1},{1,0},{2,3},{3,2},{4,5},{5,4},{6,7},{7,6},{8,9},{9,8},{10,11... | collective-permute-start | bytes 786440 | tf_op jit(solution)/shard_map/ppermute | solution.py:227
  6.8 1.4 %collective-permute-start.1 = (f32[32,1024]{1,0:T(8,128)S(1)}, f32[32,1024]{1,0:T(8,128)S(1)}, u32[]{:S(2)}, u32[]{:S(2)}) collective-permute-start(f32[32,1024]{1,0:T(8,128)S(1)} %get-tuple-element.25.own), channel_id=1, source_target_pairs={{0,1},{1,0},{2,3},{3,2},{4,5},{5,4},{6,7},{7,6},{8,9},{9,8},{10,11... | collective-permute-start | bytes 393224 | tf_op jit(solution)/shard_map/ppermute | solution.py:227
  9.1 1.4 %collective-permute-start.2 = (f32[256,128]{1,0:T(8,128)S(1)}, f32[256,128]{1,0:T(8,128)S(1)}, u32[]{:S(2)}, u32[]{:S(2)}) collective-permute-start(f32[256,128]{1,0:T(8,128)S(1)} %send.1), channel_id=1, source_target_pairs={{0,1},{1,0},{2,3},{3,2},{4,5},{5,4},{6,7},{7,6},{8,9},{9,8},{10,11... | collective-permute-start | bytes 393224 | tf_op jit(solution)/shard_map/ppermute | solution.py:227
  10.6 4.8 %collective-permute-start.3 = (f32[136,128]{1,0:T(8,128)S(1)}, f32[136,128]{1,0:T(8,128)S(1)}, u32[]{:S(2)}, u32[]{:S(2)}) collective-permute-start(f32[136,128]{1,0:T(8,128)S(1)} %pad_maximum_fusion), channel_id=1, source_target_pairs={{0,5},{1,8},{2,11},{3,6},{4,13},{5,0},{6,3},{7,14},{8,1},{9,12},{1... | collective-permute-start | bytes 208904 | tf_op jit(solution)/shard_map/ppermute | solution.py:253
  13.3 4.5 %collective-permute-start.6 = (f32[128,128]{1,0:T(8,128)S(1)}, f32[128,128]{1,0:T(8,128)S(1)}, u32[]{:S(2)}, u32[]{:S(2)}) collective-permute-start(f32[128,128]{1,0:T(8,128)S(1)} %get-tuple-element.36), channel_id=1, source_target_pairs={{0,5},{1,8},{2,11},{3,6},{4,13},{5,0},{6,3},{7,14},{8,1},{9,12},{1... | collective-permute-start | bytes 196616 | tf_op jit(solution)/shard_map/ppermute | solution.py:253
  15.4 4.7 %collective-permute-start.4 = (f32[136,128]{1,0:T(8,128)S(1)}, f32[136,128]{1,0:T(8,128)S(1)}, u32[]{:S(2)}, u32[]{:S(2)}) collective-permute-start(f32[136,128]{1,0:T(8,128)S(1)} %add.22), channel_id=1, source_target_pairs={{0,3},{1,4},{2,7},{3,0},{4,1},{5,6},{6,5},{7,2},{8,13},{9,10},{10,... | collective-permute-start | bytes 208904 | tf_op jit(solution)/shard_map/ppermute | solution.py:253
  17.8 4.7 %collective-permute-start.7 = (f32[128,128]{1,0:T(8,128)S(1)}, f32[128,128]{1,0:T(8,128)S(1)}, u32[]{:S(2)}, u32[]{:S(2)}) collective-permute-start(f32[128,128]{1,0:T(8,128)S(1)} %add.25), channel_id=1, source_target_pairs={{0,9},{1,2},{2,1},{3,10},{4,7},{5,12},{6,15},{7,4},{8,11},{9,0},{1... | collective-permute-start | bytes 196616 | tf_op jit(solution)/shard_map/ppermute | solution.py:253
  20.1 4.7 %collective-permute-start.5 = (f32[136,128]{1,0:T(8,128)S(1)}, f32[136,128]{1,0:T(8,128)S(1)}, u32[]{:S(2)}, u32[]{:S(2)}) collective-permute-start(f32[136,128]{1,0:T(8,128)S(1)} %add.23), channel_id=1, source_target_pairs={{0,9},{1,2},{2,1},{3,10},{4,7},{5,12},{6,15},{7,4},{8,11},{9,0},{1... | collective-permute-start | bytes 208904 | tf_op jit(solution)/shard_map/ppermute | solution.py:253
  22.5 3.8 %collective-permute-start.8 = (f32[128,128]{1,0:T(8,128)S(1)}, f32[128,128]{1,0:T(8,128)S(1)}, u32[]{:S(2)}, u32[]{:S(2)}) collective-permute-start(f32[128,128]{1,0:T(8,128)S(1)} %add.26), channel_id=1, source_target_pairs={{0,3},{1,4},{2,7},{3,0},{4,1},{5,6},{6,5},{7,2},{8,13},{9,10},{10,... | collective-permute-start | bytes 196616 | tf_op jit(solution)/shard_map/ppermute | solution.py:253
  24.8 2.0 %collective-permute-start.9 = (f32[128,128]{1,0:T(8,128)S(1)}, f32[128,128]{1,0:T(8,128)S(1)}, u32[]{:S(2)}, u32[]{:S(2)}) collective-permute-start(f32[128,128]{1,0:T(8,128)S(1)} %slice.14), channel_id=1, source_target_pairs={{0,1},{1,0},{2,3},{3,2},{4,5},{5,4},{6,7},{7,6},{8,9},{9,8},{10,11... | collective-permute-start | bytes 196616 | tf_op jit(solution)/shard_map/ppermute | solution.py:227
  26.3 1.4 %collective-permute-start.10 = (f32[128,128]{1,0:T(8,128)S(1)}, f32[128,128]{1,0:T(8,128)S(1)}, u32[]{:S(2)}, u32[]{:S(2)}) collective-permute-start(f32[128,128]{1,0:T(8,128)S(1)} %add.27.sums), channel_id=1, source_target_pairs={{0,1},{1,0},{2,3},{3,2},{4,5},{5,4},{6,7},{7,6},{8,9},{9,8},{10,11... | collective-permute-start | bytes 196616 | tf_op jit(solution)/shard_map/ppermute | solution.py:227
